TPU v7x, 32 devices: a whole 2x2x4 slice. The times are simulated.
32 devices in a mesh: rows: 8 (over z, core), seq: 4 (over y, x).
Axes of the slice: x: 2, y: 2, z: 4, core: 2. Of those that a mesh axis runs over, the one named last changes fastest.
Arguments:
- frames: bfloat16 [16, 1024, 1024], P('rows', 'seq'), may hold values from -6 to 6
- text_states: bfloat16 [16, 256, 768], P('rows', 'seq'), may hold values from -6 to 6
- clip_lengths: int32 [16, 4], P('rows'), may hold values from 1 to 1021, as said below
- text_lengths: int32 [16, 4], P('rows'), may hold values from 1 to 253, as said below
- self_gain: float32 [1024], replicated, may hold values from 0.5 to 1.5
- self_shift: float32 [1024], replicated, may hold values from -3 to 3
- self_qkv: bfloat16 [1024, 3072], replicated, may hold values from -0.1875 to 0.1875
- self_out: bfloat16 [1024, 1024], replicated, may hold values from -2 to 2
- cross_gain: float32 [1024], replicated, may hold values from 0.5 to 1.5
- cross_shift: float32 [1024], replicated, may hold values from -3 to 3
- cross_query: bfloat16 [1024, 1024], replicated, may hold values from -0.1875 to 0.1875
- text_proj: bfloat16 [768, 1024], replicated, may hold values from -0.21875 to 0.21875
- text_bias: float32 [1024], replicated, may hold values from -3 to 3
- cross_kv: bfloat16 [1024, 2048], replicated, may hold values from -0.1875 to 0.1875
- cross_out: bfloat16 [1024, 1024], replicated, may hold values from -1.5 to 1.5
- feed_gain: float32 [1024], replicated, may hold values from 0.5 to 1.5
- feed_shift: float32 [1024], replicated, may hold values from -3 to 3
- feed_in: bfloat16 [1024, 4096], replicated, may hold values from -0.1875 to 0.1875
- feed_out: bfloat16 [4096, 1024], replicated, may hold values from -0.09375 to 0.09375
- grad_out: bfloat16 [16, 1024, 1024], P('rows', 'seq'), may hold values from -6 to 6
Outputs:
- result: bfloat16 [16, 1024, 1024], P('rows', 'seq')
- grad_frames: float32 [16, 1024, 1024], P('rows', 'seq')
- grad_text: float32 [16, 256, 768], P('rows', 'seq')
- grad_self_gain: float32 [1024], P('seq')
- grad_self_shift: float32 [1024], P('seq')
- grad_self_qkv: float32 [1024, 3072], P('rows', 'seq')
- grad_self_out: float32 [1024, 1024], P('rows', 'seq')
- grad_cross_gain: float32 [1024], P('seq')
- grad_cross_shift: float32 [1024], P('seq')
- grad_cross_query: float32 [1024, 1024], P('rows', 'seq')
- grad_text_proj: float32 [768, 1024], P('rows', 'seq')
- grad_text_bias: float32 [1024], P('seq')
- grad_cross_kv: float32 [1024, 2048], P('rows', 'seq')
- grad_cross_out: float32 [1024, 1024], P('rows', 'seq')
- grad_feed_gain: float32 [1024], P('seq')
- grad_feed_shift: float32 [1024], P('seq')
- grad_feed_in: float32 [1024, 4096], P('rows', 'seq')
- grad_feed_out: float32 [4096, 1024], P('seq', 'rows')
Inputs may be any that keep to these rules, and one draw needn't show every extreme that they name: `clip_lengths`: the 4 clip lengths of a row sum to 1024; among the rows of one index of rows, one has a clip of exactly 1021 frames. `text_lengths`: the 4 text lengths of a row sum to 256; clip c of a row reads the text tokens of its clip c; among the rows of one index of rows, one has a clip of exactly 253 text tokens.
All inputs are finite; a program needn't handle non-finite values.
Results may differ from a plain program's by a relative error of at most 0.014.
Values may be sent and summed in bfloat16 or wider, within the bound.
A program may use at most 256 MiB of HBM per device.

v0:
```python
import functools
import math

import jax
import jax.numpy as jnp
from jax import lax
from jax.experimental import pallas as pl
from jax.experimental.pallas import tpu as pltpu
from jax.sharding import PartitionSpec as P

HD = 64
PAIR = 2 * HD
EPSILON = 1e-05
MASKED = -1e30
ROWS = "rows"
SEQ = "seq"
BF = jnp.bfloat16
F32 = jnp.float32
VMEM_LIMIT = 48 * 1024 * 1024


def dot(left, right, left_dim=1, right_dim=0):
    return lax.dot_general(
        left, right, (((left_dim,), (right_dim,)), ((), ())), preferred_element_type=F32
    )


def pick(array, index, axis):
    return lax.dynamic_index_in_dim(array, index, axis, keepdims=False)


def after(value, *others):
    return lax.optimization_barrier((value,) + others)[0]


class Place:
    def __init__(self):
        self.rows, self.seq = lax.axis_size(ROWS), lax.axis_size(SEQ)
        self.nz = self.rows // 2
        self.nx = math.isqrt(self.seq)
        self.ny = self.seq // self.nx
        row, self.spot = lax.axis_index(ROWS), lax.axis_index(SEQ)
        self.core, self.z = row % 2, row // 2
        self.x, self.y = self.spot % self.nx, self.spot // self.nx
        self.owner = [0 if 4 * s // self.seq in (0, 3) else 1 for s in range(self.seq)]
        self.members = [[s for s in range(self.seq) if self.owner[s] == c] for c in (0, 1)]
        self.rank = [self.members[self.owner[s]].index(s) for s in range(self.seq)]

    def permute(self, value, target):
        pairs = []
        for z in range(self.nz):
            for c in range(2):
                for s in range(self.seq):
                    tz, tc, ts = target(z, c, s)
                    pairs.append(((2 * z + c) * self.seq + s, (2 * tz + tc) * self.seq + ts))
        return lax.ppermute(value, (ROWS, SEQ), pairs)

    def swap_core(self, value):
        return self.permute(value, lambda z, c, s: (z, 1 - c, s))

    def next_z(self, value):
        return self.permute(value, lambda z, c, s: ((z + 1) % self.nz, c, s))

    def next_x(self, value):
        nx = self.nx
        return self.permute(value, lambda z, c, s: (z, c, s // nx * nx + (s % nx + 1) % nx))

    def next_y(self, value):
        return self.permute(value, lambda z, c, s: (z, c, (s + self.nx) % self.seq))

    def to_rows(self, value):
        count = value.shape[0]
        my_rank = jnp.array(self.rank, jnp.int32)[self.spot]
        got = []
        for t in range(count):

            def target(z, c, s, t=t):
                return z, self.owner[s], c * count + (t + self.rank[s]) % count

            got.append(self.permute(pick(value, (t + my_rank) % count, 0), target))
        stacked = jnp.stack(got)
        here = self.spot % count
        return jnp.concatenate([pick(stacked, (here - k) % count, 0) for k in range(count)], axis=0)

    def from_rows(self, value, count):
        my_rank = jnp.array(self.rank, jnp.int32)[self.spot]
        slots = value.reshape(count, value.shape[0] // count, value.shape[1])
        here = self.spot % count
        got = []
        for t in range(count):

            def target(z, c, s, t=t):
                return z, s // count, self.members[c][(s % count - t) % count]

            got.append(self.permute(pick(slots, (here - t) % count, 0), target))
        stacked = jnp.stack(got)
        return jnp.stack([pick(stacked, (i - my_rank) % count, 0) for i in range(count)])

    def positions(self, total, core):
        quarter = total // 4
        inner = jnp.arange(quarter, dtype=jnp.int32)
        return jnp.concatenate([inner + core * quarter, inner + (3 - core) * quarter])

    def offset(self, i, j):
        return (self.y + 1 + i) % self.ny * self.nx + (self.x + 1 + j) % self.nx

    def relative_columns(self, value, outer_x):
        blocks = value.reshape(value.shape[0], self.seq, -1)
        if outer_x:
            order = [self.offset(i, j) for j in range(self.nx) for i in range(self.ny)]
        else:
            order = [self.offset(i, j) for i in range(self.ny) for j in range(self.nx)]
        return jnp.concatenate([pick(blocks, place, 1) for place in order], axis=1)


    def vector_sum(self, value):
        bit = 1
        while bit < self.rows:
            value = value + self.permute(
                value,
                lambda z, c, s: ((2 * z + c ^ bit) // 2, (2 * z + c ^ bit) % 2, s),
            )
            bit *= 2
        bit = 1
        while bit < self.seq:
            value = value + self.permute(value, lambda z, c, s: (z, c, s ^ bit))
            bit *= 2
        return value


def ring_order(count):
    return list(range(count - 2, -1, -1)) + [count - 1]


def ring_sum(pieces, send):
    order = ring_order(len(pieces))
    value = pieces[order[0]]()
    for k in order[1:]:
        value = pieces[k]() + send(value.astype(BF)).astype(F32)
    return value


def normalize(values):
    centered = values - jnp.mean(values, axis=-1, keepdims=True)
    scale = lax.rsqrt(jnp.mean(centered * centered, axis=-1, keepdims=True) + EPSILON)
    return centered * scale, scale


def layer_norm(values, gain, shift):
    return (normalize(values)[0] * gain + shift).astype(BF)


def norm_backward(values, gain, cotangent):
    normal, scale = normalize(values)
    grown = cotangent * gain
    inner = jnp.mean(grown, axis=-1, keepdims=True)
    along = jnp.mean(grown * normal, axis=-1, keepdims=True)
    grad = scale * (grown - inner - normal * along)
    return grad, jnp.sum(cotangent * normal, axis=0), jnp.sum(cotangent, axis=0)


def nt(left, right):
    return dot(left, right, 1, 1)


def head_lanes(values, head):
    lane = lax.broadcasted_iota(jnp.int32, values.shape, 1)
    return jnp.where((lane < HD) == (head == 0), values, jnp.zeros_like(values))


def turned(values):
    return jnp.swapaxes(values.astype(F32), 0, 1).astype(BF)


def segment_bias(key_segment, query_segment, causal):
    allowed = key_segment == query_segment
    if causal:
        key = lax.broadcasted_iota(jnp.int32, allowed.shape, 0)
        query = lax.broadcasted_iota(jnp.int32, allowed.shape, 1)
        allowed = allowed & (key <= query)
    return jnp.where(allowed, 0.0, MASKED).astype(F32)


def forward_heads(queries, blocks, lse_ref, at):
    parts = []
    for head in range(2):
        query = head_lanes(queries, head)
        scores = [nt(keys, query) + bias() for keys, _, bias in blocks]
        highest = functools.reduce(
            jnp.maximum, [jnp.max(s, axis=0, keepdims=True) for s in scores]
        )
        weights = [jnp.exp(s - highest) for s in scores]
        total = sum(jnp.sum(w, axis=0, keepdims=True) for w in weights)
        mixed = sum(
            dot(values[head * HD : (head + 1) * HD], w.astype(BF))
            for (_, values, _), w in zip(blocks, weights)
        )
        parts.append(mixed * (1.0 / total))
        lse_ref[0, head : head + 1, at] = highest + jnp.log(total)
    return jnp.swapaxes(jnp.concatenate(parts, axis=0), 0, 1).astype(BF)


def backward_heads(queries, grads, mixed, blocks, lse_ref, at):
    product = jnp.swapaxes(grads.astype(F32) * mixed.astype(F32), 0, 1)
    parts = []
    for head in range(2):
        query, grad = head_lanes(queries, head), head_lanes(grads, head)
        rows = slice(head * HD, (head + 1) * HD)
        inner = jnp.sum(product[rows], axis=0, keepdims=True)
        totals = lse_ref[0, head : head + 1, at]
        grad_query = None
        for keys, turned_keys, values, bias, sums in blocks:
            weights = jnp.exp(nt(keys, query) + bias() - totals)
            scores = (weights * (nt(values, grad) - inner)).astype(BF)
            add_to(sums, 0, dot(scores, query))
            add_to(sums, 1, dot(weights.astype(BF), grad))
            term = dot(turned_keys[rows], scores)
            grad_query = term if grad_query is None else grad_query + term
        parts.append(grad_query)
    return (jnp.swapaxes(jnp.concatenate(parts, axis=0), 0, 1) * HD**-0.5).astype(BF)


def add_to(sums, index, term):
    sums[index] = term if sums[index] is None else sums[index] + term


def scaled(values):
    return values * jnp.array(HD**-0.5, BF)


def self_plan(core):
    if core == 0:
        return [(0, 0, 0)], [(0, 0, 1), (0, 1, 2), (1, 0, 3), (1, 1, 4)]
    return [(0, 0, 0), (1, 0, 4)], [(0, 0, 1), (0, 1, 2), (1, 0, 3)]


def self_biases(core, qseg_ref, kseg_refs, bias_ref):
    length = bias_ref.shape[1]
    low, high = slice(0, length), slice(length, 2 * length)
    own, other = kseg_refs
    bias_ref[0] = segment_bias(own[low], qseg_ref[:, low], True)
    bias_ref[1] = segment_bias(own[low], qseg_ref[:, high], False)
    bias_ref[2] = segment_bias(own[high], qseg_ref[:, high], True)
    bias_ref[3] = segment_bias(other[low], qseg_ref[:, high], False)

    @pl.when(core == 0)
    def _():
        bias_ref[4] = segment_bias(other[high], qseg_ref[:, high], False)

    @pl.when(core != 0)
    def _():
        bias_ref[4] = segment_bias(other[low], qseg_ref[:, low], False)


def self_forward_kernel(
    core_ref, qseg_ref, own_ref, other_ref, q_ref, k_ref, v_ref, ko_ref, vo_ref, o_ref, lse_ref, bias_ref
):
    core = core_ref[0]
    length = bias_ref.shape[1]

    @pl.when(pl.program_id(0) == 0)
    def _():
        self_biases(core, qseg_ref, (own_ref, other_ref), bias_ref)

    keys, values = (k_ref, ko_ref), (v_ref, vo_ref)
    for which in range(2):

        @pl.when((core == 0) == (which == 0))
        def _(which=which):
            for half, plan in enumerate(self_plan(which)):
                at = slice(half * length, (half + 1) * length)
                blocks = []
                for source, part, number in plan:
                    where = slice(part * length, (part + 1) * length)
                    blocks.append(
                        (
                            keys[source][where],
                            turned(values[source][where]),
                            functools.partial(bias_ref.__getitem__, number),
                        )
                    )
                o_ref[at] = forward_heads(scaled(q_ref[at]), blocks, lse_ref, at)


def self_backward_kernel(
    core_ref,
    qseg_ref,
    own_ref,
    other_ref,
    q_ref,
    k_ref,
    v_ref,
    ko_ref,
    vo_ref,
    g_ref,
    o_ref,
    lse_ref,
    dq_ref,
    dk_ref,
    dv_ref,
    dko_ref,
    dvo_ref,
    bias_ref,
):
    core = core_ref[0]
    length = bias_ref.shape[1]

    @pl.when(pl.program_id(0) == 0)
    def _():
        self_biases(core, qseg_ref, (own_ref, other_ref), bias_ref)

    keys, values = (k_ref, ko_ref), (v_ref, vo_ref)
    for which in range(2):

        @pl.when((core == 0) == (which == 0))
        def _(which=which):
            sums = {(s, p): [None, None] for s in range(2) for p in range(2)}
            for half, plan in enumerate(self_plan(which)):
                at = slice(half * length, (half + 1) * length)
                blocks = []
                for source, part, number in plan:
                    where = slice(part * length, (part + 1) * length)
                    blocks.append(
                        (
                            keys[source][where],
                            turned(keys[source][where]),
                            values[source][where],
                            functools.partial(bias_ref.__getitem__, number),
                            sums[source, part],
                        )
                    )
                dq_ref[at] = backward_heads(
                    scaled(q_ref[at]), g_ref[at], o_ref[at], blocks, lse_ref, at
                )
            for (source, part), pair in sums.items():
                where = slice(part * length, (part + 1) * length)
                for ref, value in zip(((dk_ref, dv_ref), (dko_ref, dvo_ref))[source], pair):
                    if value is None:
                        ref[where] = jnp.zeros((length, PAIR), BF)
                    else:
                        ref[where] = value.astype(BF)


def cross_forward_kernel(qseg_ref, kseg_ref, q_ref, k_ref, v_ref, o_ref, lse_ref, bias_ref):
    length = q_ref.shape[0] // 2

    @pl.when(pl.program_id(0) == 0)
    def _():
        bias_ref[...] = segment_bias(kseg_ref[...], qseg_ref[...], False)

    turned_values = turned(v_ref[...])
    for half in range(2):
        at = slice(half * length, (half + 1) * length)
        blocks = [(k_ref[...], turned_values, lambda at=at: bias_ref[:, at])]
        o_ref[at] = forward_heads(scaled(q_ref[at]), blocks, lse_ref, at)


def cross_backward_kernel(
    qseg_ref,
    kseg_ref,
    q_ref,
    k_ref,
    v_ref,
    g_ref,
    o_ref,
    lse_ref,
    dq_ref,
    dk_ref,
    dv_ref,
    bias_ref,
):
    length = q_ref.shape[0] // 2

    @pl.when(pl.program_id(0) == 0)
    def _():
        bias_ref[...] = segment_bias(kseg_ref[...], qseg_ref[...], False)

    turned_keys = turned(k_ref[...])
    sums = [None, None]
    for half in range(2):
        at = slice(half * length, (half + 1) * length)
        blocks = [(k_ref[...], turned_keys, v_ref[...], lambda at=at: bias_ref[:, at], sums)]
        dq_ref[at] = backward_heads(scaled(q_ref[at]), g_ref[at], o_ref[at], blocks, lse_ref, at)
    dk_ref[...] = sums[0].astype(BF)
    dv_ref[...] = sums[1].astype(BF)


def column(rows, first=0):
    return pl.BlockSpec((rows, PAIR), lambda i: (0, first + i))


def whole(array):
    return pl.BlockSpec(array.shape, lambda i: (0,) * array.ndim)


SMEM_SPEC = pl.BlockSpec(memory_space=pltpu.SMEM)


def without(kernel, first, count):
    def run(*refs):
        kernel(*refs[:first], *refs[first + count :])

    return run


ANY_SPEC = pl.BlockSpec(memory_space=pl.ANY)
WHOLE_SPEC = pl.BlockSpec(memory_space=pltpu.VMEM)


def attention_call(kernel, heads, in_specs, outs, bias_shape, flops, arguments, before=()):
    pairs = heads // 2
    kernel = without(kernel, len(arguments), len(before))
    in_specs = list(in_specs) + [ANY_SPEC] * len(before)
    arguments = tuple(arguments) + tuple(before)
    out_shape, out_specs = [], []
    for rows in outs:
        if rows is None:
            queries = outs[0]
            out_shape.append(jax.ShapeDtypeStruct((pairs, 8, queries), F32))
            out_specs.append(pl.BlockSpec((1, 8, queries), lambda i: (i, 0, 0)))
        else:
            out_shape.append(jax.ShapeDtypeStruct((rows, pairs * PAIR), BF))
            out_specs.append(column(rows))
    return pl.pallas_call(
        kernel,
        grid=(pairs,),
        in_specs=in_specs,
        out_specs=out_specs,
        out_shape=out_shape,
        scratch_shapes=[pltpu.VMEM(bias_shape, F32)],
        compiler_params=pltpu.CompilerParams(vmem_limit_bytes=VMEM_LIMIT),
        cost_estimate=pl.CostEstimate(flops=flops, bytes_accessed=8 << 20, transcendentals=flops >> 8),
    )(*arguments)


def lse_spec(queries):
    return pl.BlockSpec((1, 8, queries), lambda i: (i, 0, 0))


def self_forward(core, qseg, own, other, queries, pair, pair_other):
    rows, width = queries.shape
    heads = width // HD
    length = rows // 2
    half = heads // 2
    return attention_call(
        self_forward_kernel,
        heads,
        [
            SMEM_SPEC,
            whole(qseg),
            whole(own),
            whole(other),
            column(rows),
            column(rows),
            column(rows, half),
            column(rows),
            column(rows, half),
        ],
        (rows, None),
        (5, length, length),
        heads * 5 * 4 * length * length * PAIR * 2,
        (core, qseg, own, other, queries, pair, pair, pair_other, pair_other),
    )


def self_backward(core, qseg, own, other, queries, pair, pair_other, grads, mixed, lse, before=()):
    rows, width = queries.shape
    heads = width // HD
    length = rows // 2
    half = heads // 2
    return attention_call(
        self_backward_kernel,
        heads,
        [
            SMEM_SPEC,
            whole(qseg),
            whole(own),
            whole(other),
            column(rows),
            column(rows),
            column(rows, half),
            column(rows),
            column(rows, half),
            column(rows),
            column(rows),
            lse_spec(rows),
        ],
        (rows,) * 5,
        (5, length, length),
        heads * 5 * 10 * length * length * PAIR * 2,
        (core, qseg, own, other, queries, pair, pair, pair_other, pair_other, grads, mixed, lse),
        before,
    )


def cross_forward(qseg, kseg, queries, pair):
    rows, width = queries.shape
    heads = width // HD
    count = pair.shape[0]
    return attention_call(
        cross_forward_kernel,
        heads,
        [whole(qseg), whole(kseg), column(rows), column(count), column(count, heads // 2)],
        (rows, None),
        (count, rows),
        heads * 4 * rows * count * PAIR * 2,
        (qseg, kseg, queries, pair, pair),
    )


def cross_backward(qseg, kseg, queries, pair, grads, mixed, lse, before=()):
    rows, width = queries.shape
    heads = width // HD
    count = pair.shape[0]
    return attention_call(
        cross_backward_kernel,
        heads,
        [
            whole(qseg),
            whole(kseg),
            column(rows),
            column(count),
            column(count, heads // 2),
            column(rows),
            column(rows),
            lse_spec(rows),
        ],
        (rows, count, count),
        (count, rows),
        heads * 10 * rows * count * PAIR * 2,
        (qseg, kseg, queries, pair, pair, grads, mixed, lse),
        before,
    )


def gelu_and_slope(values):
    inside = 0.5 * (1.0 + lax.erf(values * (0.5**0.5)))
    bell = jnp.exp(-0.5 * values * values) * ((2.0 * math.pi) ** -0.5)
    return values * inside, inside + values * bell

def feed_kernel(shape, meta_ref, own_ref, other_ref, gown_ref, gother_ref, win_ref, wout_ref, *refs):
    nx, ny, nz, chunk = shape
    res_ref, res_other_ref, grad_ref, grad_other_ref = refs[:4]
    gin_refs, gout_refs = refs[4 : 4 + nx], refs[4 + nx : 4 + nx + ny]
    act_ref, pre_ref, turned_ref, gturned_ref, res_acc, grad_acc = refs[4 + nx + ny :]
    j, i = pl.program_id(0), pl.program_id(1)
    z = meta_ref[3]
    tokens = own_ref.shape[0]
    sources = ((own_ref, gown_ref, res_ref, grad_ref), (other_ref, gother_ref, res_acc, grad_acc))

    @pl.when((i == 0) & (j == 0))
    def _():
        for side, (values, grads, res, grad) in enumerate(sources):
            at = slice(side * tokens, (side + 1) * tokens)
            turned_ref[:, at] = turned(values[...])
            gturned_ref[:, at] = turned(grads[...])
            res[...] = jnp.zeros_like(res)
            grad[...] = jnp.zeros_like(grad)

    for side, (values, grads, res, grad) in enumerate(sources):
        for m in range(tokens // chunk):
            at = slice(m * chunk, (m + 1) * chunk)
            activated, slope = gelu_and_slope(dot(values[at], win_ref[...]))
            activated = activated.astype(BF)
            before = (nt(grads[at], wout_ref[...]) * slope).astype(BF)
            to = slice(side * tokens + m * chunk, side * tokens + (m + 1) * chunk)
            act_ref[to] = activated
            pre_ref[to] = before
            res[at] += dot(activated, wout_ref[...])
            grad[at] += nt(before, win_ref[...])

    rows = turned_ref.shape[0] // nz
    for k in range(nz):
        source = pl.ds(pl.multiple_of((z + 1 + k) % nz * rows, rows), rows)
        to = slice(k * rows, (k + 1) * rows)
        gin = dot(turned_ref[source], pre_ref[...]).astype(BF)
        gout = dot(gturned_ref[source], act_ref[...]).astype(BF)
        for number, ref in enumerate(gin_refs):

            @pl.when(j == number)
            def _(ref=ref):
                ref[0, to] = gin

        for number, ref in enumerate(gout_refs):

            @pl.when(i == number)
            def _(ref=ref):
                ref[0, to] = gout

    @pl.when((i == ny - 1) & (j == nx - 1))
    def _():
        res_other_ref[...] = res_acc[...].astype(BF)
        grad_other_ref[...] = grad_acc[...].astype(BF)


def feed(place, meta, own, other, gown, gother, feed_in, feed_out):
    nx, ny, nz = place.nx, place.ny, place.nz
    tokens, width = own.shape
    part = feed_in.shape[1] // place.seq // 2
    chunk = min(256, tokens)

    def unit(j, i, meta):
        return 2 * ((meta[2] + 1 + i) % ny * nx + (meta[1] + 1 + j) % nx) + meta[0]

    def gin_spec(number):
        def index(j, i, meta):
            return jnp.where(j == number, i, jnp.where(j < number, 0, ny - 1)), 0, 0

        return pl.BlockSpec((1, width, part), index)

    gout_spec = pl.BlockSpec((1, width, part), lambda j, i, meta: (j, 0, 0))
    total = 2 * tokens
    return pl.pallas_call(
        functools.partial(feed_kernel, (nx, ny, nz, chunk)),
        grid_spec=pltpu.PrefetchScalarGridSpec(
            num_scalar_prefetch=1,
            grid=(nx, ny),
            in_specs=[WHOLE_SPEC] * 4
            + [
                pl.BlockSpec((width, part), lambda j, i, meta: (0, unit(j, i, meta))),
                pl.BlockSpec((part, width), lambda j, i, meta: (unit(j, i, meta), 0)),
            ],
            out_specs=[WHOLE_SPEC] * 4 + [gin_spec(n) for n in range(nx)] + [gout_spec] * ny,
            scratch_shapes=[
                pltpu.VMEM((total, part), BF),
                pltpu.VMEM((total, part), BF),
                pltpu.VMEM((width, total), BF),
                pltpu.VMEM((width, total), BF),
                pltpu.VMEM((tokens, width), F32),
                pltpu.VMEM((tokens, width), F32),
            ],
        ),
        out_shape=[
            jax.ShapeDtypeStruct((tokens, width), F32),
            jax.ShapeDtypeStruct((tokens, width), BF),
            jax.ShapeDtypeStruct((tokens, width), F32),
            jax.ShapeDtypeStruct((tokens, width), BF),
        ]
        + [jax.ShapeDtypeStruct((ny, width, part), BF)] * nx
        + [jax.ShapeDtypeStruct((nx, width, part), BF)] * ny,
        compiler_params=pltpu.CompilerParams(vmem_limit_bytes=60 * 1024 * 1024),
        cost_estimate=pl.CostEstimate(
            flops=12 * total * width * part * place.seq,
            bytes_accessed=40 << 20,
            transcendentals=2 * total * part * place.seq,
        ),
    )(meta, own, other, gown, gother, feed_in, feed_out)


def weight_kernel(shape, meta_ref, *refs):
    count, nz = shape
    lefts, rights = refs[:count], refs[count : 2 * count]
    own_ref, other_ref, turned_ref = refs[2 * count :]
    core, z = meta_ref[0], meta_ref[3]
    block = own_ref.shape[1] // nz
    for number in range(count):

        @pl.when(pl.program_id(0) == number)
        def _(left=lefts[number], right=rights[number]):
            tokens = left.shape[0]
            turned_ref[:, :tokens] = turned(left[...])
            for k in range(nz):
                start = (z + 1 + k) % nz * 2
                to = slice(k * block, (k + 1) * block)
                for which, ref in ((core, own_ref), (1 - core, other_ref)):
                    at = pl.ds(pl.multiple_of((start + which) * block, block), block)
                    ref[0, to] = dot(turned_ref[at, :tokens], right[...]).astype(BF)


def weight_parts(place, meta, lefts, rights, before=()):
    count = len(lefts)
    depth, width = lefts[0].shape[1], rights[0].shape[1]
    tokens = max(left.shape[0] for left in lefts)
    out = jax.ShapeDtypeStruct((count, depth // 2, width), BF)
    spec = pl.BlockSpec((1, depth // 2, width), lambda u: (u, 0, 0))
    return pl.pallas_call(
        without(functools.partial(weight_kernel, (count, place.nz)), 1 + 2 * count, len(before)),
        grid=(count,),
        in_specs=[SMEM_SPEC] + [WHOLE_SPEC] * (2 * count) + [ANY_SPEC] * len(before),
        out_specs=[spec, spec],
        out_shape=[out, out],
        scratch_shapes=[pltpu.VMEM((depth, tokens), BF)],
        compiler_params=pltpu.CompilerParams(vmem_limit_bytes=VMEM_LIMIT),
        cost_estimate=pl.CostEstimate(
            flops=2 * count * tokens * depth * width,
            bytes_accessed=count * depth * width * 4,
            transcendentals=0,
        ),
    )(meta, *lefts, *rights, *before)


def shards(
    frames,
    text_states,
    clip_lengths,
    text_lengths,
    self_gain,
    self_shift,
    self_qkv,
    self_out,
    cross_gain,
    cross_shift,
    cross_query,
    text_proj,
    text_bias,
    cross_kv,
    cross_out,
    feed_gain,
    feed_shift,
    feed_in,
    feed_out,
    grad_out,
):
    place = Place()
    count = frames.shape[0]
    width = frames.shape[2]
    frame_total = frames.shape[1] * place.seq
    text_total = text_states.shape[1] * place.seq

    lengths = jnp.concatenate([clip_lengths, text_lengths], axis=1)
    lengths_other = place.swap_core(lengths)
    mine = place.spot // count == place.core
    row_lengths = pick(jnp.where(mine, lengths, lengths_other), place.spot % count, 0)
    clips = clip_lengths.shape[1]
    frame_ends = jnp.cumsum(row_lengths[:clips])
    text_ends = jnp.cumsum(row_lengths[clips:])

    def segments(positions, ends):
        return jnp.sum((positions[:, None] >= ends[None, :]).astype(jnp.int32), axis=1)

    own_segment = segments(place.positions(frame_total, place.core), frame_ends)
    other_segment = segments(place.positions(frame_total, 1 - place.core), frame_ends)
    text_positions = jnp.concatenate(
        [place.positions(text_total, place.core), place.positions(text_total, 1 - place.core)]
    )
    text_segment = segments(text_positions, text_ends)
    query_segment = own_segment[None, :]
    own_segment, other_segment = own_segment[:, None], other_segment[:, None]
    text_segment = text_segment[:, None]
    core = place.core.reshape(1).astype(jnp.int32)

    text_half = place.to_rows(text_states)
    layer_raw = place.to_rows(frames)
    text_input = jnp.concatenate([text_half, place.swap_core(text_half)], axis=0)
    cotangent = place.to_rows(after(grad_out, layer_raw))
    cotangent_other = place.swap_core(cotangent)
    projected = (dot(text_input, text_proj) + text_bias).astype(BF)
    text_pair = dot(projected, cross_kv).astype(BF)

    layer_input = layer_raw.astype(F32)
    normed_self = layer_norm(layer_input, self_gain, self_shift)
    pair = dot(normed_self, self_qkv[:, width:]).astype(BF)
    pair_other = place.swap_core(pair)
    queries = dot(normed_self, self_qkv[:, :width]).astype(BF)
    self_mix, self_lse = self_forward(
        core, query_segment, own_segment, other_segment, queries, pair, pair_other
    )
    first = layer_input + dot(self_mix, self_out)
    normed_cross = layer_norm(first, cross_gain, cross_shift)
    cross_queries = dot(normed_cross, cross_query).astype(BF)
    cross_mix, cross_lse = cross_forward(query_segment, text_segment, cross_queries, text_pair)
    second = first + dot(cross_mix, cross_out)
    normed_feed = layer_norm(second, feed_gain, feed_shift)

    nx, ny, nz, seq = place.nx, place.ny, place.nz, place.seq
    meta = jnp.stack([place.core, place.x, place.y, place.z]).astype(jnp.int32)
    normed_other = place.swap_core(normed_feed)
    fed = feed(
        place, meta, normed_feed, normed_other, cotangent, cotangent_other, feed_in, feed_out
    )
    result, result_away, grad_normed_feed, grad_away = fed[:4]
    grad_in, grad_out_parts = fed[4 : 4 + nx], fed[4 + nx :]
    grad_normed_feed = grad_normed_feed + place.swap_core(grad_away).astype(F32)

    def x_piece(k):
        return lambda: grad_in[k].astype(F32)

    def y_piece(k):
        return lambda: grad_out_parts[k].astype(F32)

    in_half = ring_sum([x_piece(k) for k in range(nx)], place.next_x).astype(BF)
    out_half = ring_sum([y_piece(k) for k in range(ny)], place.next_y).astype(BF)

    grad_part, grad_feed_gain, grad_feed_shift = norm_backward(second, feed_gain, grad_normed_feed)
    grad_second = cotangent.astype(F32) + grad_part
    grad_second_branch = grad_second.astype(BF)
    grad_cross_mix = dot(grad_second_branch, cross_out, 1, 1).astype(BF)
    grad_cross_queries, grad_text_keys, grad_text_values = cross_backward(
        query_segment,
        text_segment,
        cross_queries,
        text_pair,
        grad_cross_mix,
        cross_mix,
        cross_lse,
    )
    result = (second + result + place.swap_core(after(result_away, grad_cross_mix)).astype(F32)).astype(BF)
    result = place.from_rows(result, count)
    grad_normed_cross = dot(grad_cross_queries, cross_query, 1, 1)
    grad_part, grad_cross_gain, grad_cross_shift = norm_backward(first, cross_gain, grad_normed_cross)
    grad_first = grad_second + grad_part
    grad_first_branch = grad_first.astype(BF)
    grad_self_mix = dot(grad_first_branch, self_out, 1, 1).astype(BF)

    grad_pair = jnp.concatenate([grad_text_keys, grad_text_values], axis=1)
    grad_projected = dot(grad_pair, cross_kv, 1, 1).astype(BF)
    text_blocks = text_input.reshape(text_total, place.rows, -1)
    padding = width // place.rows - text_blocks.shape[2]
    text_padded = jnp.pad(text_blocks, ((0, 0), (0, 0), (0, padding))).reshape(text_total, width)
    middle_own, middle_away = weight_parts(
        place,
        meta,
        [cross_mix, normed_cross, projected, projected, text_padded],
        [grad_second_branch, grad_cross_queries, grad_text_keys, grad_text_values, grad_projected],
    )
    out_own, out_away = weight_parts(place, meta, [self_mix], [grad_first_branch])
    middle_got = place.swap_core(middle_away)
    out_got = place.swap_core(out_away)
    grad_text_bias = jnp.sum(grad_projected.astype(F32), axis=0)
    grad_text = dot(grad_projected, text_proj, 1, 1)

    grad_queries, grad_keys, grad_values, keys_away, values_away = self_backward(
        core,
        query_segment,
        own_segment,
        other_segment,
        queries,
        pair,
        pair_other,
        grad_self_mix,
        self_mix,
        self_lse,
        before=(in_half, out_half, middle_got, out_got),
    )
    grad_keys = (grad_keys.astype(F32) + place.swap_core(keys_away).astype(F32)).astype(BF)
    grad_values = (grad_values.astype(F32) + place.swap_core(values_away).astype(F32)).astype(BF)
    grad_packed = jnp.concatenate([grad_queries, grad_keys, grad_values], axis=1)

    in_quarter = ring_sum([lambda k=k: in_half[k].astype(F32) for k in range(ny)], place.next_y)
    out_quarter = ring_sum([lambda k=k: out_half[k].astype(F32) for k in range(nx)], place.next_x)
    feed_quarter = jnp.stack([in_quarter, out_quarter]).astype(BF)
    feed_quarter = feed_quarter.reshape(2, nz, -1, feed_quarter.shape[2])
    feed_own = ring_sum([lambda k=k: feed_quarter[:, k].astype(F32) for k in range(nz)], place.next_z)
    block = width // place.rows
    feed_own = feed_own.reshape(2, 2, block, -1)
    feed_got = place.swap_core(pick(feed_own, 1 - place.core, 1))
    feed_own = pick(feed_own, place.core, 1)
    low = jnp.where(place.core == 0, feed_own, feed_got)
    high = jnp.where(place.core == 0, feed_got, feed_own)
    sum_feed = jnp.concatenate([low, high], axis=2)

    def middle_piece(k):
        at = slice(k * block, (k + 1) * block)
        return lambda: middle_own[:, at].astype(F32) + middle_got[:, at].astype(F32)

    middle = ring_sum([middle_piece(k) for k in range(nz)], place.next_z).astype(BF)
    spread = jnp.concatenate(
        [
            middle[0].reshape(block, seq, -1),
            middle[1].reshape(block, seq, -1),
            jnp.concatenate([middle[2], middle[3]], axis=1).reshape(block, seq, -1),
            middle[4].reshape(block, seq, -1),
        ],
        axis=2,
    ).reshape(block, ny, nx, -1)

    def shifted(array, index, number, length, axis):
        return lambda: pick(array, (index + 1 + number) % length, axis).astype(F32)

    spread = ring_sum([shifted(spread, place.x, k, nx, 2) for k in range(nx)], place.next_x).astype(BF)
    spread = ring_sum([shifted(spread, place.y, k, ny, 1) for k in range(ny)], place.next_y)
    piece = width // seq
    sum_cross_out, sum_cross_query = spread[:, :piece], spread[:, piece : 2 * piece]
    sum_cross_kv, sum_text_proj = spread[:, 2 * piece : 4 * piece], spread[:, 4 * piece :]
    sum_text_proj = sum_text_proj[: block - padding]

    relative_parts = place.relative_columns(grad_packed, True)
    qkv_own, qkv_away = weight_parts(place, meta, [normed_self], [relative_parts])
    qkv_got = place.swap_core(qkv_away)

    def columns(array):
        return array[0].reshape(array.shape[1], nx, ny, -1)

    def natural(array):
        return jnp.stack(
            [
                jnp.stack(
                    [
                        pick(array[0].reshape(array.shape[1], seq, -1), place.offset(i, j), 1)
                        for i in range(ny)
                    ],
                    axis=1,
                )
                for j in range(nx)
            ],
            axis=1,
        )

    last_own = jnp.concatenate([columns(qkv_own), natural(out_own)], axis=3)
    last_got = jnp.concatenate([columns(qkv_got), natural(out_got)], axis=3)
    last = (last_own.astype(F32) + last_got.astype(F32)).astype(BF)
    last = last.reshape(nz, 2, block // 2, nx, ny, -1)
    upper = ring_sum([lambda k=k: last[:, 0, :, k].astype(F32) for k in range(nx)], place.next_x).astype(BF)
    lower = ring_sum([lambda k=k: last[:, 1, :, :, k].astype(F32) for k in range(ny)], place.next_y).astype(BF)
    upper = ring_sum([lambda a=upper[:, :, k]: a.astype(F32) for k in range(ny)], place.next_y)
    lower = ring_sum([lambda a=lower[:, :, k]: a.astype(F32) for k in range(nx)], place.next_x)
    last = jnp.stack([upper, lower], axis=1).astype(BF)
    last = ring_sum([lambda a=last[k]: a.astype(F32) for k in range(nz)], place.next_z)
    last = last.reshape(block, -1)
    sum_self_qkv, sum_self_out = last[:, : 3 * piece], last[:, 3 * piece :]

    grad_normed_self = dot(grad_packed, self_qkv, 1, 1)
    grad_part, grad_self_gain, grad_self_shift = norm_backward(layer_input, self_gain, grad_normed_self)
    grad_frames = place.from_rows((grad_first + grad_part).astype(BF), count)
    half = grad_text.shape[0] // 2
    text_away = place.swap_core(grad_text[half:].astype(BF))
    grad_text = place.from_rows((grad_text[:half] + text_away.astype(F32)).astype(BF), count)

    vectors = place.vector_sum(
        jnp.stack(
            [
                grad_self_gain,
                grad_self_shift,
                grad_cross_gain,
                grad_cross_shift,
                grad_text_bias,
                grad_feed_gain,
                grad_feed_shift,
            ]
        )
    )
    vectors = pick(vectors.reshape(7, seq, width // seq), place.spot, 1)
    return (
        result,
        grad_frames.astype(F32),
        grad_text.astype(F32),
        vectors[0],
        vectors[1],
        sum_self_qkv,
        sum_self_out,
        vectors[2],
        vectors[3],
        sum_cross_query,
        sum_text_proj,
        vectors[4],
        sum_cross_kv,
        sum_cross_out,
        vectors[5],
        vectors[6],
        sum_feed[0],
        jnp.swapaxes(sum_feed[1], 0, 1),
    )


def solution(mesh):
    split, copied, table = P(ROWS, SEQ, None), P(), P(ROWS, None)
    vector, matrix = P(SEQ), P(ROWS, SEQ)
    return jax.shard_map(
        shards,
        mesh=mesh,
        in_specs=(split, split, table, table) + (copied,) * 15 + (split,),
        out_specs=(
            (split,) * 3
            + (vector, vector, matrix, matrix)
            + (vector, vector, matrix, matrix)
            + (vector, matrix, matrix)
            + (vector, vector, matrix, P(SEQ, ROWS))
        ),
        check_vma=False,
    )
```

profile of v0, /device:TPU:0, one launch (start us, length us, event | category | flops | bytes accessed | tf_op | source)
XLA Modules:
  0.0 494.7 jit_solution(2318615019465754868)
XLA Ops:
  6.5 2.2 dynamic-slice_bitcast_fusion.8
  8.7 5.4 %collective-permute-start = (bf16[256,1024]{1,0:T(8,128)(2,1)}, bf16[256,1024]{1,0:T(8,128)(2,1)}, u32[]{:S(2)}, u32[]{:S(2)}) collective-permute-start(bf16[256,1024]{1,0:T(8,128)(2,1)} %get-tuple-element.202), channel_id=1, source_target_pairs={{0,0},{1,4},{2,5},{3,1},{4,2},{5,6},{6,7},{7,3},{8,8},{9,12},{10,1... | collective-permute-start | bytes 1572872 | tf_op jit(solution)/shard_map/ppermute | solution.py:56
  16.7 5.4 %collective-permute-start.5 = (bf16[64,768]{1,0:T(8,128)(2,1)S(1)}, bf16[64,768]{1,0:T(8,128)(2,1)S(1)}, u32[]{:S(2)}, u32[]{:S(2)}) collective-permute-start(bf16[64,768]{1,0:T(8,128)(2,1)S(1)} %get-tuple-element.211), channel_id=1, source_target_pairs={{0,1},{1,5},{2,4},{3,0},{4,3},{5,7},{6,6},{7,2},{8,9},{9,13},{10,1... | collective-permute-start | bytes 294920 | tf_op jit(solution)/shard_map/ppermute | solution.py:56
  26.3 5.4 %collective-permute-start.8 = (bf16[256,1024]{1,0:T(8,128)(2,1)}, bf16[256,1024]{1,0:T(8,128)(2,1)}, u32[]{:S(2)}, u32[]{:S(2)}) collective-permute-start(bf16[256,1024]{1,0:T(8,128)(2,1)} %get-tuple-element.198), channel_id=1, source_target_pairs={{0,0},{1,4},{2,5},{3,1},{4,2},{5,6},{6,7},{7,3},{8,8},{9,12},{10,1... | collective-permute-start | bytes 1572872 | tf_op jit(solution)/shard_map/ppermute | solution.py:56
  38.2 3.7 fusion.2.refs_5_.refs_6_
  50.9 3.6 convolution_convert_fusion.refs_3_.refs_4_
  58.3 2.8 fusion.26.refs_4_
  61.2 18.1 %shard_map.385 = (bf16[512,1024]{1,0:T(8,128)(2,1)S(1)}, f32[8,8,512]{2,1,0:T(8,128)S(1)}) custom-call(s32[1]{0:T(128)} %bitcast.7.refs_0_, s32[1,512]{1,0:T(1,128)S(1)} %bitcast.245, s32[512,1]{1,0:T(8,128)S(1)} %copy.173.refs_2_, s32[512,1]{1,0:T(8,128)S(1)} %copy-done.7, bf16[512,1024]{1,0:T(8,128)(2,1)S(1)} %fusion.26.refs_4_, ...), custom_call_target="tpu_custom_call" | custom-call | flops 5368709120 | bytes 8388608 | tf_op jit(solution)/shard_map/pallas_call | solution.py:424
  83.2 11.9 %shard_map.386 = (bf16[512,1024]{1,0:T(8,128)(2,1)S(1)}, f32[8,8,512]{2,1,0:T(8,128)S(1)}) custom-call(s32[1,512]{1,0:T(1,128)S(1)} %bitcast.246, s32[256,1]{1,0:T(8,128)S(1)} %copy.175.refs_1_, bf16[512,1024]{1,0:T(8,128)(2,1)S(1)} %convolution_convert_fusion.3.refs_2_, bf16[256,2048]{1,0:T(8,128)(2,1)S(1)} %convolution_convert_fusion.refs_3_.refs_4_, ...), custom_call_target="tpu_custom_call" | custom-call | flops 2147483648 | bytes 8388608 | tf_op jit(solution)/shard_map/pallas_call | solution.py:424
  99.9 2.4 collective-permute-done.7.other_ref
  102.3 40.9 %shard_map.387 = (f32[512,1024]{1,0:T(8,128)}, bf16[512,1024]{1,0:T(8,128)(2,1)}, f32[512,1024]{1,0:T(8,128)}, bf16[512,1024]{1,0:T(8,128)(2,1)}, bf16[2,1024,51...) custom-call(s32[4]{0:T(128)} %pad_add_fusion.4.meta_ref.refs_0_, ...), custom_call_target="tpu_custom_call" | custom-call | flops 25769803776 | bytes 41943040 | tf_op jit(solution)/shard_map/pallas_call | solution.py:613
  154.1 2.2 collective-permute-start.16
  156.4 4.2 multiply_reduce_fusion
  160.7 3.0 fusion.92
  165.3 12.1 %shard_map.388 = (bf16[512,1024]{1,0:T(8,128)(2,1)S(1)}, bf16[256,1024]{1,0:T(8,128)(2,1)S(1)}, bf16[256,1024]{1,0:T(8,128)(2,1)S(1)}) custom-call(s32[1,512]{1,0:T(1,128)S(1)} %bitcast.247, s32[256,1]{1,0:T(8,128)S(1)} %copy.175.refs_1_, bf16[512,1024]{1,0:T(8,128)(2,1)S(1)} %copy-done.21, bf16[256,2048]{1,0:T(8,128)(2,1)S(1)} %copy-done.11, ...), custom_call_target="tpu_custom_call" | custom-call | flops 5368709120 | bytes 8388608 | tf_op jit(solution)/shard_map/pallas_call | solution.py:424
  178.4 3.7 convert_reduce_fusion.1
  182.2 9.5 %shard_map.389 = (bf16[5,512,1024]{2,1,0:T(8,128)(2,1)}, bf16[5,512,1024]{2,1,0:T(8,128)(2,1)}) custom-call(s32[4]{0:T(128)S(1)} %copy-done.9, bf16[512,1024]{1,0:T(8,128)(2,1)S(1)} %copy-done.17, bf16[512,1024]{1,0:T(8,128)(2,1)S(1)} %add_convert_fusion.11.refs_2_, bf16[256,1024]{1,0:T(8,128)(2,1)S(1)} %copy-done.13, bf16[256,1024]{1,0:T(8,128)(2,1)S(1)} %copy-done.13, ...), custom_call_target="tpu_custom_call" | custom-call | flops 5368709120 | bytes 20971520 | tf_op jit(solution)/shard_map/pallas_call | solution.py:676
  202.6 2.8 add_convert_fusion.1.refs_13_
  207.7 2.2 add_convert_fusion.2.refs_12_
  212.3 2.3 convolution_convert_fusion.1.refs_9_
  218.8 11.3 %collective-permute-done.45 = bf16[1024,512]{1,0:T(8,128)(2,1)S(1)} collective-permute-done((bf16[1024,512]{1,0:T(8,128)(2,1)S(1)}, bf16[1024,512]{1,0:T(8,128)(2,1)S(1)}, u32[]{:S(2)}, u32[]{:S(2)}) %collective-permute-start.45) | collective-permute-done | bytes 1048608 | tf_op jit(solution)/shard_map/ppermute | solution.py:56
  230.5 4.3 collective-permute-done.44
  237.5 9.5 %collective-permute-start.25 = (bf16[64,768]{1,0:T(8,128)(2,1)S(1)}, bf16[64,768]{1,0:T(8,128)(2,1)S(1)}, u32[]{:S(2)}, u32[]{:S(2)}) collective-permute-start(bf16[64,768]{1,0:T(8,128)(2,1)S(1)} %get-tuple-element.207), channel_id=1, source_target_pairs={{0,3},{1,0},{2,7},{3,4},{4,2},{5,1},{6,6},{7,5},{8,11},{9,8},{10,1... | collective-permute-start | bytes 294920 | tf_op jit(solution)/shard_map/ppermute | solution.py:56
  255.8 5.4 %collective-permute-start.13 = (bf16[256,1024]{1,0:T(8,128)(2,1)}, bf16[256,1024]{1,0:T(8,128)(2,1)}, u32[]{:S(2)}, u32[]{:S(2)}) collective-permute-start(bf16[256,1024]{1,0:T(8,128)(2,1)} %get-tuple-element.194), channel_id=1, source_target_pairs={{0,0},{1,3},{2,4},{3,7},{4,1},{5,2},{6,5},{7,6},{8,8},{9,11},{10,1... | collective-permute-start | bytes 1572872 | tf_op jit(solution)/shard_map/ppermute | solution.py:56
  271.1 25.4 %shard_map.391 = (bf16[512,1024]{1,0:T(8,128)(2,1)S(1)}, bf16[512,1024]{1,0:T(8,128)(2,1)S(1)}, bf16[512,1024]{1,0:T(8,128)(2,1)S(1)}, bf16[512,1024]{1,0:T(8,128)(2,1)S(1)}, bf16[512,1024]{1,0:T(8,128)(2,1)S(1)}) custom-call(s32[1]{0:T(128)} %bitcast.7.refs_0_, s32[1,512]{1,0:T(1,128)S(1)} %bitcast.248, s32[512,1]{1,0:T(8,128)S(1)} %copy.173.refs_2_, ...), custom_call_target="tpu_custom_call" | custom-call | flops 13421772800 | bytes 8388608 | tf_op jit(solution)/shard_map/pallas_call | solution.py:424
  301.9 3.3 add_convert_fusion.6
  309.1 5.6 %reshape.288 = bf16[512,4,768]{2,1,0:T(4,128)(2,1)S(1)} reshape(bf16[512,3072]{1,0:T(8,128)(2,1)} %pad_maximum_fusion) | data formatting | bytes 6291456 | tf_op jit(solution)/shard_map/reshape | solution.py:108
  314.7 6.5 %constant_dynamic-slice_fusion.1 = (bf16[512,1,768]{2,1,0:T(2,128)(2,1)S(1)}, bf16[512,1,768]{2,1,0:T(2,128)(2,1)S(1)}, bf16[512,1,768]{2,1,0:T(2,128)(2,1)S(1)}, bf16[512,1,768]{2,1,0:T(2,128)(2,1)S(1)}) fusion(bf16[512,4,768]{2,1,0:T(4,128)(2,1)S(1)} %reshape.288, s32[]{:T(128)S(6)} %select_n.342, s32[]{:T(128)S(6)} %select_n.346, s32[]{:T(128)S(6)} %select_n.344, ...), kind=kLoop, calls=%fused_computation.228 | loop fusion | bytes 6291472 | tf_op jit(solution)/shard_map/jit(dynamic_index_in_dim)/dynamic_slice | solution.py:29
  323.7 8.4 %shard_map.392 = (bf16[1,512,3072]{2,1,0:T(8,128)(2,1)S(1)}, bf16[1,512,3072]{2,1,0:T(8,128)(2,1)}) custom-call(s32[4]{0:T(128)S(1)} %copy-done.9, bf16[512,1024]{1,0:T(8,128)(2,1)S(1)} %copy-done.3, bf16[512,3072]{1,0:T(8,128)(2,1)} %pad_maximum_fusion.1.refs_2_), custom_call_target="tpu_custom_call" | custom-call | flops 3221225472 | bytes 12582912 | tf_op jit(solution)/shard_map/pallas_call | solution.py:676
  334.6 3.9 collective-permute-done.39
  338.5 4.1 add_convert_fusion.5
  342.7 5.2 %fusion.18 = (f32[1024]{0:T(1024)S(1)}, f32[512]{0:T(512)S(1)}, f32[512]{0:T(512)S(1)}, f32[1024]{0:T(1024)S(1)}, f32[512,1024]{1,0:T(8,128)}) fusion(f32[512]{0:T(512)S(1)} %copy-done.78, f32[512]{0:T(512)S(1)} %copy-done.72, bf16[256,1024]{1,0:T(8,128)(2,1)S(1)} %copy-done.39, bf16[256,1024]{1,0:T(8,128)(2,1)S(1)} %copy-done.35, f32[1024]{0:T(1024)S(1)} %copy-done.82, ...), kind=kOutput, calls=%fused_computation.35 | convolution fusion | flops 3237475328 | bytes 12603392 | tf_op jit(solution)/shard_map/dot_general | solution.py:23
  348.1 2.3 fusion.66
  352.8 22.7 %collective-permute-done.27 = f32[7,1024]{1,0:T(8,128)S(1)} collective-permute-done((f32[7,1024]{1,0:T(8,128)S(1)}, f32[7,1024]{1,0:T(8,128)S(1)}, u32[]{:S(2)}, u32[]{:S(2)}) %collective-permute-start.27) | collective-permute-done | bytes 28704 | tf_op jit(solution)/shard_map/ppermute | solution.py:56
  376.1 4.2 collective-permute-done.28
  382.5 4.1 add_convert_fusion.4
  388.6 5.4 %collective-permute-start.21 = (bf16[256,1024]{1,0:T(8,128)(2,1)}, bf16[256,1024]{1,0:T(8,128)(2,1)}, u32[]{:S(2)}, u32[]{:S(2)}) collective-permute-start(bf16[256,1024]{1,0:T(8,128)(2,1)} %get-tuple-element.190), channel_id=1, source_target_pairs={{0,0},{1,3},{2,4},{3,7},{4,1},{5,2},{6,5},{7,6},{8,8},{9,11},{10,1... | collective-permute-start | bytes 1572872 | tf_op jit(solution)/shard_map/ppermute | solution.py:56
  396.0 3.5 concatenate.97
  399.6 4.1 copy.191
  404.4 7.1 %concatenate.99 = bf16[4,2,64,2,2,768]{5,4,3,2,1,0:T(2,128)(2,1)S(1)} reshape(bf16[1,512,3072]{2,1,0:T(8,128)(2,1)} %collective-permute-done.31) | data formatting | bytes 6291456 | tf_op jit(solution)/shard_map/concatenate | solution.py:900
  413.9 3.7 add_convert_fusion
  419.3 3.0 add_convert_fusion.3
  446.5 3.0 collective-permute-done.32
  455.1 5.7 %collective-permute-done.35 = bf16[4,64,1024]{2,1,0:T(8,128)(2,1)S(1)} collective-permute-done((bf16[4,64,1024]{2,1,0:T(8,128)(2,1)S(1)}, bf16[4,64,1024]{2,1,0:T(8,128)(2,1)S(1)}, u32[]{:S(2)}, u32[]{:S(2)}) %collective-permute-start.35) | collective-permute-done | bytes 524320 | tf_op jit(solution)/shard_map/ppermute | solution.py:56
  461.0 3.1 collective-permute-done.33
  464.4 9.9 %collective-permute-done.42 = bf16[128,2,1280]{2,0,1:T(8,128)(2,1)S(1)} collective-permute-done((bf16[128,2,1280]{2,0,1:T(8,128)(2,1)S(1)}, bf16[128,2,1280]{2,0,1:T(8,128)(2,1)S(1)}, u32[]{:S(2)}, u32[]{:S(2)}) %collective-permute-start.42) | collective-permute-done | bytes 655392 | tf_op jit(solution)/shard_map/ppermute | solution.py:56
  477.3 6.8 %collective-permute-done.37 = bf16[2,64,1024]{2,1,0:T(8,128)(2,1)S(1)} collective-permute-done((bf16[2,64,1024]{2,1,0:T(8,128)(2,1)S(1)}, bf16[2,64,1024]{2,1,0:T(8,128)(2,1)S(1)}, u32[]{:S(2)}, u32[]{:S(2)}) %collective-permute-start.37) | collective-permute-done | bytes 262176 | tf_op jit(solution)/shard_map/ppermute | solution.py:56
  486.5 6.4 %collective-permute-done.38 = bf16[2,64,1024]{2,1,0:T(8,128)(2,1)S(1)} collective-permute-done((bf16[2,64,1024]{2,1,0:T(8,128)(2,1)S(1)}, bf16[2,64,1024]{2,1,0:T(8,128)(2,1)S(1)}, u32[]{:S(2)}, u32[]{:S(2)}) %collective-permute-start.38) | collective-permute-done | bytes 262176 | tf_op jit(solution)/shard_map/ppermute | solution.py:56
  (428 shorter events, 156.0 us)
Async XLA Ops:
  2.2 24.1 %collective-permute-start.2 = (s32[2,8]{1,0:T(2,128)}, s32[2,8]{1,0:T(2,128)}, u32[]{:S(2)}, u32[]{:S(2)}) collective-permute-start(s32[2,8]{1,0:T(2,128)} %pad_add_fusion.2), channel_id=1, source_target_pairs={{0,4},{1,5},{2,6},{3,7},{4,0},{5,1},{6,2},{7,3},{8,12},{9,13},{10,... | collective-permute-start | bytes 200 | tf_op jit(solution)/shard_map/ppermute | solution.py:56
  8.7 23.7 %collective-permute-start = (bf16[256,1024]{1,0:T(8,128)(2,1)}, bf16[256,1024]{1,0:T(8,128)(2,1)}, u32[]{:S(2)}, u32[]{:S(2)}) collective-permute-start(bf16[256,1024]{1,0:T(8,128)(2,1)} %get-tuple-element.202), channel_id=1, source_target_pairs={{0,0},{1,4},{2,5},{3,1},{4,2},{5,6},{6,7},{7,3},{8,8},{9,12},{10,1... | collective-permute-start | bytes 1572872 | tf_op jit(solution)/shard_map/ppermute | solution.py:56
  14.1 20.2 %collective-permute-start.1 = (bf16[256,1024]{1,0:T(8,128)(2,1)}, bf16[256,1024]{1,0:T(8,128)(2,1)}, u32[]{:S(2)}, u32[]{:S(2)}) collective-permute-start(bf16[256,1024]{1,0:T(8,128)(2,1)} %get-tuple-element.201), channel_id=1, source_target_pairs={{0,1},{1,5},{2,4},{3,0},{4,3},{5,7},{6,6},{7,2},{8,9},{9,13},{10,1... | collective-permute-start | bytes 1572872 | tf_op jit(solution)/shard_map/ppermute | solution.py:56
  16.1 29.0 %collective-permute-start.4 = (bf16[64,768]{1,0:T(8,128)(2,1)S(1)}, bf16[64,768]{1,0:T(8,128)(2,1)S(1)}, u32[]{:S(2)}, u32[]{:S(2)}) collective-permute-start(bf16[64,768]{1,0:T(8,128)(2,1)S(1)} %get-tuple-element.212), channel_id=1, source_target_pairs={{0,0},{1,4},{2,5},{3,1},{4,2},{5,6},{6,7},{7,3},{8,8},{9,12},{10,1... | collective-permute-start | bytes 294920 | tf_op jit(solution)/shard_map/ppermute | solution.py:56
  16.7 28.4 %collective-permute-start.5 = (bf16[64,768]{1,0:T(8,128)(2,1)S(1)}, bf16[64,768]{1,0:T(8,128)(2,1)S(1)}, u32[]{:S(2)}, u32[]{:S(2)}) collective-permute-start(bf16[64,768]{1,0:T(8,128)(2,1)S(1)} %get-tuple-element.211), channel_id=1, source_target_pairs={{0,1},{1,5},{2,4},{3,0},{4,3},{5,7},{6,6},{7,2},{8,9},{9,13},{10,1... | collective-permute-start | bytes 294920 | tf_op jit(solution)/shard_map/ppermute | solution.py:56
  26.3 28.3 %collective-permute-start.8 = (bf16[256,1024]{1,0:T(8,128)(2,1)}, bf16[256,1024]{1,0:T(8,128)(2,1)}, u32[]{:S(2)}, u32[]{:S(2)}) collective-permute-start(bf16[256,1024]{1,0:T(8,128)(2,1)} %get-tuple-element.198), channel_id=1, source_target_pairs={{0,0},{1,4},{2,5},{3,1},{4,2},{5,6},{6,7},{7,3},{8,8},{9,12},{10,1... | collective-permute-start | bytes 1572872 | tf_op jit(solution)/shard_map/ppermute | solution.py:56
  32.4 22.2 %collective-permute-start.9 = (bf16[256,1024]{1,0:T(8,128)(2,1)}, bf16[256,1024]{1,0:T(8,128)(2,1)}, u32[]{:S(2)}, u32[]{:S(2)}) collective-permute-start(bf16[256,1024]{1,0:T(8,128)(2,1)} %get-tuple-element.197), channel_id=1, source_target_pairs={{0,1},{1,5},{2,4},{3,0},{4,3},{5,7},{6,6},{7,2},{8,9},{9,13},{10,1... | collective-permute-start | bytes 1572872 | tf_op jit(solution)/shard_map/ppermute | solution.py:56
  41.9 19.3 %collective-permute-start.3 = (bf16[512,2048]{1,0:T(8,128)(2,1)}, bf16[512,2048]{1,0:T(8,128)(2,1)}, u32[]{:S(2)}, u32[]{:S(2)}) collective-permute-start(bf16[512,2048]{1,0:T(8,128)(2,1)} %fusion.2.refs_5_.refs_6_), channel_id=1, source_target_pairs={{0,4},{1,5},{2,6},{3,7},{4,0},{5,1},{6,2},{7,3},{8,12},{9,13},{10,... | collective-permute-start | bytes 6291464 | tf_op jit(solution)/shard_map/ppermute | solution.py:56
  57.7 42.1 %collective-permute-start.10 = (bf16[512,1024]{1,0:T(8,128)(2,1)}, bf16[512,1024]{1,0:T(8,128)(2,1)}, u32[]{:S(2)}, u32[]{:S(2)}) collective-permute-start(bf16[512,1024]{1,0:T(8,128)(2,1)} %pad_maximum_fusion.4.gown_ref), channel_id=1, source_target_pairs={{0,4},{1,5},{2,6},{3,7},{4,0},{5,1},{6,2},{7,3},{8,12},{9,13},{10,... | collective-permute-start | bytes 3145736 | tf_op jit(solution)/shard_map/ppermute | solution.py:56
  99.3 3.0 collective-permute-start.7
  143.2 13.2 %collective-permute-start.11 = (bf16[512,1024]{1,0:T(8,128)(2,1)}, bf16[512,1024]{1,0:T(8,128)(2,1)}, u32[]{:S(2)}, u32[]{:S(2)}) collective-permute-start(bf16[512,1024]{1,0:T(8,128)(2,1)} %get-tuple-element.52), channel_id=1, source_target_pairs={{0,4},{1,5},{2,6},{3,7},{4,0},{5,1},{6,2},{7,3},{8,12},{9,13},{10,... | collective-permute-start | bytes 3145736 | tf_op jit(solution)/shard_map/ppermute | solution.py:56
  154.1 53.0 %collective-permute-start.15 = (bf16[2,1024,512]{2,1,0:T(8,128)(2,1)}, bf16[2,1024,512]{2,1,0:T(8,128)(2,1)}, u32[]{:S(2)}, u32[]{:S(2)}) collective-permute-start(bf16[2,1024,512]{2,1,0:T(8,128)(2,1)} %get-tuple-element.58), channel_id=1, source_target_pairs={{0,1},{1,0},{2,3},{3,2},{4,5},{5,4},{6,7},{7,6},{8,9},{9,8},{10,11... | collective-permute-start | bytes 6291464 | tf_op jit(solution)/shard_map/ppermute | solution.py:56
  154.1 48.4 %collective-permute-start.16 = (bf16[2,1024,512]{2,1,0:T(8,128)(2,1)}, bf16[2,1024,512]{2,1,0:T(8,128)(2,1)}, u32[]{:S(2)}, u32[]{:S(2)}) collective-permute-start(bf16[2,1024,512]{2,1,0:T(8,128)(2,1)} %get-tuple-element.60), channel_id=1, source_target_pairs={{0,2},{1,3},{2,0},{3,1},{4,6},{5,7},{6,4},{7,5},{8,10},{9,11},{10,... | collective-permute-start | bytes 6291464 | tf_op jit(solution)/shard_map/ppermute | solution.py:56
  165.1 87.8 %collective-permute-start.12 = (bf16[512,1024]{1,0:T(8,128)(2,1)}, bf16[512,1024]{1,0:T(8,128)(2,1)}, u32[]{:S(2)}, u32[]{:S(2)}) collective-permute-start(bf16[512,1024]{1,0:T(8,128)(2,1)} %get-tuple-element.53), channel_id=1, source_target_pairs={{0,4},{1,5},{2,6},{3,7},{4,0},{5,1},{6,2},{7,3},{8,12},{9,13},{10,... | collective-permute-start | bytes 3145736 | tf_op jit(solution)/shard_map/ppermute | solution.py:56
  191.8 79.3 %collective-permute-start.17 = (bf16[5,512,1024]{2,1,0:T(8,128)(2,1)}, bf16[5,512,1024]{2,1,0:T(8,128)(2,1)}, u32[]{:S(2)}, u32[]{:S(2)}) collective-permute-start(bf16[5,512,1024]{2,1,0:T(8,128)(2,1)} %get-tuple-element.63), channel_id=1, source_target_pairs={{0,4},{1,5},{2,6},{3,7},{4,0},{5,1},{6,2},{7,3},{8,12},{9,13},{10,... | collective-permute-start | bytes 15728648 | tf_op jit(solution)/shard_map/ppermute | solution.py:56
  193.6 23.4 %collective-permute-start.23 = (bf16[128,768]{1,0:T(8,128)(2,1)}, bf16[128,768]{1,0:T(8,128)(2,1)}, u32[]{:S(2)}, u32[]{:S(2)}) collective-permute-start(bf16[128,768]{1,0:T(8,128)(2,1)} %slice.384), channel_id=1, source_target_pairs={{0,4},{1,5},{2,6},{3,7},{4,0},{5,1},{6,2},{7,3},{8,12},{9,13},{10,... | collective-permute-start | bytes 589832 | tf_op jit(solution)/shard_map/ppermute | solution.py:56
  205.5 24.7 %collective-permute-start.45 = (bf16[1024,512]{1,0:T(8,128)(2,1)S(1)}, bf16[1024,512]{1,0:T(8,128)(2,1)S(1)}, u32[]{:S(2)}, u32[]{:S(2)}) collective-permute-start(bf16[1024,512]{1,0:T(8,128)(2,1)S(1)} %slice_bitcast_fusion), channel_id=1, source_target_pairs={{0,1},{1,0},{2,3},{3,2},{4,5},{5,4},{6,7},{7,6},{8,9},{9,8},{10,11... | collective-permute-start | bytes 3145736 | tf_op jit(solution)/shard_map/ppermute | solution.py:56
  210.1 24.7 %collective-permute-start.44 = (bf16[1024,512]{1,0:T(8,128)(2,1)S(1)}, bf16[1024,512]{1,0:T(8,128)(2,1)S(1)}, u32[]{:S(2)}, u32[]{:S(2)}) collective-permute-start(bf16[1024,512]{1,0:T(8,128)(2,1)S(1)} %slice_bitcast_fusion.2), channel_id=1, source_target_pairs={{0,2},{1,3},{2,0},{3,1},{4,6},{5,7},{6,4},{7,5},{8,10},{9,11},{10,... | collective-permute-start | bytes 3145736 | tf_op jit(solution)/shard_map/ppermute | solution.py:56
  217.0 46.1 %collective-permute-start.18 = (bf16[1,512,1024]{2,1,0:T(8,128)(2,1)S(1)}, bf16[1,512,1024]{2,1,0:T(8,128)(2,1)}, u32[]{:S(2)}, u32[]{:S(2)}) collective-permute-start(bf16[1,512,1024]{2,1,0:T(8,128)(2,1)S(1)} %get-tuple-element.64), channel_id=1, source_target_pairs={{0,4},{1,5},{2,6},{3,7},{4,0},{5,1},{6,2},{7,3},{8,12},{9,13},{10,... | collective-permute-start | bytes 3145736 | tf_op jit(solution)/shard_map/ppermute | solution.py:56
  235.1 14.9 %collective-permute-start.46 = (bf16[2,256,512]{2,1,0:T(8,128)(2,1)S(1)}, bf16[2,256,512]{2,1,0:T(8,128)(2,1)S(1)}, u32[]{:S(2)}, u32[]{:S(2)}) collective-permute-start(bf16[2,256,512]{2,1,0:T(8,128)(2,1)S(1)} %fusion.67), channel_id=1, source_target_pairs={{0,8},{1,9},{2,10},{3,11},{4,12},{5,13},{6,14},{7,15},{8,16},{9,17... | collective-permute-start | bytes 1572872 | tf_op jit(solution)/shard_map/ppermute | solution.py:56
  237.5 11.7 %collective-permute-start.25 = (bf16[64,768]{1,0:T(8,128)(2,1)S(1)}, bf16[64,768]{1,0:T(8,128)(2,1)S(1)}, u32[]{:S(2)}, u32[]{:S(2)}) collective-permute-start(bf16[64,768]{1,0:T(8,128)(2,1)S(1)} %get-tuple-element.207), channel_id=1, source_target_pairs={{0,3},{1,0},{2,7},{3,4},{4,2},{5,1},{6,6},{7,5},{8,11},{9,8},{10,1... | collective-permute-start | bytes 294920 | tf_op jit(solution)/shard_map/ppermute | solution.py:56
  250.9 17.3 %collective-permute-start.47 = (bf16[2,256,512]{2,1,0:T(8,128)(2,1)}, bf16[2,256,512]{2,1,0:T(8,128)(2,1)}, u32[]{:S(2)}, u32[]{:S(2)}) collective-permute-start(bf16[2,256,512]{2,1,0:T(8,128)(2,1)} %fusion.38), channel_id=1, source_target_pairs={{0,8},{1,9},{2,10},{3,11},{4,12},{5,13},{6,14},{7,15},{8,16},{9,17... | collective-permute-start | bytes 1572872 | tf_op jit(solution)/shard_map/ppermute | solution.py:56
  255.8 41.7 %collective-permute-start.13 = (bf16[256,1024]{1,0:T(8,128)(2,1)}, bf16[256,1024]{1,0:T(8,128)(2,1)}, u32[]{:S(2)}, u32[]{:S(2)}) collective-permute-start(bf16[256,1024]{1,0:T(8,128)(2,1)} %get-tuple-element.194), channel_id=1, source_target_pairs={{0,0},{1,3},{2,4},{3,7},{4,1},{5,2},{6,5},{7,6},{8,8},{9,11},{10,1... | collective-permute-start | bytes 1572872 | tf_op jit(solution)/shard_map/ppermute | solution.py:56
  261.2 36.3 %collective-permute-start.14 = (bf16[256,1024]{1,0:T(8,128)(2,1)}, bf16[256,1024]{1,0:T(8,128)(2,1)}, u32[]{:S(2)}, u32[]{:S(2)}) collective-permute-start(bf16[256,1024]{1,0:T(8,128)(2,1)} %get-tuple-element.193), channel_id=1, source_target_pairs={{0,3},{1,0},{2,7},{3,4},{4,2},{5,1},{6,6},{7,5},{8,11},{9,8},{10,1... | collective-permute-start | bytes 1572872 | tf_op jit(solution)/shard_map/ppermute | solution.py:56
  269.5 31.2 %collective-permute-start.48 = (bf16[2,256,512]{2,1,0:T(8,128)(2,1)S(1)}, bf16[2,256,512]{2,1,0:T(8,128)(2,1)S(1)}, u32[]{:S(2)}, u32[]{:S(2)}) collective-permute-start(bf16[2,256,512]{2,1,0:T(8,128)(2,1)S(1)} %fusion.39), channel_id=1, source_target_pairs={{0,8},{1,9},{2,10},{3,11},{4,12},{5,13},{6,14},{7,15},{8,16},{9,17... | collective-permute-start | bytes 1572872 | tf_op jit(solution)/shard_map/ppermute | solution.py:56
  296.5 8.9 %collective-permute-start.20 = (bf16[512,1024]{1,0:T(8,128)(2,1)S(1)}, bf16[512,1024]{1,0:T(8,128)(2,1)S(1)}, u32[]{:S(2)}, u32[]{:S(2)}) collective-permute-start(bf16[512,1024]{1,0:T(8,128)(2,1)S(1)} %get-tuple-element.69), channel_id=1, source_target_pairs={{0,4},{1,5},{2,6},{3,7},{4,0},{5,1},{6,2},{7,3},{8,12},{9,13},{10,... | collective-permute-start | bytes 3145736 | tf_op jit(solution)/shard_map/ppermute | solution.py:56
  299.1 6.7 %collective-permute-start.19 = (bf16[512,1024]{1,0:T(8,128)(2,1)S(1)}, bf16[512,1024]{1,0:T(8,128)(2,1)S(1)}, u32[]{:S(2)}, u32[]{:S(2)}) collective-permute-start(bf16[512,1024]{1,0:T(8,128)(2,1)S(1)} %get-tuple-element.67), channel_id=1, source_target_pairs={{0,4},{1,5},{2,6},{3,7},{4,0},{5,1},{6,2},{7,3},{8,12},{9,13},{10,... | collective-permute-start | bytes 3145736 | tf_op jit(solution)/shard_map/ppermute | solution.py:56
  301.7 30.7 %collective-permute-start.49 = (f32[2,128,512]{2,1,0:T(8,128)}, f32[2,128,512]{2,1,0:T(8,128)}, u32[]{:S(2)}, u32[]{:S(2)}) collective-permute-start(f32[2,128,512]{2,1,0:T(8,128)} %dynamic-slice_bitcast_fusion.1), channel_id=1, source_target_pairs={{0,4},{1,5},{2,6},{3,7},{4,0},{5,1},{6,2},{7,3},{8,12},{9,13},{10,... | collective-permute-start | bytes 1572872 | tf_op jit(solution)/shard_map/ppermute | solution.py:56
  305.2 33.3 %collective-permute-start.39 = (bf16[5,128,1024]{2,1,0:T(8,128)(2,1)}, bf16[5,128,1024]{2,1,0:T(8,128)(2,1)}, u32[]{:S(2)}, u32[]{:S(2)}) collective-permute-start(bf16[5,128,1024]{2,1,0:T(8,128)(2,1)} %add_convert_fusion.6), channel_id=1, source_target_pairs={{0,8},{1,9},{2,10},{3,11},{4,12},{5,13},{6,14},{7,15},{8,16},{9,17... | collective-permute-start | bytes 3932168 | tf_op jit(solution)/shard_map/ppermute | solution.py:56
  332.1 72.3 %collective-permute-start.31 = (bf16[1,512,3072]{2,1,0:T(8,128)(2,1)}, bf16[1,512,3072]{2,1,0:T(8,128)(2,1)}, u32[]{:S(2)}, u32[]{:S(2)}) collective-permute-start(bf16[1,512,3072]{2,1,0:T(8,128)(2,1)} %get-tuple-element.72), channel_id=1, source_target_pairs={{0,4},{1,5},{2,6},{3,7},{4,0},{5,1},{6,2},{7,3},{8,12},{9,13},{10,... | collective-permute-start | bytes 9437192 | tf_op jit(solution)/shard_map/ppermute | solution.py:56
  342.6 39.9 %collective-permute-start.40 = (bf16[5,128,1024]{2,1,0:T(8,128)(2,1)}, bf16[5,128,1024]{2,1,0:T(8,128)(2,1)}, u32[]{:S(2)}, u32[]{:S(2)}) collective-permute-start(bf16[5,128,1024]{2,1,0:T(8,128)(2,1)} %add_convert_fusion.5), channel_id=1, source_target_pairs={{0,8},{1,9},{2,10},{3,11},{4,12},{5,13},{6,14},{7,15},{8,16},{9,17... | collective-permute-start | bytes 3932168 | tf_op jit(solution)/shard_map/ppermute | solution.py:56
  348.0 4.4 collective-permute-start.26
  352.4 23.2 %collective-permute-start.27 = (f32[7,1024]{1,0:T(8,128)S(1)}, f32[7,1024]{1,0:T(8,128)S(1)}, u32[]{:S(2)}, u32[]{:S(2)}) collective-permute-start(f32[7,1024]{1,0:T(8,128)S(1)} %add.601), channel_id=1, source_target_pairs={{0,8},{1,9},{2,10},{3,11},{4,12},{5,13},{6,14},{7,15},{8,0},{9,1},... | collective-permute-start | bytes 86024 | tf_op jit(solution)/shard_map/ppermute | solution.py:56
  375.5 4.8 collective-permute-start.28
  380.4 6.9 %collective-permute-start.29 = (f32[7,1024]{1,0:T(8,128)S(1)}, f32[7,1024]{1,0:T(8,128)S(1)}, u32[]{:S(2)}, u32[]{:S(2)}) collective-permute-start(f32[7,1024]{1,0:T(8,128)S(1)} %add.603), channel_id=1, source_target_pairs={{0,1},{1,0},{2,3},{3,2},{4,5},{5,4},{6,7},{7,6},{8,9},{9,8},{10,11... | collective-permute-start | bytes 86024 | tf_op jit(solution)/shard_map/ppermute | solution.py:56
  386.5 32.8 %collective-permute-start.41 = (bf16[5,128,1024]{2,1,0:T(8,128)(2,1)}, bf16[5,128,1024]{2,1,0:T(8,128)(2,1)}, u32[]{:S(2)}, u32[]{:S(2)}) collective-permute-start(bf16[5,128,1024]{2,1,0:T(8,128)(2,1)} %add_convert_fusion.4), channel_id=1, source_target_pairs={{0,8},{1,9},{2,10},{3,11},{4,12},{5,13},{6,14},{7,15},{8,16},{9,17... | collective-permute-start | bytes 3932168 | tf_op jit(solution)/shard_map/ppermute | solution.py:56
  387.4 16.4 %collective-permute-start.30 = (f32[7,1024]{1,0:T(8,128)S(1)}, f32[7,1024]{1,0:T(8,128)S(1)}, u32[]{:S(2)}, u32[]{:S(2)}) collective-permute-start(f32[7,1024]{1,0:T(8,128)S(1)} %add.604), channel_id=1, source_target_pairs={{0,2},{1,3},{2,0},{3,1},{4,6},{5,7},{6,4},{7,5},{8,10},{9,11},{10,... | collective-permute-start | bytes 86024 | tf_op jit(solution)/shard_map/ppermute | solution.py:56
  388.6 65.0 %collective-permute-start.21 = (bf16[256,1024]{1,0:T(8,128)(2,1)}, bf16[256,1024]{1,0:T(8,128)(2,1)}, u32[]{:S(2)}, u32[]{:S(2)}) collective-permute-start(bf16[256,1024]{1,0:T(8,128)(2,1)} %get-tuple-element.190), channel_id=1, source_target_pairs={{0,0},{1,3},{2,4},{3,7},{4,1},{5,2},{6,5},{7,6},{8,8},{9,11},{10,1... | collective-permute-start | bytes 1572872 | tf_op jit(solution)/shard_map/ppermute | solution.py:56
  393.9 59.6 %collective-permute-start.22 = (bf16[256,1024]{1,0:T(8,128)(2,1)}, bf16[256,1024]{1,0:T(8,128)(2,1)}, u32[]{:S(2)}, u32[]{:S(2)}) collective-permute-start(bf16[256,1024]{1,0:T(8,128)(2,1)} %get-tuple-element.189), channel_id=1, source_target_pairs={{0,3},{1,0},{2,7},{3,4},{4,2},{5,1},{6,6},{7,5},{8,11},{9,8},{10,1... | collective-permute-start | bytes 1572872 | tf_op jit(solution)/shard_map/ppermute | solution.py:56
  419.3 24.4 %collective-permute-start.34 = (bf16[4,64,2,1024]{3,1,2,0:T(8,128)(2,1)}, bf16[4,64,2,1024]{3,1,2,0:T(8,128)(2,1)}, u32[]{:S(2)}, u32[]{:S(2)}) collective-permute-start(bf16[4,64,2,1024]{3,1,2,0:T(8,128)(2,1)} %bitcast.239), channel_id=1, source_target_pairs={{0,2},{1,3},{2,0},{3,1},{4,6},{5,7},{6,4},{7,5},{8,10},{9,11},{10,... | collective-permute-start | bytes 3145736 | tf_op jit(solution)/shard_map/ppermute | solution.py:56
  423.3 26.2 %collective-permute-start.32 = (bf16[4,64,2,1024]{3,1,0,2:T(8,128)(2,1)}, bf16[4,64,2,1024]{3,1,0,2:T(8,128)(2,1)S(1)}, u32[]{:S(2)}, u32[]{:S(2)}) collective-permute-start(bf16[4,64,2,1024]{3,1,0,2:T(8,128)(2,1)} %slice_bitcast_fusion.5), channel_id=1, source_target_pairs={{0,1},{1,0},{2,3},{3,2},{4,5},{5,4},{6,7},{7,6},{8,9},{9,8},{10,11... | collective-permute-start | bytes 3145736 | tf_op jit(solution)/shard_map/ppermute | solution.py:56
  445.4 15.4 %collective-permute-start.35 = (bf16[4,64,1024]{2,1,0:T(8,128)(2,1)S(1)}, bf16[4,64,1024]{2,1,0:T(8,128)(2,1)S(1)}, u32[]{:S(2)}, u32[]{:S(2)}) collective-permute-start(bf16[4,64,1024]{2,1,0:T(8,128)(2,1)S(1)} %slice_bitcast_fusion.7), channel_id=1, source_target_pairs={{0,1},{1,0},{2,3},{3,2},{4,5},{5,4},{6,7},{7,6},{8,9},{9,8},{10,11... | collective-permute-start | bytes 1572872 | tf_op jit(solution)/shard_map/ppermute | solution.py:56
  451.2 12.9 %collective-permute-start.33 = (bf16[4,64,1024]{2,1,0:T(8,128)(2,1)S(1)}, bf16[4,64,1024]{2,1,0:T(8,128)(2,1)S(1)}, u32[]{:S(2)}, u32[]{:S(2)}) collective-permute-start(bf16[4,64,1024]{2,1,0:T(8,128)(2,1)S(1)} %slice_bitcast_fusion.9), channel_id=1, source_target_pairs={{0,2},{1,3},{2,0},{3,1},{4,6},{5,7},{6,4},{7,5},{8,10},{9,11},{10,... | collective-permute-start | bytes 1572872 | tf_op jit(solution)/shard_map/ppermute | solution.py:56
  451.4 22.9 %collective-permute-start.42 = (bf16[128,2,1280]{2,0,1:T(8,128)(2,1)S(1)}, bf16[128,2,1280]{2,0,1:T(8,128)(2,1)S(1)}, u32[]{:S(2)}, u32[]{:S(2)}) collective-permute-start(bf16[128,2,1280]{2,0,1:T(8,128)(2,1)S(1)} %dynamic-slice_bitcast_fusion), channel_id=1, source_target_pairs={{0,1},{1,0},{2,3},{3,2},{4,5},{5,4},{6,7},{7,6},{8,9},{9,8},{10,11... | collective-permute-start | bytes 1966088 | tf_op jit(solution)/shard_map/ppermute | solution.py:56
  464.3 10.1 %collective-permute-start.36 = (bf16[2,64,1024]{2,1,0:T(8,128)(2,1)S(1)}, bf16[2,64,1024]{2,1,0:T(8,128)(2,1)S(1)}, u32[]{:S(2)}, u32[]{:S(2)}) collective-permute-start(bf16[2,64,1024]{2,1,0:T(8,128)(2,1)S(1)} %fusion.82), channel_id=1, source_target_pairs={{0,8},{1,9},{2,10},{3,11},{4,12},{5,13},{6,14},{7,15},{8,16},{9,17... | collective-permute-start | bytes 786440 | tf_op jit(solution)/shard_map/ppermute | solution.py:56
  474.5 9.6 %collective-permute-start.37 = (bf16[2,64,1024]{2,1,0:T(8,128)(2,1)S(1)}, bf16[2,64,1024]{2,1,0:T(8,128)(2,1)S(1)}, u32[]{:S(2)}, u32[]{:S(2)}) collective-permute-start(bf16[2,64,1024]{2,1,0:T(8,128)(2,1)S(1)} %fusion.68), channel_id=1, source_target_pairs={{0,8},{1,9},{2,10},{3,11},{4,12},{5,13},{6,14},{7,15},{8,16},{9,17... | collective-permute-start | bytes 786440 | tf_op jit(solution)/shard_map/ppermute | solution.py:56
  475.2 9.1 %collective-permute-start.43 = (bf16[128,1280]{1,0:T(8,128)(2,1)S(1)}, bf16[128,1280]{1,0:T(8,128)(2,1)S(1)}, u32[]{:S(2)}, u32[]{:S(2)}) collective-permute-start(bf16[128,1280]{1,0:T(8,128)(2,1)S(1)} %dynamic-slice_bitcast_fusion.10), channel_id=1, source_target_pairs={{0,2},{1,3},{2,0},{3,1},{4,6},{5,7},{6,4},{7,5},{8,10},{9,11},{10,... | collective-permute-start | bytes 983048 | tf_op jit(solution)/shard_map/ppermute | solution.py:56
  484.2 8.7 %collective-permute-start.38 = (bf16[2,64,1024]{2,1,0:T(8,128)(2,1)S(1)}, bf16[2,64,1024]{2,1,0:T(8,128)(2,1)S(1)}, u32[]{:S(2)}, u32[]{:S(2)}) collective-permute-start(bf16[2,64,1024]{2,1,0:T(8,128)(2,1)S(1)} %fusion.69), channel_id=1, source_target_pairs={{0,8},{1,9},{2,10},{3,11},{4,12},{5,13},{6,14},{7,15},{8,16},{9,17... | collective-permute-start | bytes 786440 | tf_op jit(solution)/shard_map/ppermute | solution.py:56
  (98 other events, 690.1 us)
where the time goes:
time: 504 us; the launch traced here: 495 us
  Pallas kernels  128 us (25%)
  local copies, waits for them, and re-layouts  86.9 us (17%)
  waiting for transfers between devices  86.3 us (17%)
  other arithmetic  84.1 us (17%)
  starting transfers between devices  70.8 us (14%)
  matrix products  31.2 us (6%)
  between operations  6.91 us (1%)
    ppermute x50, waiting for transfers between devices, permute(): return lax.ppermute(value, (ROWS, SEQ), pairs)  86.3 us
    ppermute x50, starting transfers between devices, permute(): return lax.ppermute(value, (ROWS, SEQ), pairs)  70.8 us
    pallas_call x4, Pallas kernels, attention_call(): pl.pallas_call(kernel, grid=(pairs,), in_specs=in_specs, out_specs=out_sp...  67.5 us
    pallas_call x1, Pallas kernels, feed(): pl.pallas_call(functools.partial(feed_kernel, (nx, ny, nz, chunk)), grid_...  40.9 us
    dot_general x13, matrix products, dot(): lax.dot_general(left, right, (((left_dim,), (right_dim,)), ((), ())), pre...  31.2 us
    pallas_call x3, Pallas kernels, weight_parts(): pl.pallas_call(without(functools.partial(weight_kernel, (count, place.nz)...  20 us
    convert_element_type x7, other arithmetic, ring_sum(): value = pieces[k]() + send(value.astype(BF)).astype(F32)  13.7 us
    unnamed x205, local copies, waits for them, and re-layouts  11.3 us
  transfers between devices with their start and end apart: 50, of which 14 were waited for; matrix products, arithmetic and copies ran while one was open for 39% of the time, Pallas kernels for 18%

commit v1 on v0

--- a/solution.py
+++ b/solution.py
@@ -689,6 +689,634 @@
     )(meta, *lefts, *rights, *before)
 
 
+MESH = pl.DeviceIdType.MESH
+
+
+class Mail:
+    def __init__(self, send_sems, recv_sems):
+        self.send_sems, self.recv_sems, self.sent = send_sems, recv_sems, []
+
+    def send(self, source, target, device):
+        number = len(self.sent)
+        copy = pltpu.make_async_remote_copy(
+            src_ref=source,
+            dst_ref=target,
+            send_sem=self.send_sems.at[number],
+            recv_sem=self.recv_sems.at[number],
+            device_id=device,
+            device_id_type=MESH,
+        )
+        copy.start()
+        self.sent.append(copy)
+        return copy
+
+    def finish(self):
+        for copy in self.sent:
+            copy.wait_send()
+
+
+class Ways:
+    def __init__(self, nz):
+        self.row, self.spot = lax.axis_index(ROWS), lax.axis_index(SEQ)
+        self.core, self.z = self.row % 2, self.row // 2
+        self.x, self.y = self.spot % 2, self.spot // 2
+        self.nz = nz
+        self.sibling = (self.row + 1 - 2 * self.core, self.spot)
+        self.across_x = (self.row, self.spot + 1 - 2 * self.x)
+        self.across_y = (self.row, self.y * -2 + 2 + self.x)
+        self.above = ((self.row + 2) % (2 * nz), self.spot)
+        self.below = ((self.row + 2 * nz - 2) % (2 * nz), self.spot)
+
+    def plane(self):
+        devices = []
+        for other in range(2):
+            row = self.row if other == 0 else self.sibling[0]
+            devices += [(row, (self.spot + s) % 4) for s in range(4) if other or s]
+        return devices
+
+    def meet(self, devices):
+        barrier = pltpu.get_barrier_semaphore()
+        for device in devices:
+            pl.semaphore_signal(barrier, inc=1, device_id=device, device_id_type=MESH)
+        pl.semaphore_wait(barrier, len(devices))
+
+    def place(self, q):
+        return (self.y + 1 + q % 2) % 2 * 2 + (self.x + 1 + q // 2) % 2
+
+    def rows(self, k, which, block):
+        start = ((self.z + 1 + k) % self.nz * 2 + which) * block
+        return pl.ds(pl.multiple_of(start, block), block)
+
+
+class Home:
+    def __init__(self, ways, out_ref, send_sems, recv_sems):
+        self.ways, self.out_ref = ways, out_ref
+        self.send_sems, self.recv_sems = send_sems, recv_sems
+        self.started = []
+
+    def send(self, source, slot):
+        ways = self.ways
+        spot = jnp.where(ways.core == 0, 3 * slot, 1 + slot)
+        row = 2 * ways.z + ways.spot // 2
+        stays = (spot == ways.spot) & (row == ways.row)
+        to = self.out_ref.at[ways.spot % 2]
+        copy = pltpu.make_async_remote_copy(
+            src_ref=source,
+            dst_ref=to,
+            send_sem=self.send_sems.at[slot],
+            recv_sem=self.recv_sems.at[ways.spot % 2],
+            device_id=(row, spot),
+            device_id_type=MESH,
+        )
+        local = pltpu.make_async_copy(source, to, self.recv_sems.at[ways.spot % 2])
+
+        @pl.when(stays)
+        def _():
+            local.start()
+
+        @pl.when(jnp.logical_not(stays))
+        def _():
+            copy.start()
+
+        self.started.append((stays, copy))
+
+    def finish(self):
+        for r in range(2):
+            to = self.out_ref.at[r]
+            pltpu.make_async_copy(to, to, self.recv_sems.at[r]).wait()
+        for stays, copy in self.started:
+
+            @pl.when(jnp.logical_not(stays))
+            def _(copy=copy):
+                copy.wait_send()
+
+
+def middle_kernel(
+    shape,
+    mixed_ref,
+    normed_ref,
+    projected_ref,
+    text_ref,
+    self_ref,
+    g_second_ref,
+    g_query_ref,
+    g_keys_ref,
+    g_values_ref,
+    g_projected_ref,
+    g_first_ref,
+    send_up_ref,
+    send_low_ref,
+    keep_up_ref,
+    keep_low_ref,
+    mixed_t,
+    normed_t,
+    projected_t,
+    text_t,
+    self_t,
+    own_ref,
+    away_ref,
+    got_ref,
+    send_sems,
+    recv_sems,
+):
+    nz, piece = shape
+    ways = Ways(nz)
+    ways.meet([ways.sibling])
+    mail = Mail(send_sems, recv_sems)
+    for left, to in ((mixed_ref, mixed_t), (normed_ref, normed_t), (projected_ref, projected_t), (self_ref, self_t)):
+        to[...] = turned(left[...])
+    turned_text = turned(text_ref[...])
+    block = own_ref.shape[2]
+    count = 2 * nz
+    part = turned_text.shape[0] // count
+    text_t[...] = jnp.zeros_like(text_t)
+    for b in range(count):
+        text_t[b * block : b * block + part] = turned_text[b * part : (b + 1) * part]
+    half = block // 2
+    up, low = slice(0, half), slice(half, block)
+    homes = (
+        (send_up_ref.at[0], send_low_ref.at[0]),
+        (send_up_ref.at[1], keep_low_ref.at[0]),
+        (keep_up_ref.at[0], send_low_ref.at[1]),
+        (keep_up_ref.at[1], keep_low_ref.at[1]),
+    )
+    copies = []
+
+    def settle(q):
+        copies[q].wait_recv()
+        total = own_ref[q] + got_ref[q]
+        homes[q][0][...] = total[:, up]
+        homes[q][1][...] = total[:, low]
+
+    for q in range(4):
+        place = ways.place(q)
+        columns = pl.ds(pl.multiple_of(place * piece, piece), piece)
+        twice = pl.ds(pl.multiple_of(place % 2 * 2 * piece, piece), 2 * piece)
+        pair = jnp.where(place < 2, g_keys_ref[:, twice], g_values_ref[:, twice])
+        units = (
+            (mixed_t, g_second_ref[:, columns]),
+            (normed_t, g_query_ref[:, columns]),
+            (projected_t, pair),
+            (text_t, g_projected_ref[:, columns]),
+            (self_t, g_first_ref[:, columns]),
+        )
+        for which, ref in ((1 - ways.core, away_ref), (ways.core, own_ref)):
+            first = 0
+            for left, right in units:
+                to = slice(first, first + right.shape[1])
+                first += right.shape[1]
+                for k in range(nz):
+                    ref[q, k, :, to] = dot(left[ways.rows(k, which, block)], right).astype(BF)
+            if ref is away_ref:
+                copies.append(mail.send(away_ref.at[q], got_ref.at[q], ways.sibling))
+        if q > 0:
+            settle(q - 1)
+    settle(3)
+    mail.finish()
+
+
+def middle_parts(place, lefts, rights):
+    nz = place.nz
+    depth, width = lefts[0].shape[1], rights[0].shape[1]
+    piece, block = width // place.seq, depth // place.rows
+    columns = piece * len(rights)
+    out = jax.ShapeDtypeStruct((2, nz, block // 2, columns), BF)
+    big = pltpu.VMEM((4, nz, block, columns), BF)
+    return pl.pallas_call(
+        functools.partial(middle_kernel, (nz, piece)),
+        in_specs=[WHOLE_SPEC] * 11,
+        out_specs=[WHOLE_SPEC] * 4,
+        out_shape=[out] * 4,
+        scratch_shapes=[pltpu.VMEM((depth, left.shape[0]), BF) for left in lefts]
+        + [big] * 3
+        + [pltpu.SemaphoreType.DMA((4,))] * 2,
+        compiler_params=pltpu.CompilerParams(
+            collective_id=2, has_side_effects=True, vmem_limit_bytes=VMEM_LIMIT
+        ),
+        cost_estimate=pl.CostEstimate(
+            flops=2 * 8 * 512 * depth * width, bytes_accessed=24 << 20, transcendentals=0
+        ),
+    )(*lefts, *rights)
+
+
+def final_kernel(nz, *refs):
+    (
+        normed_ref,
+        input_ref,
+        first_ref,
+        gain_ref,
+        weight_ref,
+        gq_ref,
+        gk_ref,
+        gv_ref,
+        k_away_ref,
+        v_away_ref,
+        upper_ref,
+        upper_got_ref,
+        lower_ref,
+        lower_got_ref,
+        in_keep_ref,
+        in_got_ref,
+        out_keep_ref,
+        out_got_ref,
+        vector_ref,
+        result_ref,
+        result_away_ref,
+        text_ref,
+    ) = refs[:22]
+    (qkv_ref, middle_ref, feed_ref, sum_ref, result_out, frames_out, text_out) = refs[22:29]
+    (
+        packed_ref,
+        k_got_ref,
+        v_got_ref,
+        acc_ref,
+        turned_ref,
+        own_ref,
+        away_ref,
+        got_ref,
+        first_x_ref,
+        first_y_ref,
+        second_y_ref,
+        second_x_ref,
+        mid_up_ref,
+        mid_low_ref,
+        mid_ref,
+        mid_ring_ref,
+        qkv_ring_ref,
+        feed_send_ref,
+        feed_ring_ref,
+        feed_away_ref,
+        feed_other_ref,
+        vector_out_ref,
+        vector_in_ref,
+        result_got_ref,
+        text_away_ref,
+        text_got_ref,
+        send_sems,
+        recv_sems,
+        home_sends,
+        home_recvs,
+    ) = refs[29:]
+    ways = Ways(nz)
+    core, z = ways.core, ways.z
+    sibling, across_x, across_y, above = ways.sibling, ways.across_x, ways.across_y, ways.above
+    ways.meet(ways.plane() + [ways.above, ways.below])
+    mail = Mail(send_sems, recv_sems)
+    ring = ring_order(nz)
+    half = upper_ref.shape[2]
+    feed_rows = feed_ring_ref.shape[2]
+    tokens, width = normed_ref.shape
+
+    k_copy = mail.send(k_away_ref, k_got_ref, sibling)
+    v_copy = mail.send(v_away_ref, v_got_ref, sibling)
+
+    def feed_piece(kind, k):
+        keep, got = ((in_keep_ref, in_got_ref), (out_keep_ref, out_got_ref))[kind]
+        at = slice(k * feed_rows, (k + 1) * feed_rows)
+        return keep[at].astype(F32) + got[at].astype(F32)
+
+    def feed_send(t, kind):
+        return mail.send(feed_send_ref.at[kind, t], feed_ring_ref.at[kind, t], above)
+
+    feed_copies = {}
+    for kind in range(2):
+        feed_send_ref[kind, 0] = feed_piece(kind, ring[0]).astype(BF)
+        feed_copies[kind, 0] = feed_send(0, kind)
+
+    mid_copies = {}
+    for k in ring:
+        mid_ref[k, :half] = upper_ref[0, k] + upper_got_ref[0, k]
+        mid_ref[k, half:] = lower_ref[0, k] + lower_got_ref[0, k]
+        mid_copies[k] = (
+            mail.send(mid_ref.at[k, :half], mid_up_ref.at[k], across_y),
+            mail.send(mid_ref.at[k, half:], mid_low_ref.at[k], across_x),
+        )
+    result_copy = mail.send(result_away_ref, result_got_ref, sibling)
+    text_rows = text_ref.shape[0] // 2
+    text_away_ref[...] = text_ref[text_rows:].astype(BF)
+    text_copy = mail.send(text_away_ref, text_got_ref, sibling)
+
+    turned_ref[...] = turned(normed_ref[...])
+    packed_ref[:, :width] = gq_ref[...]
+    k_copy.wait_recv()
+    packed_ref[:, width : 2 * width] = gk_ref[...] + k_got_ref[...]
+    v_copy.wait_recv()
+    packed_ref[:, 2 * width :] = gv_ref[...] + v_got_ref[...]
+
+    block = own_ref.shape[2]
+    columns = own_ref.shape[3]
+    core_copies = []
+    for q in range(4):
+        right = packed_ref[:, pl.ds(pl.multiple_of(ways.place(q) * columns, columns), columns)]
+        for which, ref in ((1 - core, away_ref), (core, own_ref)):
+            for k in range(nz):
+                ref[q, k] = dot(turned_ref[ways.rows(k, which, block)], right).astype(BF)
+            if ref is away_ref:
+                core_copies.append(mail.send(away_ref.at[q], got_ref.at[q], sibling))
+
+    def feed_step(t):
+        for kind in range(2):
+            feed_copies[kind, t - 1].wait_recv()
+            total = feed_piece(kind, ring[t]) + feed_ring_ref[kind, t - 1].astype(F32)
+            if t < nz - 1:
+                feed_send_ref[kind, t] = total.astype(BF)
+                feed_copies[kind, t] = feed_send(t, kind)
+            else:
+                feed_finish(kind, total)
+
+    def feed_finish(kind, total):
+        rows = total.shape[0] // 2
+        away = jnp.where(core == 0, total[rows:], total[:rows])
+        own = jnp.where(core == 0, total[:rows], total[rows:])
+        across = total.shape[1]
+        feed_away_ref[kind] = away
+        feed_copies[kind, nz] = mail.send(feed_away_ref.at[kind], feed_other_ref.at[kind], sibling)
+        at = pl.ds(pl.multiple_of(core * across, across), across)
+        feed_ref[kind, :, at] = own
+
+    def feed_last(kind):
+        feed_copies[kind, nz].wait_recv()
+        across = feed_other_ref.shape[2]
+        at = pl.ds(pl.multiple_of((1 - core) * across, across), across)
+        feed_ref[kind, :, at] = feed_other_ref[kind]
+
+    def core_step(q):
+        core_copies[q].wait_recv()
+        own_ref[q] = own_ref[q] + got_ref[q]
+
+    mid_ring = {}
+
+    def mid_send(t):
+        k = ring[t]
+        up, low = mid_copies[k]
+        up.wait()
+        low.wait()
+        mid_ref[k, :half] = upper_ref[1, k] + upper_got_ref[1, k] + mid_up_ref[k]
+        mid_ref[k, half:] = lower_ref[1, k] + lower_got_ref[1, k] + mid_low_ref[k]
+        if t > 0:
+            mid_ring[t - 1].wait_recv()
+        if t == nz - 1:
+            middle_ref[...] = mid_ref[k].astype(F32) + mid_ring_ref[t - 1].astype(F32)
+            return
+        if t > 0:
+            mid_ref[k] = mid_ref[k] + mid_ring_ref[t - 1]
+        mid_ring[t] = mail.send(mid_ref.at[k], mid_ring_ref.at[t], above)
+
+    qkv_ring = {}
+
+    def qkv_send(t):
+        k = ring[t]
+        if t > 0:
+            qkv_ring[t - 1].wait_recv()
+        if t == nz - 1:
+            qkv_ref[...] = own_ref[3, k].astype(F32) + qkv_ring_ref[t - 1].astype(F32)
+            return
+        if t > 0:
+            own_ref[3, k] = own_ref[3, k] + qkv_ring_ref[t - 1]
+        qkv_ring[t] = mail.send(own_ref.at[3, k], qkv_ring_ref.at[t], above)
+
+    up, low = slice(0, half), slice(half, 2 * half)
+    core_step(0)
+    upper_first = [mail.send(own_ref.at[0, :, up], first_x_ref.at[0], across_x)]
+    lower_first = [mail.send(own_ref.at[0, :, low], first_y_ref.at[0], across_y)]
+    core_step(1)
+    upper_first.append(mail.send(own_ref.at[1, :, up], first_x_ref.at[1], across_x))
+    core_step(2)
+    lower_first.append(mail.send(own_ref.at[2, :, low], first_y_ref.at[1], across_y))
+    core_step(3)
+
+    result_copy.wait_recv()
+    slots = tokens // 2
+    result_got_ref[...] = (result_ref[...] + result_got_ref[...].astype(F32)).astype(BF)
+    result_home = Home(ways, result_out, home_sends.at[0], home_recvs.at[0])
+    for slot in range(2):
+        result_home.send(result_got_ref.at[slot * slots : (slot + 1) * slots], slot)
+    text_copy.wait_recv()
+    text_got_ref[...] = (text_ref[:text_rows] + text_got_ref[...].astype(F32)).astype(BF)
+    text_home = Home(ways, text_out, home_sends.at[1], home_recvs.at[1])
+    for slot in range(2):
+        at = slice(slot * text_rows // 2, (slot + 1) * text_rows // 2)
+        text_home.send(text_got_ref.at[at], slot)
+
+    acc_ref[...] = nt(packed_ref[:, :width], weight_ref[:, :width])
+    acc_ref[...] += nt(packed_ref[:, width : 2 * width], weight_ref[:, width : 2 * width])
+    mid_send(0)
+    feed_step(1)
+    acc_ref[...] += nt(packed_ref[:, 2 * width :], weight_ref[:, 2 * width :])
+    gain_sum = jnp.zeros((1, width), F32)
+    shift_sum = jnp.zeros((1, width), F32)
+    chunk = min(128, tokens)
+    for m in range(tokens // chunk):
+        at = slice(m * chunk, (m + 1) * chunk)
+        grad, gain_part, shift_part = norm_backward(
+            input_ref[at].astype(F32), gain_ref[...], acc_ref[at]
+        )
+        k_got_ref[at] = (first_ref[at] + grad).astype(BF)
+        gain_sum += gain_part[None]
+        shift_sum += shift_part[None]
+    frames_home = Home(ways, frames_out, home_sends.at[2], home_recvs.at[2])
+    for slot in range(2):
+        frames_home.send(k_got_ref.at[slot * slots : (slot + 1) * slots], slot)
+    vector_out_ref[0] = vector_ref[...]
+    vector_out_ref[0, 0:1] = gain_sum
+    vector_out_ref[0, 1:2] = shift_sum
+    vector_copy = mail.send(vector_out_ref.at[0], vector_in_ref.at[0], sibling)
+    mid_send(1)
+
+    vector_copy.wait_recv()
+    vector_out_ref[1] = vector_out_ref[0] + vector_in_ref[0]
+    vector_copy = mail.send(vector_out_ref.at[1], vector_in_ref.at[1], across_x)
+    for t in range(2, nz):
+        feed_step(t)
+        if t < nz - 1:
+            mid_send(t)
+    vector_copy.wait_recv()
+    vector_out_ref[2] = vector_out_ref[1] + vector_in_ref[1]
+    vector_copy = mail.send(vector_out_ref.at[2], vector_in_ref.at[2], across_y)
+
+    upper_first[0].wait_recv()
+    own_ref[2, :, up] = own_ref[2, :, up] + first_x_ref[0]
+    upper_second = mail.send(own_ref.at[2, :, up], second_y_ref, across_y)
+    lower_first[0].wait_recv()
+    own_ref[1, :, low] = own_ref[1, :, low] + first_y_ref[0]
+    lower_second = mail.send(own_ref.at[1, :, low], second_x_ref, across_x)
+    vector_copy.wait_recv()
+    vector_out_ref[3] = vector_out_ref[2] + vector_in_ref[2]
+    vector_copy = mail.send(vector_out_ref.at[3], vector_in_ref.at[3], above)
+    upper_first[1].wait_recv()
+    own_ref[3, :, up] = own_ref[3, :, up] + first_x_ref[1]
+    lower_first[1].wait_recv()
+    own_ref[3, :, low] = own_ref[3, :, low] + first_y_ref[1]
+    mid_send(nz - 1)
+    for kind in range(2):
+        feed_last(kind)
+    total = vector_out_ref[3]
+    for t in range(nz - 1):
+        vector_copy.wait_recv()
+        total = total + vector_in_ref[3 + t]
+        if t < nz - 2:
+            vector_copy = mail.send(vector_in_ref.at[3 + t], vector_in_ref.at[4 + t], above)
+    sum_ref[...] = total
+    upper_second.wait_recv()
+    own_ref[3, :, up] = own_ref[3, :, up] + second_y_ref[...]
+    lower_second.wait_recv()
+    own_ref[3, :, low] = own_ref[3, :, low] + second_x_ref[...]
+    for t in range(nz):
+        qkv_send(t)
+    result_home.finish()
+    text_home.finish()
+    frames_home.finish()
+    for number, copy in enumerate(mail.sent):
+        if not any(copy is c for pair in mid_copies.values() for c in pair):
+            copy.wait_send()
+
+
+def final_sums(place, count, *operands):
+    nz = place.nz
+    normed, weight, upper, in_keep = operands[0], operands[4], operands[10], operands[14]
+    vectors, text = operands[18], operands[21]
+    tokens, width = normed.shape
+    block, piece = width // place.rows, weight.shape[1] // place.seq
+    half, middle = block // 2, upper.shape[3]
+    feed_width = in_keep.shape[1]
+    feed_rows = width // nz
+    copies = 2 + 2 * nz + 2 * nz + 2 + 4 + 3 + nz - 1 + 4 + 2 + 2 * (nz - 1)
+    vmem = pltpu.VMEM
+    return pl.pallas_call(
+        functools.partial(final_kernel, nz),
+        in_specs=[WHOLE_SPEC] * 22,
+        out_specs=[WHOLE_SPEC] * 4 + [ANY_SPEC] * 3,
+        out_shape=[
+            jax.ShapeDtypeStruct((block, piece), F32),
+            jax.ShapeDtypeStruct((block, middle), F32),
+            jax.ShapeDtypeStruct((2, block, 2 * feed_width), F32),
+            jax.ShapeDtypeStruct(vectors.shape, F32),
+            jax.ShapeDtypeStruct((count, tokens // count, width), BF),
+            jax.ShapeDtypeStruct((count, tokens // count, width), BF),
+            jax.ShapeDtypeStruct((count, text.shape[0] // 2 // count, text.shape[1]), BF),
+        ],
+        scratch_shapes=[
+            vmem((tokens, 3 * width), BF),
+            vmem((tokens, width), BF),
+            vmem((tokens, width), BF),
+            vmem((tokens, width), F32),
+            vmem((width, tokens), BF),
+            vmem((4, nz, block, piece), BF),
+            vmem((4, nz, block, piece), BF),
+            vmem((4, nz, block, piece), BF),
+            vmem((2, nz, half, piece), BF),
+            vmem((2, nz, half, piece), BF),
+            vmem((nz, half, piece), BF),
+            vmem((nz, half, piece), BF),
+            vmem((nz, half, middle), BF),
+            vmem((nz, half, middle), BF),
+            vmem((nz, block, middle), BF),
+            vmem((nz - 1, block, middle), BF),
+            vmem((nz - 1, block, piece), BF),
+            vmem((2, nz - 1, feed_rows, feed_width), BF),
+            vmem((2, nz - 1, feed_rows, feed_width), BF),
+            vmem((2, feed_rows // 2, feed_width), F32),
+            vmem((2, feed_rows // 2, feed_width), F32),
+            vmem((4,) + vectors.shape, F32),
+            vmem((2 + nz,) + vectors.shape, F32),
+            vmem((tokens, width), BF),
+            vmem((text.shape[0] // 2, text.shape[1]), BF),
+            vmem((text.shape[0] // 2, text.shape[1]), BF),
+            pltpu.SemaphoreType.DMA((copies,)),
+            pltpu.SemaphoreType.DMA((copies,)),
+            pltpu.SemaphoreType.DMA((3, 2)),
+            pltpu.SemaphoreType.DMA((3, 2)),
+        ],
+        compiler_params=pltpu.CompilerParams(
+            collective_id=1, has_side_effects=True, vmem_limit_bytes=63 * 1024 * 1024
+        ),
+        cost_estimate=pl.CostEstimate(
+            flops=60 * tokens * width * weight.shape[1], bytes_accessed=40 << 20, transcendentals=0
+        ),
+    )(*operands)
+
+
+def permuted_sums(place, meta, in_half, out_half, lefts, rights, normed_self, backward_self):
+    nx, ny, nz, seq = place.nx, place.ny, place.nz, place.seq
+    width = normed_self.shape[1]
+    block, piece = width // place.rows, width // seq
+    middle_own, middle_away = weight_parts(
+        place, meta, lefts[:3] + lefts[2:4], rights[:5]
+    )
+    out_own, out_away = weight_parts(place, meta, lefts[4:], rights[5:])
+    middle_got = place.swap_core(middle_away)
+    out_got = place.swap_core(out_away)
+    grad_packed = backward_self(in_half, out_half, middle_got, out_got)
+    in_quarter = ring_sum([lambda k=k: in_half[k].astype(F32) for k in range(ny)], place.next_y)
+    out_quarter = ring_sum([lambda k=k: out_half[k].astype(F32) for k in range(nx)], place.next_x)
+    feed_quarter = jnp.stack([in_quarter, out_quarter]).astype(BF)
+    feed_quarter = feed_quarter.reshape(2, nz, -1, feed_quarter.shape[2])
+    feed_own = ring_sum([lambda k=k: feed_quarter[:, k].astype(F32) for k in range(nz)], place.next_z)
+    feed_own = feed_own.reshape(2, 2, block, -1)
+    feed_got = place.swap_core(pick(feed_own, 1 - place.core, 1))
+    feed_own = pick(feed_own, place.core, 1)
+    low = jnp.where(place.core == 0, feed_own, feed_got)
+    high = jnp.where(place.core == 0, feed_got, feed_own)
+    sum_feed = jnp.concatenate([low, high], axis=2)
+
+    def middle_piece(k):
+        at = slice(k * block, (k + 1) * block)
+        return lambda: middle_own[:, at].astype(F32) + middle_got[:, at].astype(F32)
+
+    middle = ring_sum([middle_piece(k) for k in range(nz)], place.next_z).astype(BF)
+    spread = jnp.concatenate(
+        [
+            middle[0].reshape(block, seq, -1),
+            middle[1].reshape(block, seq, -1),
+            jnp.concatenate([middle[2], middle[3]], axis=1).reshape(block, seq, -1),
+            middle[4].reshape(block, seq, -1),
+        ],
+        axis=2,
+    ).reshape(block, ny, nx, -1)
+
+    def shifted(array, index, number, length, axis):
+        return lambda: pick(array, (index + 1 + number) % length, axis).astype(F32)
+
+    spread = ring_sum([shifted(spread, place.x, k, nx, 2) for k in range(nx)], place.next_x).astype(BF)
+    spread = ring_sum([shifted(spread, place.y, k, ny, 1) for k in range(ny)], place.next_y)
+    relative_parts = place.relative_columns(grad_packed, True)
+    qkv_own, qkv_away = weight_parts(place, meta, [normed_self], [relative_parts])
+    qkv_got = place.swap_core(qkv_away)
+
+    def columns(array):
+        return array[0].reshape(array.shape[1], nx, ny, -1)
+
+    def natural(array):
+        return jnp.stack(
+            [
+                jnp.stack(
+                    [
+                        pick(array[0].reshape(array.shape[1], seq, -1), place.offset(i, j), 1)
+                        for i in range(ny)
+                    ],
+                    axis=1,
+                )
+                for j in range(nx)
+            ],
+            axis=1,
+        )
+
+    last_own = jnp.concatenate([columns(qkv_own), natural(out_own)], axis=3)
+    last_got = jnp.concatenate([columns(qkv_got), natural(out_got)], axis=3)
+    last = (last_own.astype(F32) + last_got.astype(F32)).astype(BF)
+    last = last.reshape(nz, 2, block // 2, nx, ny, -1)
+    upper = ring_sum([lambda k=k: last[:, 0, :, k].astype(F32) for k in range(nx)], place.next_x).astype(BF)
+    lower = ring_sum([lambda k=k: last[:, 1, :, :, k].astype(F32) for k in range(ny)], place.next_y).astype(BF)
+    upper = ring_sum([lambda a=upper[:, :, k]: a.astype(F32) for k in range(ny)], place.next_y)
+    lower = ring_sum([lambda a=lower[:, :, k]: a.astype(F32) for k in range(nx)], place.next_x)
+    last = jnp.stack([upper, lower], axis=1).astype(BF)
+    last = ring_sum([lambda a=last[k]: a.astype(F32) for k in range(nz)], place.next_z)
+    last = last.reshape(block, -1)
+    sum_self_qkv, sum_self_out = last[:, : 3 * piece], last[:, 3 * piece :]
+
+    return sum_feed, spread, sum_self_qkv, sum_self_out, grad_packed
+
+
 def shards(
     frames,
     text_states,
@@ -794,8 +1422,6 @@
         cross_mix,
         cross_lse,
     )
-    result = (second + result + place.swap_core(after(result_away, grad_cross_mix)).astype(F32)).astype(BF)
-    result = place.from_rows(result, count)
     grad_normed_cross = dot(grad_cross_queries, cross_query, 1, 1)
     grad_part, grad_cross_gain, grad_cross_shift = norm_backward(first, cross_gain, grad_normed_cross)
     grad_first = grad_second + grad_part
@@ -804,132 +1430,107 @@
 
     grad_pair = jnp.concatenate([grad_text_keys, grad_text_values], axis=1)
     grad_projected = dot(grad_pair, cross_kv, 1, 1).astype(BF)
-    text_blocks = text_input.reshape(text_total, place.rows, -1)
-    padding = width // place.rows - text_blocks.shape[2]
-    text_padded = jnp.pad(text_blocks, ((0, 0), (0, 0), (0, padding))).reshape(text_total, width)
-    middle_own, middle_away = weight_parts(
-        place,
-        meta,
-        [cross_mix, normed_cross, projected, projected, text_padded],
-        [grad_second_branch, grad_cross_queries, grad_text_keys, grad_text_values, grad_projected],
-    )
-    out_own, out_away = weight_parts(place, meta, [self_mix], [grad_first_branch])
-    middle_got = place.swap_core(middle_away)
-    out_got = place.swap_core(out_away)
     grad_text_bias = jnp.sum(grad_projected.astype(F32), axis=0)
     grad_text = dot(grad_projected, text_proj, 1, 1)
-
-    grad_queries, grad_keys, grad_values, keys_away, values_away = self_backward(
-        core,
-        query_segment,
-        own_segment,
-        other_segment,
-        queries,
-        pair,
-        pair_other,
-        grad_self_mix,
-        self_mix,
-        self_lse,
-        before=(in_half, out_half, middle_got, out_got),
-    )
-    grad_keys = (grad_keys.astype(F32) + place.swap_core(keys_away).astype(F32)).astype(BF)
-    grad_values = (grad_values.astype(F32) + place.swap_core(values_away).astype(F32)).astype(BF)
-    grad_packed = jnp.concatenate([grad_queries, grad_keys, grad_values], axis=1)
-
-    in_quarter = ring_sum([lambda k=k: in_half[k].astype(F32) for k in range(ny)], place.next_y)
-    out_quarter = ring_sum([lambda k=k: out_half[k].astype(F32) for k in range(nx)], place.next_x)
-    feed_quarter = jnp.stack([in_quarter, out_quarter]).astype(BF)
-    feed_quarter = feed_quarter.reshape(2, nz, -1, feed_quarter.shape[2])
-    feed_own = ring_sum([lambda k=k: feed_quarter[:, k].astype(F32) for k in range(nz)], place.next_z)
-    block = width // place.rows
-    feed_own = feed_own.reshape(2, 2, block, -1)
-    feed_got = place.swap_core(pick(feed_own, 1 - place.core, 1))
-    feed_own = pick(feed_own, place.core, 1)
-    low = jnp.where(place.core == 0, feed_own, feed_got)
-    high = jnp.where(place.core == 0, feed_got, feed_own)
-    sum_feed = jnp.concatenate([low, high], axis=2)
-
-    def middle_piece(k):
-        at = slice(k * block, (k + 1) * block)
-        return lambda: middle_own[:, at].astype(F32) + middle_got[:, at].astype(F32)
-
-    middle = ring_sum([middle_piece(k) for k in range(nz)], place.next_z).astype(BF)
-    spread = jnp.concatenate(
-        [
-            middle[0].reshape(block, seq, -1),
-            middle[1].reshape(block, seq, -1),
-            jnp.concatenate([middle[2], middle[3]], axis=1).reshape(block, seq, -1),
-            middle[4].reshape(block, seq, -1),
-        ],
-        axis=2,
-    ).reshape(block, ny, nx, -1)
-
-    def shifted(array, index, number, length, axis):
-        return lambda: pick(array, (index + 1 + number) % length, axis).astype(F32)
-
-    spread = ring_sum([shifted(spread, place.x, k, nx, 2) for k in range(nx)], place.next_x).astype(BF)
-    spread = ring_sum([shifted(spread, place.y, k, ny, 1) for k in range(ny)], place.next_y)
-    piece = width // seq
-    sum_cross_out, sum_cross_query = spread[:, :piece], spread[:, piece : 2 * piece]
-    sum_cross_kv, sum_text_proj = spread[:, 2 * piece : 4 * piece], spread[:, 4 * piece :]
-    sum_text_proj = sum_text_proj[: block - padding]
-
-    relative_parts = place.relative_columns(grad_packed, True)
-    qkv_own, qkv_away = weight_parts(place, meta, [normed_self], [relative_parts])
-    qkv_got = place.swap_core(qkv_away)
-
-    def columns(array):
-        return array[0].reshape(array.shape[1], nx, ny, -1)
-
-    def natural(array):
+    block, piece = width // place.rows, width // seq
+    padding = block - text_input.shape[1] // place.rows
+    lefts = [cross_mix, normed_cross, projected, text_input, self_mix]
+    rights = [
+        grad_second_branch,
+        grad_cross_queries,
+        grad_text_keys,
+        grad_text_values,
+        grad_projected,
+        grad_first_branch,
+    ]
+    result = second + result
+
+    def backward_self(*before):
+        return self_backward(
+            core,
+            query_segment,
+            own_segment,
+            other_segment,
+            queries,
+            pair,
+            pair_other,
+            grad_self_mix,
+            self_mix,
+            self_lse,
+            before=before,
+        )
+
+    def vector_list(grad_gain, grad_shift):
         return jnp.stack(
             [
-                jnp.stack(
-                    [
-                        pick(array[0].reshape(array.shape[1], seq, -1), place.offset(i, j), 1)
-                        for i in range(ny)
-                    ],
-                    axis=1,
-                )
-                for j in range(nx)
-            ],
-            axis=1,
-        )
-
-    last_own = jnp.concatenate([columns(qkv_own), natural(out_own)], axis=3)
-    last_got = jnp.concatenate([columns(qkv_got), natural(out_got)], axis=3)
-    last = (last_own.astype(F32) + last_got.astype(F32)).astype(BF)
-    last = last.reshape(nz, 2, block // 2, nx, ny, -1)
-    upper = ring_sum([lambda k=k: last[:, 0, :, k].astype(F32) for k in range(nx)], place.next_x).astype(BF)
-    lower = ring_sum([lambda k=k: last[:, 1, :, :, k].astype(F32) for k in range(ny)], place.next_y).astype(BF)
-    upper = ring_sum([lambda a=upper[:, :, k]: a.astype(F32) for k in range(ny)], place.next_y)
-    lower = ring_sum([lambda a=lower[:, :, k]: a.astype(F32) for k in range(nx)], place.next_x)
-    last = jnp.stack([upper, lower], axis=1).astype(BF)
-    last = ring_sum([lambda a=last[k]: a.astype(F32) for k in range(nz)], place.next_z)
-    last = last.reshape(block, -1)
-    sum_self_qkv, sum_self_out = last[:, : 3 * piece], last[:, 3 * piece :]
-
-    grad_normed_self = dot(grad_packed, self_qkv, 1, 1)
-    grad_part, grad_self_gain, grad_self_shift = norm_backward(layer_input, self_gain, grad_normed_self)
-    grad_frames = place.from_rows((grad_first + grad_part).astype(BF), count)
-    half = grad_text.shape[0] // 2
-    text_away = place.swap_core(grad_text[half:].astype(BF))
-    grad_text = place.from_rows((grad_text[:half] + text_away.astype(F32)).astype(BF), count)
-
-    vectors = place.vector_sum(
-        jnp.stack(
-            [
-                grad_self_gain,
-                grad_self_shift,
+                grad_gain,
+                grad_shift,
                 grad_cross_gain,
                 grad_cross_shift,
                 grad_text_bias,
                 grad_feed_gain,
                 grad_feed_shift,
+                jnp.zeros_like(grad_feed_shift),
             ]
         )
-    )
-    vectors = pick(vectors.reshape(7, seq, width // seq), place.spot, 1)
+
+    if nx == 2 and ny == 2 and piece % 128 == 0:
+        send_up, send_low, keep_up, keep_low = middle_parts(place, lefts, rights)
+        up_got, low_got = place.next_x(send_up), place.next_y(send_low)
+        in_got, out_got = place.next_y(in_half[0]), place.next_x(out_half[0])
+        grads = backward_self(in_half[0], out_half[0])
+        nothing = jnp.zeros_like(grad_feed_shift)
+        sum_self_qkv, spread, sum_feed, vectors, result, grad_frames, grad_text = final_sums(
+            place,
+            count,
+            normed_self,
+            layer_raw,
+            grad_first,
+            self_gain[None],
+            self_qkv,
+            *grads,
+            keep_up,
+            up_got,
+            keep_low,
+            low_got,
+            in_half[1],
+            in_got,
+            out_half[1],
+            out_got,
+            vector_list(nothing, nothing),
+            result,
+            result_away,
+            grad_text,
+        )
+        sum_self_out = spread[:, 5 * piece :]
+    else:
+
+        def packed_self(*before):
+            grads = backward_self(*before)
+            keys = (grads[1].astype(F32) + place.swap_core(grads[3]).astype(F32)).astype(BF)
+            values = (grads[2].astype(F32) + place.swap_core(grads[4]).astype(F32)).astype(BF)
+            return jnp.concatenate([grads[0], keys, values], axis=1)
+
+        text_blocks = text_input.reshape(text_total, place.rows, -1)
+        text_padded = jnp.pad(text_blocks, ((0, 0), (0, 0), (0, padding))).reshape(text_total, width)
+        lefts[3] = text_padded
+        sum_feed, spread, sum_self_qkv, sum_self_out, grad_packed = permuted_sums(
+            place, meta, in_half, out_half, lefts, rights, normed_self, packed_self
+        )
+        result = (result + place.swap_core(result_away).astype(F32)).astype(BF)
+        result = place.from_rows(result, count)
+        grad_normed_self = dot(grad_packed, self_qkv, 1, 1)
+        grad_part, grad_gain, grad_shift = norm_backward(layer_input, self_gain, grad_normed_self)
+        grad_frames = place.from_rows((grad_first + grad_part).astype(BF), count)
+        half = grad_text.shape[0] // 2
+        text_away = place.swap_core(grad_text[half:].astype(BF))
+        grad_text = (grad_text[:half] + text_away.astype(F32)).astype(BF)
+        grad_text = place.from_rows(grad_text, count)
+        vectors = place.vector_sum(vector_list(grad_gain, grad_shift))
+    sum_cross_out, sum_cross_query = spread[:, :piece], spread[:, piece : 2 * piece]
+    sum_cross_kv, sum_text_proj = spread[:, 2 * piece : 4 * piece], spread[:, 4 * piece : 5 * piece]
+    sum_text_proj = sum_text_proj[: block - padding]
+    vectors = pick(vectors.reshape(8, seq, width // seq), place.spot, 1)
     return (
         result,
         grad_frames.astype(F32),

time: 504 us -> 380 us (0.75)
  Pallas kernels: 128 us -> 232 us
  local copies, waits for them, and re-layouts: 86.9 us -> 26.5 us
  other arithmetic: 84.1 us -> 26.4 us
  waiting for transfers between devices: 86.3 us -> 31.7 us
  starting transfers between devices: 70.8 us -> 26.4 us
    pallas_call x3 -> x2, Pallas kernels: 20 us -> 123 us  [the longest x1 107 us: final_sums(): pl.pallas_call(functools.partial(final_kernel, nz), in_specs=[WHOLE_SPEC]...]
    ppermute x50 -> x18, waiting for transfers between devices: 86.3 us -> 31.7 us  [permute(): return lax.ppermute(value, (ROWS, SEQ), pairs)]
    ppermute x50 -> x18, starting transfers between devices: 70.8 us -> 26.4 us  [permute(): return lax.ppermute(value, (ROWS, SEQ), pairs)]
    concatenate x16 -> x0, local copies, waits for them, and re-layouts: 33.9 us -> none  [the longest x6 8.19 us: shards(): jnp.concatenate([middle[0].reshape(block, seq, -1), middle[1].reshape(blo...]
    convert_element_type x17 -> x0, other arithmetic: 28.1 us -> none  [the longest x7 13.7 us: ring_sum(): value = pieces[k]() + send(value.astype(BF)).astype(F32)]
    dynamic_slice x4 -> x1, local copies, waits for them, and re-layouts: 10.9 us -> 0.01 us  [pick(): return lax.dynamic_index_in_dim(array, index, axis, keepdims=False)]
    another operation x16 -> x2, other arithmetic: 10.5 us -> 0.36 us  [the longest x3 3.24 us: from_rows(): stacked = jnp.stack(got)]
    reshape x3 -> x0, local copies, waits for them, and re-layouts: 7.64 us -> none  [the longest x1 5.59 us: relative_columns(): blocks = value.reshape(value.shape[0], self.seq, -1)]
  transfers between devices with their start and end apart: 50 -> 18, of which waited for: 14 -> 7; matrix products, arithmetic and copies ran while one was open for 39% -> 15% of each run, Pallas kernels for 18% -> 22%
where the time goes in v1:
time: 380 us; the launch traced here: 375 us
  Pallas kernels  232 us (61%)
  waiting for transfers between devices  31.7 us (8%)
  matrix products  27.4 us (7%)
  local copies, waits for them, and re-layouts  26.5 us (7%)
  starting transfers between devices  26.4 us (7%)
  other arithmetic  26.4 us (7%)
  between operations  4.72 us (1%)
    pallas_call x1, Pallas kernels, final_sums(): pl.pallas_call(functools.partial(final_kernel, nz), in_specs=[WHOLE_SPEC]...  107 us
    pallas_call x4, Pallas kernels, attention_call(): pl.pallas_call(kernel, grid=(pairs,), in_specs=in_specs, out_specs=out_sp...  67.5 us
    pallas_call x1, Pallas kernels, feed(): pl.pallas_call(functools.partial(feed_kernel, (nx, ny, nz, chunk)), grid_...  41.2 us
    ppermute x18, waiting for transfers between devices, permute(): return lax.ppermute(value, (ROWS, SEQ), pairs)  31.7 us
    dot_general x12, matrix products, dot(): lax.dot_general(left, right, (((left_dim,), (right_dim,)), ((), ())), pre...  27.4 us
    ppermute x18, starting transfers between devices, permute(): return lax.ppermute(value, (ROWS, SEQ), pairs)  26.4 us
    pallas_call x1, Pallas kernels, middle_parts(): pl.pallas_call(functools.partial(middle_kernel, (nz, piece)), in_specs=[W...  16.7 us
    unnamed x133, local copies, waits for them, and re-layouts  12.8 us
  transfers between devices with their start and end apart: 18, of which 7 were waited for; matrix products, arithmetic and copies ran while one was open for 15% of the time, Pallas kernels for 22%

profile of v1, /device:TPU:0, one launch (start us, length us, event | category | flops | bytes accessed | tf_op | source)
XLA Modules:
  0.0 375.3 jit_solution(17693468743437897483)
XLA Ops:
  0.7 1.3 dynamic_slice.55
  4.6 1.3 dynamic-slice_bitcast_fusion.2
  6.6 6.1 %collective-permute-start.1 = (bf16[256,1024]{1,0:T(8,128)(2,1)S(1)}, bf16[256,1024]{1,0:T(8,128)(2,1)S(1)}, u32[]{:S(2)}, u32[]{:S(2)}) collective-permute-start(bf16[256,1024]{1,0:T(8,128)(2,1)S(1)} %get-tuple-element.163), channel_id=1, source_target_pairs={{0,1},{1,5},{2,4},{3,0},{4,3},{5,7},{6,6},{7,2},{8,9},{9,13},{10,1... | collective-permute-start | bytes 1572872 | tf_op jit(solution)/shard_map/ppermute | solution.py:56
  12.8 1.6 collective-permute-start.4
  15.0 4.8 %collective-permute-start.7 = (bf16[64,768]{1,0:T(8,128)(2,1)S(1)}, bf16[64,768]{1,0:T(8,128)(2,1)S(1)}, u32[]{:S(2)}, u32[]{:S(2)}) collective-permute-start(bf16[64,768]{1,0:T(8,128)(2,1)S(1)} %get-tuple-element.170), channel_id=1, source_target_pairs={{0,1},{1,5},{2,4},{3,0},{4,3},{5,7},{6,6},{7,2},{8,9},{9,13},{10,1... | collective-permute-start | bytes 294920 | tf_op jit(solution)/shard_map/ppermute | solution.py:56
  20.2 6.3 %collective-permute-done.1 = bf16[256,1024]{1,0:T(8,128)(2,1)S(1)} collective-permute-done((bf16[256,1024]{1,0:T(8,128)(2,1)S(1)}, bf16[256,1024]{1,0:T(8,128)(2,1)S(1)}, u32[]{:S(2)}, u32[]{:S(2)}) %collective-permute-start.1) | collective-permute-done | bytes 524320 | tf_op jit(solution)/shard_map/ppermute | solution.py:56
  28.1 1.3 copy-done.55
  29.4 3.7 fusion.2.refs_5_.refs_6_
  35.1 2.8 collective-permute-done.8
  37.9 2.1 fusion.16.projected_ref
  41.2 2.1 collective-permute-start.3
  44.3 1.3 convolution_convert_fusion.refs_3_.refs_4_
  45.6 2.8 fusion.13.refs_4_
  48.5 9.3 %collective-permute-done.3 = bf16[256,1024]{1,0:T(8,128)(2,1)S(1)} collective-permute-done((bf16[256,1024]{1,0:T(8,128)(2,1)S(1)}, bf16[256,1024]{1,0:T(8,128)(2,1)S(1)}, u32[]{:S(2)}, u32[]{:S(2)}) %collective-permute-start.3) | collective-permute-done | bytes 524320 | tf_op jit(solution)/shard_map/ppermute | solution.py:56
  58.2 1.1 pad_maximum_fusion.1.gown_ref
  59.3 2.1 collective-permute-start.10
  61.4 17.5 %shard_map.358 = (bf16[512,1024]{1,0:T(8,128)(2,1)S(1)}, f32[8,8,512]{2,1,0:T(8,128)S(1)}) custom-call(s32[1]{0:T(128)} %bitcast.13.refs_0_, s32[1,512]{1,0:T(1,128)S(1)} %bitcast.94, s32[512,1]{1,0:T(8,128)S(1)} %copy.49.refs_2_, s32[512,1]{1,0:T(8,128)S(1)} %copy.50.refs_3_, bf16[512,1024]{1,0:T(8,128)(2,1)S(1)} %fusion.13.refs_4_, ...), custom_call_target="tpu_custom_call" | custom-call | flops 5368709120 | bytes 8388608 | tf_op jit(solution)/shard_map/pallas_call | solution.py:424
  79.0 1.3 fusion.37
  82.7 1.3 convolution_convert_fusion.3.refs_2_
  84.0 11.9 %shard_map.359 = (bf16[512,1024]{1,0:T(8,128)(2,1)S(1)}, f32[8,8,512]{2,1,0:T(8,128)S(1)}) custom-call(s32[1,512]{1,0:T(1,128)S(1)} %bitcast.95, s32[256,1]{1,0:T(8,128)S(1)} %copy.51.refs_1_, bf16[512,1024]{1,0:T(8,128)(2,1)S(1)} %convolution_convert_fusion.3.refs_2_, bf16[256,2048]{1,0:T(8,128)(2,1)S(1)} %convolution_convert_fusion.refs_3_.refs_4_, ...), custom_call_target="tpu_custom_call" | custom-call | flops 2147483648 | bytes 8388608 | tf_op jit(solution)/shard_map/pallas_call | solution.py:424
  95.9 1.4 fusion.38
  98.6 1.4 add_convert_fusion.2.own_ref
  100.6 2.4 collective-permute-done.9.other_ref
  103.0 41.2 %shard_map.360 = (f32[512,1024]{1,0:T(8,128)}, bf16[512,1024]{1,0:T(8,128)(2,1)}, f32[512,1024]{1,0:T(8,128)}, bf16[512,1024]{1,0:T(8,128)(2,1)}, bf16[2,1024,51...) custom-call(s32[4]{0:T(128)} %pad_add_fusion.4.meta_ref, ...), custom_call_target="tpu_custom_call" | custom-call | flops 25769803776 | bytes 41943040 | tf_op jit(solution)/shard_map/pallas_call | solution.py:613
  145.4 1.7 collective-permute-start.13
  147.3 4.2 %multiply_reduce_fusion = (f32[1024]{0:T(1024)}, f32[512]{0:T(512)S(1)}, f32[512]{0:T(512)S(1)}, f32[1024]{0:T(1024)}) fusion(f32[512,1024]{1,0:T(8,128)} %copy-done.15, f32[512]{0:T(512)} %copy-done.41, f32[512]{0:T(512)S(1)} %broadcast_multiply_fusion.4, f32[512,1024]{1,0:T(8,128)} %get-tuple-element.53, bf16[512,1024]{1,0:T(8,128)(2,1)} %collective-permute-done.11, ...), kind=kLoop, calls=%fused_computation.15 | loop fusion | flops 5764096 | bytes 5263360 | tf_op jit(solution)/shard_map/reduce_sum | solution.py:159
  151.6 3.9 %fusion.35 = (bf16[512,1024]{1,0:T(8,128)(2,1)S(1)}, f32[512,1024]{1,0:T(8,128)S(1)}, f32[512,1024]{1,0:T(8,128)}) fusion(f32[512]{0:T(512)S(1)} %broadcast_multiply_fusion.2, f32[512,1024]{1,0:T(8,128)S(1)} %copy-done.16, f32[512]{0:T(512)S(1)} %broadcast_multiply_fusion.4, f32[512]{0:T(512)S(1)} %broadcast_multiply_fusion.3, f32[1024]{0:T(1024)S(1)} %copy-done.40, ...), kind=kLoop, calls=%fused_computation.124 | loop fusion | flops 8388608 | bytes 13643776 | tf_op jit(solution)/shard_map/convert_element_type | solution.py:1414
  155.5 1.3 convolution_convert_fusion.2.refs_5_
  157.1 12.4 %shard_map.361 = (bf16[512,1024]{1,0:T(8,128)(2,1)S(1)}, bf16[256,1024]{1,0:T(8,128)(2,1)S(1)}, bf16[256,1024]{1,0:T(8,128)(2,1)S(1)}) custom-call(s32[1,512]{1,0:T(1,128)S(1)} %bitcast.96, s32[256,1]{1,0:T(8,128)S(1)} %copy.51.refs_1_, bf16[512,1024]{1,0:T(8,128)(2,1)S(1)} %copy-done.8, bf16[256,2048]{1,0:T(8,128)(2,1)S(1)} %convolution_convert_fusion.refs_3_.refs_4_, ...), custom_call_target="tpu_custom_call" | custom-call | flops 5368709120 | bytes 8388608 | tf_op jit(solution)/shard_map/pallas_call | solution.py:424
  169.6 3.8 %multiply_reduce_fusion.1 = (f32[1024]{0:T(1024)S(1)}, f32[512]{0:T(512)S(1)}, f32[512]{0:T(512)S(1)}, f32[1024]{0:T(1024)S(1)}, f32[512,1024]{1,0:T(8,128)S(1)}) fusion(f32[512,1024]{1,0:T(8,128)S(1)} %copy-done.18, f32[512]{0:T(512)S(1)} %copy-done.44, f32[512]{0:T(512)S(1)} %broadcast_multiply_fusion.5, f32[1024]{0:T(1024)S(1)} %copy-done.46, ...), kind=kOutput, calls=%fused_computation.16 | convolution fusion | flops 1078457344 | bytes 7360512 | tf_op jit(solution)/shard_map/dot_general | solution.py:23
  173.3 1.3 convert_reduce_fusion.1
  174.7 2.4 fusion.34
  177.2 16.7 %shard_map.363 = (bf16[2,4,64,1536]{3,2,1,0:T(8,128)(2,1)}, bf16[2,4,64,1536]{3,2,1,0:T(8,128)(2,1)}, bf16[2,4,64,1536]{3,2,1,0:T(8,128)(2,1)}, bf16[2,4,64,1536]{3,2,1,0:T(8,128)(2,1)}) custom-call(bf16[512,1024]{1,0:T(8,128)(2,1)S(1)} %copy-done.5, bf16[512,1024]{1,0:T(8,128)(2,1)S(1)} %add_convert_fusion.3.normed_ref, bf16[256,1024]{1,0:T(8,128)(2,1)S(1)} %copy-done.1, ...), custom_call_target="tpu_custom_call" | custom-call | flops 8589934592 | bytes 25165824 | tf_op jit(solution)/shard_map/pallas_call | solution.py:885
  193.9 1.9 collective-permute-start.14
  196.9 2.9 fusion.39.refs_21_
  199.8 4.3 %convolution_convert_fusion.1.refs_9_ = bf16[512,1024]{1,0:T(8,128)(2,1)} fusion(bf16[512,1024]{1,0:T(8,128)(2,1)S(1)} %copy-done.24, bf16[1024,1024]{1,0:T(8,128)(2,1)} %param.30), kind=kOutput, calls=%fused_computation.34 | convolution fusion | flops 1074266112 | bytes 4194304 | tf_op jit(solution)/shard_map/dot_general | solution.py:23
  204.1 2.2 add_convert_fusion
  207.5 1.5 collective-permute-start.17
  208.9 2.2 add_convert_fusion.1
  213.2 25.7 %shard_map.362 = (bf16[512,1024]{1,0:T(8,128)(2,1)S(1)}, bf16[512,1024]{1,0:T(8,128)(2,1)S(1)}, bf16[512,1024]{1,0:T(8,128)(2,1)S(1)}, bf16[512,1024]{1,0:T(8,128)(2,1)S(1)}, bf16[512,1024]{1,0:T(8,128)(2,1)S(1)}) custom-call(s32[1]{0:T(128)} %bitcast.13.refs_0_, s32[1,512]{1,0:T(1,128)S(1)} %bitcast.97, s32[512,1]{1,0:T(8,128)S(1)} %copy.49.refs_2_, ...), custom_call_target="tpu_custom_call" | custom-call | flops 13421772800 | bytes 8388608 | tf_op jit(solution)/shard_map/pallas_call | solution.py:424
  243.9 9.2 %collective-permute-done.17.refs_17_ = bf16[1024,512]{1,0:T(8,128)(2,1)S(1)} collective-permute-done((bf16[1024,512]{1,0:T(8,128)(2,1)S(1)}, bf16[1024,512]{1,0:T(8,128)(2,1)S(1)}, u32[]{:S(2)}, u32[]{:S(2)}) %collective-permute-start.17) | collective-permute-done | bytes 1048608 | tf_op jit(solution)/shard_map/ppermute | solution.py:56
  253.1 1.5 collective-permute-done.16.refs_15_
  255.5 106.6 %shard_map.364 = (f32[128,768]{1,0:T(8,128)}, f32[128,1536]{1,0:T(8,128)}, f32[2,128,1024]{2,1,0:T(8,128)}, f32[8,1024]{1,0:T(8,128)}, bf16[2,256,1024]{2,1,0:T(...) custom-call(bf16[512,1024]{1,0:T(8,128)(2,1)} %copy-done.26, ...), custom_call_target="tpu_custom_call" | custom-call | flops 96636764160 | bytes 41943040 | tf_op jit(solution)/shard_map/pallas_call | solution.py:1185
  362.1 1.9 fusion.36
  364.0 1.8 slice.95
  365.8 1.5 slice.93
  367.3 1.6 convert_element_type.114
  371.6 1.5 constant_dynamic-slice_fusion.6
  (205 shorter events, 28.3 us)
Async XLA Ops:
  0.7 12.0 %copy-start.54 = (s32[2,4]{1,0:T(2,128)S(1)}, s32[2,4]{1,0:T(2,128)}, u32[]{:S(2)}) copy-start(s32[2,4]{1,0:T(2,128)} %param.25) | copy-start | bytes 100
  0.7 12.0 %copy-start.53 = (s32[2,4]{1,0:T(2,128)S(1)}, s32[2,4]{1,0:T(2,128)}, u32[]{:S(2)}) copy-start(s32[2,4]{1,0:T(2,128)} %param.26) | copy-start | bytes 100
  0.7 13.7 %copy-start.37 = (bf16[2,64,768]{2,1,0:T(8,128)(2,1)S(1)}, bf16[2,64,768]{2,1,0:T(8,128)(2,1)}, u32[]{:S(2)}) copy-start(bf16[2,64,768]{2,1,0:T(8,128)(2,1)} %param.24) | copy-start | bytes 589828
  5.9 14.3 %collective-permute-start = (bf16[256,1024]{1,0:T(8,128)(2,1)S(1)}, bf16[256,1024]{1,0:T(8,128)(2,1)S(1)}, u32[]{:S(2)}, u32[]{:S(2)}) collective-permute-start(bf16[256,1024]{1,0:T(8,128)(2,1)S(1)} %get-tuple-element.164), channel_id=1, source_target_pairs={{0,0},{1,4},{2,5},{3,1},{4,2},{5,6},{6,7},{7,3},{8,8},{9,12},{10,1... | collective-permute-start | bytes 1572872 | tf_op jit(solution)/shard_map/ppermute | solution.py:56
  6.6 20.0 %collective-permute-start.1 = (bf16[256,1024]{1,0:T(8,128)(2,1)S(1)}, bf16[256,1024]{1,0:T(8,128)(2,1)S(1)}, u32[]{:S(2)}, u32[]{:S(2)}) collective-permute-start(bf16[256,1024]{1,0:T(8,128)(2,1)S(1)} %get-tuple-element.163), channel_id=1, source_target_pairs={{0,1},{1,5},{2,4},{3,0},{4,3},{5,7},{6,6},{7,2},{8,9},{9,13},{10,1... | collective-permute-start | bytes 1572872 | tf_op jit(solution)/shard_map/ppermute | solution.py:56
  12.8 7.4 %collective-permute-start.4 = (s32[2,8]{1,0:T(2,128)S(1)}, s32[2,8]{1,0:T(2,128)S(1)}, u32[]{:S(2)}, u32[]{:S(2)}) collective-permute-start(s32[2,8]{1,0:T(2,128)S(1)} %pad_add_fusion.2), channel_id=1, source_target_pairs={{0,4},{1,5},{2,6},{3,7},{4,0},{5,1},{6,2},{7,3},{8,12},{9,13},{10,... | collective-permute-start | bytes 200 | tf_op jit(solution)/shard_map/ppermute | solution.py:56
  14.3 19.7 %collective-permute-start.6 = (bf16[64,768]{1,0:T(8,128)(2,1)S(1)}, bf16[64,768]{1,0:T(8,128)(2,1)S(1)}, u32[]{:S(2)}, u32[]{:S(2)}) collective-permute-start(bf16[64,768]{1,0:T(8,128)(2,1)S(1)} %get-tuple-element.171), channel_id=1, source_target_pairs={{0,0},{1,4},{2,5},{3,1},{4,2},{5,6},{6,7},{7,3},{8,8},{9,12},{10,1... | collective-permute-start | bytes 294920 | tf_op jit(solution)/shard_map/ppermute | solution.py:56
  15.0 19.0 %collective-permute-start.7 = (bf16[64,768]{1,0:T(8,128)(2,1)S(1)}, bf16[64,768]{1,0:T(8,128)(2,1)S(1)}, u32[]{:S(2)}, u32[]{:S(2)}) collective-permute-start(bf16[64,768]{1,0:T(8,128)(2,1)S(1)} %get-tuple-element.170), channel_id=1, source_target_pairs={{0,1},{1,5},{2,4},{3,0},{4,3},{5,7},{6,6},{7,2},{8,9},{9,13},{10,1... | collective-permute-start | bytes 294920 | tf_op jit(solution)/shard_map/ppermute | solution.py:56
  29.4 8.5 %copy-start.64 = (f32[1024]{0:T(1024)S(1)}, f32[1024]{0:T(1024)}, u32[]{:S(2)}) copy-start(f32[1024]{0:T(1024)} %param.35) | copy-start | bytes 12292
  33.0 28.4 %collective-permute-start.5 = (bf16[512,2048]{1,0:T(8,128)(2,1)}, bf16[512,2048]{1,0:T(8,128)(2,1)}, u32[]{:S(2)}, u32[]{:S(2)}) collective-permute-start(bf16[512,2048]{1,0:T(8,128)(2,1)} %fusion.2.refs_5_.refs_6_), channel_id=1, source_target_pairs={{0,4},{1,5},{2,6},{3,7},{4,0},{5,1},{6,2},{7,3},{8,12},{9,13},{10,... | collective-permute-start | bytes 6291464 | tf_op jit(solution)/shard_map/ppermute | solution.py:56
  34.1 5.8 %copy-start.34 = (bf16[64,768]{1,0:T(8,128)(2,1)}, bf16[64,768]{1,0:T(8,128)(2,1)S(1)}, u32[]{:S(2)}) copy-start(bf16[64,768]{1,0:T(8,128)(2,1)S(1)} %get-tuple-element.168) | copy-start | bytes 294916
  34.1 5.8 %copy-start.35 = (bf16[64,768]{1,0:T(8,128)(2,1)}, bf16[64,768]{1,0:T(8,128)(2,1)S(1)}, u32[]{:S(2)}) copy-start(bf16[64,768]{1,0:T(8,128)(2,1)S(1)} %get-tuple-element.169) | copy-start | bytes 294916
  34.2 3.7 collective-permute-start.8
  35.1 6.0 %copy-start.30 = (bf16[2,256,1024]{2,1,0:T(8,128)(2,1)S(1)}, bf16[2,256,1024]{2,1,0:T(8,128)(2,1)}, u32[]{:S(2)}) copy-start(bf16[2,256,1024]{2,1,0:T(8,128)(2,1)} %param.42) | copy-start | bytes 3145732
  40.0 4.3 %copy-start = (bf16[256,1024]{1,0:T(8,128)(2,1)}, bf16[256,1024]{1,0:T(8,128)(2,1)S(1)}, u32[]{:S(2)}) copy-start(bf16[256,1024]{1,0:T(8,128)(2,1)S(1)} %fusion.16.projected_ref) | copy-start | bytes 1572868
  40.0 4.3 %copy-start.56 = (bf16[1024,2048]{1,0:T(8,128)(2,1)S(1)}, bf16[1024,2048]{1,0:T(8,128)(2,1)}, u32[]{:S(2)}) copy-start(bf16[1024,2048]{1,0:T(8,128)(2,1)} %param.36) | copy-start | bytes 12582916
  41.2 16.6 %collective-permute-start.3 = (bf16[256,1024]{1,0:T(8,128)(2,1)S(1)}, bf16[256,1024]{1,0:T(8,128)(2,1)S(1)}, u32[]{:S(2)}, u32[]{:S(2)}) collective-permute-start(bf16[256,1024]{1,0:T(8,128)(2,1)S(1)} %get-tuple-element.159), channel_id=1, source_target_pairs={{0,1},{1,5},{2,4},{3,0},{4,3},{5,7},{6,6},{7,2},{8,9},{9,13},{10,1... | collective-permute-start | bytes 1572872 | tf_op jit(solution)/shard_map/ppermute | solution.py:56
  43.2 14.6 %collective-permute-start.2 = (bf16[256,1024]{1,0:T(8,128)(2,1)S(1)}, bf16[256,1024]{1,0:T(8,128)(2,1)S(1)}, u32[]{:S(2)}, u32[]{:S(2)}) collective-permute-start(bf16[256,1024]{1,0:T(8,128)(2,1)S(1)} %get-tuple-element.160), channel_id=1, source_target_pairs={{0,0},{1,4},{2,5},{3,1},{4,2},{5,6},{6,7},{7,3},{8,8},{9,12},{10,1... | collective-permute-start | bytes 1572872 | tf_op jit(solution)/shard_map/ppermute | solution.py:56
  48.4 13.0 %copy-start.9 = (bf16[512,1024]{1,0:T(8,128)(2,1)}, bf16[512,1024]{1,0:T(8,128)(2,1)S(1)}, u32[]{:S(2)}) copy-start(bf16[512,1024]{1,0:T(8,128)(2,1)S(1)} %fusion.13.refs_4_) | copy-start | bytes 3145732
  59.3 41.2 %collective-permute-start.10 = (bf16[512,1024]{1,0:T(8,128)(2,1)}, bf16[512,1024]{1,0:T(8,128)(2,1)}, u32[]{:S(2)}, u32[]{:S(2)}) collective-permute-start(bf16[512,1024]{1,0:T(8,128)(2,1)} %pad_maximum_fusion.1.gown_ref), channel_id=1, source_target_pairs={{0,4},{1,5},{2,6},{3,7},{4,0},{5,1},{6,2},{7,3},{8,12},{9,13},{10,... | collective-permute-start | bytes 3145736 | tf_op jit(solution)/shard_map/ppermute | solution.py:56
  61.4 17.6 %copy-start.61 = (bf16[1024,1024]{1,0:T(8,128)(2,1)S(1)}, bf16[1024,1024]{1,0:T(8,128)(2,1)}, u32[]{:S(2)}) copy-start(bf16[1024,1024]{1,0:T(8,128)(2,1)} %param.30) | copy-start | bytes 6291460
  80.4 15.6 %copy-start.17 = (f32[512,1024]{1,0:T(8,128)}, f32[512,1024]{1,0:T(8,128)S(1)}, u32[]{:S(2)}) copy-start(f32[512,1024]{1,0:T(8,128)S(1)} %get-tuple-element.182) | copy-start | bytes 6291460
  84.0 11.9 %copy-start.7 = (bf16[512,1024]{1,0:T(8,128)(2,1)}, bf16[512,1024]{1,0:T(8,128)(2,1)S(1)}, u32[]{:S(2)}) copy-start(bf16[512,1024]{1,0:T(8,128)(2,1)S(1)} %convolution_convert_fusion.3.refs_2_) | copy-start | bytes 3145732
  84.0 11.9 %copy-start.58 = (bf16[1024,1024]{1,0:T(8,128)(2,1)S(1)}, bf16[1024,1024]{1,0:T(8,128)(2,1)}, u32[]{:S(2)}) copy-start(bf16[1024,1024]{1,0:T(8,128)(2,1)} %param.37) | copy-start | bytes 6291460
  100.0 3.0 collective-permute-start.9
  144.2 3.1 collective-permute-start.11
  145.4 58.7 %collective-permute-start.13 = (bf16[2,1024,512]{2,1,0:T(8,128)(2,1)}, bf16[2,1024,512]{2,1,0:T(8,128)(2,1)}, u32[]{:S(2)}, u32[]{:S(2)}) collective-permute-start(bf16[2,1024,512]{2,1,0:T(8,128)(2,1)} %get-tuple-element.61), channel_id=1, source_target_pairs={{0,2},{1,3},{2,0},{3,1},{4,6},{5,7},{6,4},{7,5},{8,10},{9,11},{10,... | collective-permute-start | bytes 6291464 | tf_op jit(solution)/shard_map/ppermute | solution.py:56
  147.1 61.8 %collective-permute-start.12 = (bf16[2,1024,512]{2,1,0:T(8,128)(2,1)}, bf16[2,1024,512]{2,1,0:T(8,128)(2,1)}, u32[]{:S(2)}, u32[]{:S(2)}) collective-permute-start(bf16[2,1024,512]{2,1,0:T(8,128)(2,1)} %get-tuple-element.59), channel_id=1, source_target_pairs={{0,1},{1,0},{2,3},{3,2},{4,5},{5,4},{6,7},{7,6},{8,9},{9,8},{10,11... | collective-permute-start | bytes 6291464 | tf_op jit(solution)/shard_map/ppermute | solution.py:56
  147.3 4.3 %copy-start.16 = (f32[512,1024]{1,0:T(8,128)S(1)}, f32[512,1024]{1,0:T(8,128)}, u32[]{:S(2)}) copy-start(f32[512,1024]{1,0:T(8,128)} %copy-done.15) | copy-start | bytes 6291460
  147.3 4.3 %copy-start.19 = (f32[512,1024]{1,0:T(8,128)S(1)}, f32[512,1024]{1,0:T(8,128)}, u32[]{:S(2)}) copy-start(f32[512,1024]{1,0:T(8,128)} %get-tuple-element.53) | copy-start | bytes 6291460
  147.3 4.3 %copy-start.21 = (bf16[256,1024]{1,0:T(8,128)(2,1)S(1)}, bf16[256,1024]{1,0:T(8,128)(2,1)}, u32[]{:S(2)}) copy-start(bf16[256,1024]{1,0:T(8,128)(2,1)} %copy-done.20) | copy-start | bytes 1572868
  147.3 4.3 %copy-start.42 = (f32[512]{0:T(512)S(1)}, f32[512]{0:T(512)}, u32[]{:S(2)}) copy-start(f32[512]{0:T(512)} %copy-done.41) | copy-start | bytes 6148
  151.5 3.9 %copy-start.59 = (bf16[1024,1024]{1,0:T(8,128)(2,1)S(1)}, bf16[1024,1024]{1,0:T(8,128)(2,1)}, u32[]{:S(2)}) copy-start(bf16[1024,1024]{1,0:T(8,128)(2,1)} %param.37) | copy-start | bytes 6291460
  157.1 12.4 %copy-start.18 = (f32[512,1024]{1,0:T(8,128)S(1)}, f32[512,1024]{1,0:T(8,128)}, u32[]{:S(2)}) copy-start(f32[512,1024]{1,0:T(8,128)} %copy-done.17) | copy-start | bytes 6291460
  157.1 12.5 %copy-start.44 = (f32[512]{0:T(512)S(1)}, f32[512]{0:T(512)}, u32[]{:S(2)}) copy-start(f32[512]{0:T(512)} %copy-done.43) | copy-start | bytes 6148
  157.1 12.5 %copy-start.46 = (f32[1024]{0:T(1024)S(1)}, f32[1024]{0:T(1024)}, u32[]{:S(2)}) copy-start(f32[1024]{0:T(1024)} %param.31) | copy-start | bytes 12292
  177.2 19.1 %copy-start.47 = (f32[1024]{0:T(1024)S(1)}, f32[1024]{0:T(1024)}, u32[]{:S(2)}) copy-start(f32[1024]{0:T(1024)} %get-tuple-element.136) | copy-start | bytes 12292
  177.2 19.0 %copy-start.48 = (f32[1024]{0:T(1024)S(1)}, f32[1024]{0:T(1024)}, u32[]{:S(2)}) copy-start(f32[1024]{0:T(1024)} %get-tuple-element.141) | copy-start | bytes 12292
  193.9 6.0 %copy-start.24 = (bf16[512,1024]{1,0:T(8,128)(2,1)S(1)}, bf16[512,1024]{1,0:T(8,128)(2,1)}, u32[]{:S(2)}) copy-start(bf16[512,1024]{1,0:T(8,128)(2,1)} %get-tuple-element.146.g_first_ref) | copy-start | bytes 3145732
  193.9 50.0 %collective-permute-start.14 = (bf16[2,4,64,1536]{3,2,1,0:T(8,128)(2,1)}, bf16[2,4,64,1536]{3,2,1,0:T(8,128)(2,1)}, u32[]{:S(2)}, u32[]{:S(2)}) collective-permute-start(bf16[2,4,64,1536]{3,2,1,0:T(8,128)(2,1)} %get-tuple-element.70), channel_id=1, source_target_pairs={{0,1},{1,0},{2,3},{3,2},{4,5},{5,4},{6,7},{7,6},{8,9},{9,8},{10,11... | collective-permute-start | bytes 4718600 | tf_op jit(solution)/shard_map/ppermute | solution.py:56
  195.8 48.0 %collective-permute-start.15 = (bf16[2,4,64,1536]{3,2,1,0:T(8,128)(2,1)}, bf16[2,4,64,1536]{3,2,1,0:T(8,128)(2,1)}, u32[]{:S(2)}, u32[]{:S(2)}) collective-permute-start(bf16[2,4,64,1536]{3,2,1,0:T(8,128)(2,1)} %get-tuple-element.72), channel_id=1, source_target_pairs={{0,2},{1,3},{2,0},{3,1},{4,6},{5,7},{6,4},{7,5},{8,10},{9,11},{10,... | collective-permute-start | bytes 4718600 | tf_op jit(solution)/shard_map/ppermute | solution.py:56
  199.8 4.3 %copy-start.23 = (bf16[2,1024,512]{2,1,0:T(8,128)(2,1)S(1)}, bf16[2,1024,512]{2,1,0:T(8,128)(2,1)}, u32[]{:S(2)}) copy-start(bf16[2,1024,512]{2,1,0:T(8,128)(2,1)} %get-tuple-element.60) | copy-start | bytes 6291460
  207.5 45.6 %collective-permute-start.17 = (bf16[1024,512]{1,0:T(8,128)(2,1)S(1)}, bf16[1024,512]{1,0:T(8,128)(2,1)S(1)}, u32[]{:S(2)}, u32[]{:S(2)}) collective-permute-start(bf16[1024,512]{1,0:T(8,128)(2,1)S(1)} %get-tuple-element.152.refs_13_), channel_id=1, source_target_pairs={{0,1},{1,0},{2,3},{3,2},{4,5},{5,4},{6,7},{7,6},{8,9},{9,8},{10,11... | collective-permute-start | bytes 3145736 | tf_op jit(solution)/shard_map/ppermute | solution.py:56
  212.3 42.3 %collective-permute-start.16 = (bf16[1024,512]{1,0:T(8,128)(2,1)S(1)}, bf16[1024,512]{1,0:T(8,128)(2,1)S(1)}, u32[]{:S(2)}, u32[]{:S(2)}) collective-permute-start(bf16[1024,512]{1,0:T(8,128)(2,1)S(1)} %get-tuple-element.154.refs_12_), channel_id=1, source_target_pairs={{0,2},{1,3},{2,0},{3,1},{4,6},{5,7},{6,4},{7,5},{8,10},{9,11},{10,... | collective-permute-start | bytes 3145736 | tf_op jit(solution)/shard_map/ppermute | solution.py:56
  362.1 5.2 %copy-start.25 = (bf16[2,256,1024]{2,1,0:T(8,128)(2,1)S(1)}, bf16[2,256,1024]{2,1,0:T(8,128)(2,1)}, u32[]{:S(2)}) copy-start(bf16[2,256,1024]{2,1,0:T(8,128)(2,1)} %get-tuple-element.76) | copy-start | bytes 3145732
  364.0 4.9 %copy-start.29 = (f32[2,128,1024]{2,1,0:T(8,128)S(1)}, f32[2,128,1024]{2,1,0:T(8,128)}, u32[]{:S(2)}) copy-start(f32[2,128,1024]{2,1,0:T(8,128)} %get-tuple-element.81) | copy-start | bytes 3145732
  368.9 4.2 %copy-start.28 = (bf16[2,256,1024]{2,1,0:T(8,128)(2,1)S(1)}, bf16[2,256,1024]{2,1,0:T(8,128)(2,1)}, u32[]{:S(2)}) copy-start(bf16[2,256,1024]{2,1,0:T(8,128)(2,1)} %get-tuple-element.212) | copy-start | bytes 3145732
  369.8 4.3 %copy-start.36 = (f32[128,768]{1,0:T(8,128)S(1)}, f32[128,768]{1,0:T(8,128)}, u32[]{:S(2)}) copy-start(f32[128,768]{1,0:T(8,128)} %get-tuple-element.217) | copy-start | bytes 1179652
  (35 other events, 64.7 us)

commit v2 on v1

--- a/solution.py
+++ b/solution.py
@@ -12,6 +12,7 @@
 PAIR = 2 * HD
 EPSILON = 1e-05
 MASKED = -1e30
+CLIPS = 4
 ROWS = "rows"
 SEQ = "seq"
 BF = jnp.bfloat16
@@ -170,6 +171,20 @@
 
 def turned(values):
     return jnp.swapaxes(values.astype(F32), 0, 1).astype(BF)
+
+
+def running(lengths_ref, first):
+    ends, total = [], 0
+    for c in range(CLIPS):
+        total = total + lengths_ref[first + c]
+        ends.append(total)
+    return ends
+
+
+def spans(start, length, axis, ends):
+    shape = (length, 1) if axis == 0 else (1, length)
+    positions = lax.broadcasted_iota(jnp.int32, shape, axis) + start
+    return sum((positions >= end).astype(jnp.int32) for end in ends)
 
 
 def segment_bias(key_segment, query_segment, causal):
@@ -234,33 +249,42 @@
     return [(0, 0, 0), (1, 0, 4)], [(0, 0, 1), (0, 1, 2), (1, 0, 3)]
 
 
-def self_biases(core, qseg_ref, kseg_refs, bias_ref):
+def self_biases(core, lengths_ref, bias_ref):
     length = bias_ref.shape[1]
-    low, high = slice(0, length), slice(length, 2 * length)
-    own, other = kseg_refs
-    bias_ref[0] = segment_bias(own[low], qseg_ref[:, low], True)
-    bias_ref[1] = segment_bias(own[low], qseg_ref[:, high], False)
-    bias_ref[2] = segment_bias(own[high], qseg_ref[:, high], True)
-    bias_ref[3] = segment_bias(other[low], qseg_ref[:, high], False)
-
-    @pl.when(core == 0)
-    def _():
-        bias_ref[4] = segment_bias(other[high], qseg_ref[:, high], False)
-
-    @pl.when(core != 0)
-    def _():
-        bias_ref[4] = segment_bias(other[low], qseg_ref[:, low], False)
+    ends = running(lengths_ref, 0)
+    quarters = (core, 3 - core)
+    keys = [spans(q * length, length, 0, ends) for q in quarters]
+    queries = [spans(q * length, length, 1, ends) for q in quarters]
+    others = [spans(q * length, length, 0, ends) for q in (1 - core, 2 + core)]
+    bias_ref[0] = segment_bias(keys[0], queries[0], True)
+    bias_ref[1] = segment_bias(keys[0], queries[1], False)
+    bias_ref[2] = segment_bias(keys[1], queries[1], True)
+    bias_ref[3] = segment_bias(others[0], queries[1], False)
+    last_key = jnp.where(core == 0, others[1], others[0])
+    last_query = jnp.where(core == 0, queries[1], queries[0])
+    bias_ref[4] = segment_bias(last_key, last_query, False)
+
+
+def cross_bias(lengths_ref, bias_ref):
+    core = lax.axis_index(ROWS) % 2
+    count, rows = bias_ref.shape
+    for n, token in enumerate((core, 3 - core, 1 - core, 2 + core)):
+        keys = spans(token * (count // 4), count // 4, 0, running(lengths_ref, CLIPS))
+        for m, frame in enumerate((core, 3 - core)):
+            queries = spans(frame * (rows // 2), rows // 2, 1, running(lengths_ref, 0))
+            at = slice(n * (count // 4), (n + 1) * (count // 4))
+            bias_ref[at, m * (rows // 2) : (m + 1) * (rows // 2)] = segment_bias(keys, queries, False)
 
 
 def self_forward_kernel(
-    core_ref, qseg_ref, own_ref, other_ref, q_ref, k_ref, v_ref, ko_ref, vo_ref, o_ref, lse_ref, bias_ref
+    lengths_ref, q_ref, k_ref, v_ref, ko_ref, vo_ref, o_ref, lse_ref, bias_ref
 ):
-    core = core_ref[0]
+    core = lax.axis_index(ROWS) % 2
     length = bias_ref.shape[1]
 
     @pl.when(pl.program_id(0) == 0)
     def _():
-        self_biases(core, qseg_ref, (own_ref, other_ref), bias_ref)
+        self_biases(core, lengths_ref, bias_ref)
 
     keys, values = (k_ref, ko_ref), (v_ref, vo_ref)
     for which in range(2):
@@ -283,10 +307,7 @@
 
 
 def self_backward_kernel(
-    core_ref,
-    qseg_ref,
-    own_ref,
-    other_ref,
+    lengths_ref,
     q_ref,
     k_ref,
     v_ref,
@@ -302,12 +323,12 @@
     dvo_ref,
     bias_ref,
 ):
-    core = core_ref[0]
+    core = lax.axis_index(ROWS) % 2
     length = bias_ref.shape[1]
 
     @pl.when(pl.program_id(0) == 0)
     def _():
-        self_biases(core, qseg_ref, (own_ref, other_ref), bias_ref)
+        self_biases(core, lengths_ref, bias_ref)
 
     keys, values = (k_ref, ko_ref), (v_ref, vo_ref)
     for which in range(2):
@@ -341,12 +362,12 @@
                         ref[where] = value.astype(BF)
 
 
-def cross_forward_kernel(qseg_ref, kseg_ref, q_ref, k_ref, v_ref, o_ref, lse_ref, bias_ref):
+def cross_forward_kernel(lengths_ref, q_ref, k_ref, v_ref, o_ref, lse_ref, bias_ref):
     length = q_ref.shape[0] // 2
 
     @pl.when(pl.program_id(0) == 0)
     def _():
-        bias_ref[...] = segment_bias(kseg_ref[...], qseg_ref[...], False)
+        cross_bias(lengths_ref, bias_ref)
 
     turned_values = turned(v_ref[...])
     for half in range(2):
@@ -356,8 +377,7 @@
 
 
 def cross_backward_kernel(
-    qseg_ref,
-    kseg_ref,
+    lengths_ref,
     q_ref,
     k_ref,
     v_ref,
@@ -373,7 +393,7 @@
 
     @pl.when(pl.program_id(0) == 0)
     def _():
-        bias_ref[...] = segment_bias(kseg_ref[...], qseg_ref[...], False)
+        cross_bias(lengths_ref, bias_ref)
 
     turned_keys = turned(k_ref[...])
     sums = [None, None]
@@ -389,10 +409,6 @@
     return pl.BlockSpec((rows, PAIR), lambda i: (0, first + i))
 
 
-def whole(array):
-    return pl.BlockSpec(array.shape, lambda i: (0,) * array.ndim)
-
-
 SMEM_SPEC = pl.BlockSpec(memory_space=pltpu.SMEM)
 
 
@@ -407,8 +423,20 @@
 WHOLE_SPEC = pl.BlockSpec(memory_space=pltpu.VMEM)
 
 
+MARK = jax.ShapeDtypeStruct((8, 128), F32)
+
+
+def marked(kernel, at):
+    def run(*refs):
+        refs[at][...] = jnp.zeros((8, 128), F32)
+        kernel(*refs[:at], *refs[at + 1 :])
+
+    return run
+
+
 def attention_call(kernel, heads, in_specs, outs, bias_shape, flops, arguments, before=()):
     pairs = heads // 2
+    kernel = marked(kernel, len(arguments) + len(outs))
     kernel = without(kernel, len(arguments), len(before))
     in_specs = list(in_specs) + [ANY_SPEC] * len(before)
     arguments = tuple(arguments) + tuple(before)
@@ -421,6 +449,8 @@
         else:
             out_shape.append(jax.ShapeDtypeStruct((rows, pairs * PAIR), BF))
             out_specs.append(column(rows))
+    out_shape.append(MARK)
+    out_specs.append(pl.BlockSpec((8, 128), lambda i: (0, 0)))
     return pl.pallas_call(
         kernel,
         grid=(pairs,),
@@ -437,7 +467,7 @@
     return pl.BlockSpec((1, 8, queries), lambda i: (i, 0, 0))
 
 
-def self_forward(core, qseg, own, other, queries, pair, pair_other):
+def self_forward(lengths, queries, pair, pair_other):
     rows, width = queries.shape
     heads = width // HD
     length = rows // 2
@@ -447,9 +477,6 @@
         heads,
         [
             SMEM_SPEC,
-            whole(qseg),
-            whole(own),
-            whole(other),
             column(rows),
             column(rows),
             column(rows, half),
@@ -459,11 +486,11 @@
         (rows, None),
         (5, length, length),
         heads * 5 * 4 * length * length * PAIR * 2,
-        (core, qseg, own, other, queries, pair, pair, pair_other, pair_other),
+        (lengths, queries, pair, pair, pair_other, pair_other),
     )
 
 
-def self_backward(core, qseg, own, other, queries, pair, pair_other, grads, mixed, lse, before=()):
+def self_backward(lengths, queries, pair, pair_other, grads, mixed, lse, before=()):
     rows, width = queries.shape
     heads = width // HD
     length = rows // 2
@@ -473,9 +500,6 @@
         heads,
         [
             SMEM_SPEC,
-            whole(qseg),
-            whole(own),
-            whole(other),
             column(rows),
             column(rows),
             column(rows, half),
@@ -488,27 +512,27 @@
         (rows,) * 5,
         (5, length, length),
         heads * 5 * 10 * length * length * PAIR * 2,
-        (core, qseg, own, other, queries, pair, pair, pair_other, pair_other, grads, mixed, lse),
+        (lengths, queries, pair, pair, pair_other, pair_other, grads, mixed, lse),
         before,
     )
 
 
-def cross_forward(qseg, kseg, queries, pair):
+def cross_forward(lengths, queries, pair):
     rows, width = queries.shape
     heads = width // HD
     count = pair.shape[0]
     return attention_call(
         cross_forward_kernel,
         heads,
-        [whole(qseg), whole(kseg), column(rows), column(count), column(count, heads // 2)],
+        [SMEM_SPEC, column(rows), column(count), column(count, heads // 2)],
         (rows, None),
         (count, rows),
         heads * 4 * rows * count * PAIR * 2,
-        (qseg, kseg, queries, pair, pair),
+        (lengths, queries, pair, pair),
     )
 
 
-def cross_backward(qseg, kseg, queries, pair, grads, mixed, lse, before=()):
+def cross_backward(lengths, queries, pair, grads, mixed, lse, before=()):
     rows, width = queries.shape
     heads = width // HD
     count = pair.shape[0]
@@ -516,8 +540,7 @@
         cross_backward_kernel,
         heads,
         [
-            whole(qseg),
-            whole(kseg),
+            SMEM_SPEC,
             column(rows),
             column(count),
             column(count, heads // 2),
@@ -528,7 +551,7 @@
         (rows, count, count),
         (count, rows),
         heads * 10 * rows * count * PAIR * 2,
-        (qseg, kseg, queries, pair, pair, grads, mixed, lse),
+        (lengths, queries, pair, pair, grads, mixed, lse),
         before,
     )
 
@@ -538,11 +561,12 @@
     bell = jnp.exp(-0.5 * values * values) * ((2.0 * math.pi) ** -0.5)
     return values * inside, inside + values * bell
 
+
 def feed_kernel(shape, meta_ref, own_ref, other_ref, gown_ref, gother_ref, win_ref, wout_ref, *refs):
     nx, ny, nz, chunk = shape
     res_ref, res_other_ref, grad_ref, grad_other_ref = refs[:4]
-    gin_refs, gout_refs = refs[4 : 4 + nx], refs[4 + nx : 4 + nx + ny]
-    act_ref, pre_ref, turned_ref, gturned_ref, res_acc, grad_acc = refs[4 + nx + ny :]
+    up_refs, low_refs, gout_refs = refs[4 : 4 + nx], refs[4 + nx : 4 + nx + ny], refs[4 + nx + ny : 4 + nx + ny + nz]
+    act_ref, pre_ref, turned_ref, gturned_ref, res_acc, grad_acc = refs[4 + nx + ny + nz :]
     j, i = pl.program_id(0), pl.program_id(1)
     z = meta_ref[3]
     tokens = own_ref.shape[0]
@@ -570,22 +594,23 @@
             grad[at] += nt(before, win_ref[...])
 
     rows = turned_ref.shape[0] // nz
+    half = rows // 2
     for k in range(nz):
         source = pl.ds(pl.multiple_of((z + 1 + k) % nz * rows, rows), rows)
-        to = slice(k * rows, (k + 1) * rows)
         gin = dot(turned_ref[source], pre_ref[...]).astype(BF)
-        gout = dot(gturned_ref[source], act_ref[...]).astype(BF)
-        for number, ref in enumerate(gin_refs):
+        gout_refs[k][0] = dot(gturned_ref[source], act_ref[...]).astype(BF)
+        to = slice(k * half, (k + 1) * half)
+        for number, ref in enumerate(up_refs):
 
             @pl.when(j == number)
             def _(ref=ref):
-                ref[0, to] = gin
-
-        for number, ref in enumerate(gout_refs):
+                ref[0, to] = gin[:half]
+
+        for number, ref in enumerate(low_refs):
 
             @pl.when(i == number)
             def _(ref=ref):
-                ref[0, to] = gout
+                ref[0, to] = gin[half:]
 
     @pl.when((i == ny - 1) & (j == nx - 1))
     def _():
@@ -602,14 +627,16 @@
     def unit(j, i, meta):
         return 2 * ((meta[2] + 1 + i) % ny * nx + (meta[1] + 1 + j) % nx) + meta[0]
 
-    def gin_spec(number):
+    def up_spec(number):
         def index(j, i, meta):
             return jnp.where(j == number, i, jnp.where(j < number, 0, ny - 1)), 0, 0
 
-        return pl.BlockSpec((1, width, part), index)
-
-    gout_spec = pl.BlockSpec((1, width, part), lambda j, i, meta: (j, 0, 0))
+        return pl.BlockSpec((1, width // 2, part), index)
+
+    low_spec = pl.BlockSpec((1, width // 2, part), lambda j, i, meta: (j, 0, 0))
+    gout_spec = pl.BlockSpec((1, width // nz, part), lambda j, i, meta: (j * ny + i, 0, 0))
     total = 2 * tokens
+    shape = jax.ShapeDtypeStruct
     return pl.pallas_call(
         functools.partial(feed_kernel, (nx, ny, nz, chunk)),
         grid_spec=pltpu.PrefetchScalarGridSpec(
@@ -620,7 +647,10 @@
                 pl.BlockSpec((width, part), lambda j, i, meta: (0, unit(j, i, meta))),
                 pl.BlockSpec((part, width), lambda j, i, meta: (unit(j, i, meta), 0)),
             ],
-            out_specs=[WHOLE_SPEC] * 4 + [gin_spec(n) for n in range(nx)] + [gout_spec] * ny,
+            out_specs=[WHOLE_SPEC] * 4
+            + [up_spec(n) for n in range(nx)]
+            + [low_spec] * ny
+            + [gout_spec] * nz,
             scratch_shapes=[
                 pltpu.VMEM((total, part), BF),
                 pltpu.VMEM((total, part), BF),
@@ -631,13 +661,14 @@
             ],
         ),
         out_shape=[
-            jax.ShapeDtypeStruct((tokens, width), F32),
-            jax.ShapeDtypeStruct((tokens, width), BF),
-            jax.ShapeDtypeStruct((tokens, width), F32),
-            jax.ShapeDtypeStruct((tokens, width), BF),
+            shape((tokens, width), F32),
+            shape((tokens, width), BF),
+            shape((tokens, width), F32),
+            shape((tokens, width), BF),
         ]
-        + [jax.ShapeDtypeStruct((ny, width, part), BF)] * nx
-        + [jax.ShapeDtypeStruct((nx, width, part), BF)] * ny,
+        + [shape((ny, width // 2, part), BF)] * nx
+        + [shape((nx, width // 2, part), BF)] * ny
+        + [shape((place.seq, width // nz, part), BF)] * nz,
         compiler_params=pltpu.CompilerParams(vmem_limit_bytes=60 * 1024 * 1024),
         cost_estimate=pl.CostEstimate(
             flops=12 * total * width * part * place.seq,
@@ -791,6 +822,172 @@
                 copy.wait_send()
 
 
+class Gathering:
+    def __init__(self, ways, source_ref, target_ref, send_sems, recv_sems):
+        self.ways, self.source_ref, self.target_ref = ways, source_ref, target_ref
+        self.send_sems, self.recv_sems = send_sems, recv_sems
+        self.block = source_ref.shape[1]
+        self.started = []
+
+    def start(self):
+        ways = self.ways
+        owner = jnp.where((ways.spot == 0) | (ways.spot == 3), 0, 1)
+        slot = ways.spot // 2
+        to = self.target_ref.at[pl.ds(pl.multiple_of(slot * self.block, self.block), self.block)]
+        for r in range(2):
+            row, spot = 2 * ways.z + owner, 2 * ways.core + r
+            stays = (spot == ways.spot) & (row == ways.row)
+            copy = pltpu.make_async_remote_copy(
+                src_ref=self.source_ref.at[r],
+                dst_ref=to,
+                send_sem=self.send_sems.at[r],
+                recv_sem=self.recv_sems.at[slot],
+                device_id=(row, spot),
+                device_id_type=MESH,
+            )
+            local = pltpu.make_async_copy(self.source_ref.at[r], to, self.recv_sems.at[slot])
+
+            @pl.when(stays)
+            def _(local=local):
+                local.start()
+
+            @pl.when(jnp.logical_not(stays))
+            def _(copy=copy):
+                copy.start()
+
+            self.started.append((stays, copy))
+
+    def arrived(self, slot):
+        to = self.target_ref.at[slot * self.block : (slot + 1) * self.block]
+        pltpu.make_async_copy(to, to, self.recv_sems.at[slot]).wait()
+
+    def finish(self):
+        for stays, copy in self.started:
+
+            @pl.when(jnp.logical_not(stays))
+            def _(copy=copy):
+                copy.wait_send()
+
+
+def entry_kernel(
+    nz,
+    frames_ref,
+    text_ref,
+    grad_ref,
+    lengths_ref,
+    gain_ref,
+    shift_ref,
+    qkv_ref,
+    proj_ref,
+    bias_ref,
+    kv_ref,
+    input_ref,
+    normed_ref,
+    queries_ref,
+    pair_ref,
+    pair_other_ref,
+    cotangent_ref,
+    words_ref,
+    projected_ref,
+    text_pair_ref,
+    lengths_other_ref,
+    qkv_here,
+    proj_here,
+    kv_here,
+    load_sems,
+    send_sems,
+    recv_sems,
+    gather_sends,
+    gather_recvs,
+):
+    loads = [
+        pltpu.make_async_copy(source, target, load_sems.at[number])
+        for number, (source, target) in enumerate(
+            ((proj_ref, proj_here), (kv_ref, kv_here), (qkv_ref, qkv_here))
+        )
+    ]
+    for load in loads:
+        load.start()
+    ways = Ways(nz)
+    ways.meet(ways.plane())
+    mail = Mail(send_sems, recv_sems)
+    words = Gathering(ways, text_ref, words_ref, gather_sends.at[0], gather_recvs.at[0])
+    frames = Gathering(ways, frames_ref, input_ref, gather_sends.at[1], gather_recvs.at[1])
+    grads = Gathering(ways, grad_ref, cotangent_ref, gather_sends.at[2], gather_recvs.at[2])
+    words.start()
+    frames.start()
+    lengths_copy = mail.send(lengths_ref, lengths_other_ref, ways.sibling)
+    half = words_ref.shape[0] // 2
+    for slot in range(2):
+        words.arrived(slot)
+    words_copy = mail.send(words_ref.at[:half], words_ref.at[half:], ways.sibling)
+    for load in loads:
+        load.wait()
+    words_copy.wait_recv()
+    projected = (dot(words_ref[...], proj_here[...]) + bias_ref[...]).astype(BF)
+    projected_ref[...] = projected
+    text_pair_ref[...] = dot(projected, kv_here[...]).astype(BF)
+    width = input_ref.shape[1]
+    block = input_ref.shape[0] // 2
+    copies = []
+    for slot in range(2):
+        frames.arrived(slot)
+        if slot == 1:
+            grads.start()
+        at = slice(slot * block, (slot + 1) * block)
+        normed_ref[at] = layer_norm(input_ref[at].astype(F32), gain_ref[...], shift_ref[...])
+        pair_ref[at] = dot(normed_ref[at], qkv_here[:, width:]).astype(BF)
+        copies.append(mail.send(pair_ref.at[at], pair_other_ref.at[at], ways.sibling))
+    queries_ref[...] = dot(normed_ref[...], qkv_here[:, :width]).astype(BF)
+    lengths_copy.wait_recv()
+    for copy in copies:
+        copy.wait_recv()
+    for slot in range(2):
+        grads.arrived(slot)
+    mail.finish()
+    for gathering in (words, frames, grads):
+        gathering.finish()
+
+
+def entry(place, frames, text, grads, lengths, gain, shift, qkv, proj, bias, kv):
+    count, block, width = frames.shape
+    tokens, words = count * block, 2 * count * text.shape[1]
+    shape, vmem = jax.ShapeDtypeStruct, pltpu.VMEM
+    return pl.pallas_call(
+        functools.partial(entry_kernel, place.nz),
+        in_specs=[ANY_SPEC] * 3 + [WHOLE_SPEC] * 3 + [ANY_SPEC] * 2 + [WHOLE_SPEC, ANY_SPEC],
+        out_specs=[WHOLE_SPEC] * 10,
+        out_shape=[
+            shape((tokens, width), BF),
+            shape((tokens, width), BF),
+            shape((tokens, width), BF),
+            shape((tokens, 2 * width), BF),
+            shape((tokens, 2 * width), BF),
+            shape((tokens, width), BF),
+            shape((words, text.shape[2]), BF),
+            shape((words, width), BF),
+            shape((words, 2 * width), BF),
+            shape(lengths.shape, jnp.int32),
+        ],
+        scratch_shapes=[
+            vmem(qkv.shape, BF),
+            vmem(proj.shape, BF),
+            vmem(kv.shape, BF),
+            pltpu.SemaphoreType.DMA((3,)),
+            pltpu.SemaphoreType.DMA((4,)),
+            pltpu.SemaphoreType.DMA((4,)),
+            pltpu.SemaphoreType.DMA((3, 2)),
+            pltpu.SemaphoreType.DMA((3, 2)),
+        ],
+        compiler_params=pltpu.CompilerParams(
+            collective_id=3, has_side_effects=True, vmem_limit_bytes=VMEM_LIMIT
+        ),
+        cost_estimate=pl.CostEstimate(
+            flops=20 * tokens * width * width, bytes_accessed=20 << 20, transcendentals=0
+        ),
+    )(frames, text, grads, lengths, gain[None], shift[None], qkv, proj, bias[None], kv)
+
+
 def middle_kernel(
     shape,
     mixed_ref,
@@ -804,10 +1001,13 @@
     g_values_ref,
     g_projected_ref,
     g_first_ref,
+    result_ref,
+    result_away_ref,
     send_up_ref,
     send_low_ref,
     keep_up_ref,
     keep_low_ref,
+    result_out,
     mixed_t,
     normed_t,
     projected_t,
@@ -816,13 +1016,18 @@
     own_ref,
     away_ref,
     got_ref,
+    result_got_ref,
     send_sems,
     recv_sems,
+    home_sends,
+    home_recvs,
 ):
     nz, piece = shape
     ways = Ways(nz)
-    ways.meet([ways.sibling])
+    ways.meet(ways.plane())
     mail = Mail(send_sems, recv_sems)
+    result_copy = mail.send(result_away_ref, result_got_ref, ways.sibling)
+    home = Home(ways, result_out, home_sends, home_recvs)
     for left, to in ((mixed_ref, mixed_t), (normed_ref, normed_t), (projected_ref, projected_t), (self_ref, self_t)):
         to[...] = turned(left[...])
     turned_text = turned(text_ref[...])
@@ -869,13 +1074,20 @@
                     ref[q, k, :, to] = dot(left[ways.rows(k, which, block)], right).astype(BF)
             if ref is away_ref:
                 copies.append(mail.send(away_ref.at[q], got_ref.at[q], ways.sibling))
-        if q > 0:
+        if q == 0:
+            result_copy.wait_recv()
+            result_got_ref[...] = (result_ref[...] + result_got_ref[...].astype(F32)).astype(BF)
+            slots = result_ref.shape[0] // 2
+            for slot in range(2):
+                home.send(result_got_ref.at[slot * slots : (slot + 1) * slots], slot)
+        else:
             settle(q - 1)
     settle(3)
     mail.finish()
-
-
-def middle_parts(place, lefts, rights):
+    home.finish()
+
+
+def middle_parts(place, count, lefts, rights, result, result_away, before):
     nz = place.nz
     depth, width = lefts[0].shape[1], rights[0].shape[1]
     piece, block = width // place.seq, depth // place.rows
@@ -883,20 +1095,23 @@
     out = jax.ShapeDtypeStruct((2, nz, block // 2, columns), BF)
     big = pltpu.VMEM((4, nz, block, columns), BF)
     return pl.pallas_call(
-        functools.partial(middle_kernel, (nz, piece)),
-        in_specs=[WHOLE_SPEC] * 11,
-        out_specs=[WHOLE_SPEC] * 4,
-        out_shape=[out] * 4,
+        without(marked(functools.partial(middle_kernel, (nz, piece)), 18), 13, len(before)),
+        in_specs=[WHOLE_SPEC] * 12 + [ANY_SPEC] * (1 + len(before)),
+        out_specs=[WHOLE_SPEC] * 4 + [ANY_SPEC, WHOLE_SPEC],
+        out_shape=[out] * 4
+        + [jax.ShapeDtypeStruct((count, result.shape[0] // count, width), BF), MARK],
         scratch_shapes=[pltpu.VMEM((depth, left.shape[0]), BF) for left in lefts]
         + [big] * 3
-        + [pltpu.SemaphoreType.DMA((4,))] * 2,
+        + [pltpu.VMEM(result.shape, BF)]
+        + [pltpu.SemaphoreType.DMA((5,))] * 2
+        + [pltpu.SemaphoreType.DMA((2,))] * 2,
         compiler_params=pltpu.CompilerParams(
-            collective_id=2, has_side_effects=True, vmem_limit_bytes=VMEM_LIMIT
+            collective_id=2, has_side_effects=True, vmem_limit_bytes=60 * 1024 * 1024
         ),
         cost_estimate=pl.CostEstimate(
             flops=2 * 8 * 512 * depth * width, bytes_accessed=24 << 20, transcendentals=0
         ),
-    )(*lefts, *rights)
+    )(*lefts, *rights, result, result_away, *before)
 
 
 def final_kernel(nz, *refs):
@@ -915,17 +1130,19 @@
         upper_got_ref,
         lower_ref,
         lower_got_ref,
-        in_keep_ref,
-        in_got_ref,
-        out_keep_ref,
-        out_got_ref,
+        in_up_ref,
+        in_up_got_ref,
+        in_low_ref,
+        in_low_got_ref,
+        out_ref,
         vector_ref,
-        result_ref,
-        result_away_ref,
         text_ref,
-    ) = refs[:22]
-    (qkv_ref, middle_ref, feed_ref, sum_ref, result_out, frames_out, text_out) = refs[22:29]
+    ) = refs[:21]
+    (qkv_ref, middle_ref, feed_ref, sum_ref, frames_out, text_out) = refs[21:27]
     (
+        weight_here,
+        first_here,
+        load_sems,
         packed_ref,
         k_got_ref,
         v_got_ref,
@@ -945,18 +1162,29 @@
         qkv_ring_ref,
         feed_send_ref,
         feed_ring_ref,
+        out_x_ref,
+        out_own_ref,
+        out_y_ref,
         feed_away_ref,
         feed_other_ref,
         vector_out_ref,
         vector_in_ref,
-        result_got_ref,
         text_away_ref,
         text_got_ref,
         send_sems,
         recv_sems,
         home_sends,
         home_recvs,
-    ) = refs[29:]
+    ) = refs[27:]
+    loads = [
+        pltpu.make_async_copy(source, target, load_sems.at[number])
+        for number, (source, target) in enumerate(
+            ((weight_ref, weight_here), (first_ref, first_here))
+        )
+    ]
+    for load in loads:
+        load.start()
+    weight_ref, first_ref = weight_here, first_here
     ways = Ways(nz)
     core, z = ways.core, ways.z
     sibling, across_x, across_y, above = ways.sibling, ways.across_x, ways.across_y, ways.above
@@ -964,24 +1192,36 @@
     mail = Mail(send_sems, recv_sems)
     ring = ring_order(nz)
     half = upper_ref.shape[2]
-    feed_rows = feed_ring_ref.shape[2]
+    feed_half = feed_ring_ref.shape[1] // 2
     tokens, width = normed_ref.shape
 
     k_copy = mail.send(k_away_ref, k_got_ref, sibling)
     v_copy = mail.send(v_away_ref, v_got_ref, sibling)
 
-    def feed_piece(kind, k):
-        keep, got = ((in_keep_ref, in_got_ref), (out_keep_ref, out_got_ref))[kind]
-        at = slice(k * feed_rows, (k + 1) * feed_rows)
-        return keep[at].astype(F32) + got[at].astype(F32)
-
-    def feed_send(t, kind):
-        return mail.send(feed_send_ref.at[kind, t], feed_ring_ref.at[kind, t], above)
-
-    feed_copies = {}
-    for kind in range(2):
-        feed_send_ref[kind, 0] = feed_piece(kind, ring[0]).astype(BF)
-        feed_copies[kind, 0] = feed_send(0, kind)
+    out_copies = [mail.send(out_ref.at[q], out_x_ref.at[q], across_x) for q in range(2)]
+    feed_copies, feed_last_copies = [], {}
+
+    def feed_piece(t):
+        at = slice(ring[t] * feed_half, (ring[t] + 1) * feed_half)
+        return (
+            in_up_ref[at].astype(F32) + in_up_got_ref[at].astype(F32),
+            in_low_ref[at].astype(F32) + in_low_got_ref[at].astype(F32),
+        )
+
+    def feed_step(t):
+        upper_part, lower_part = feed_piece(t)
+        if t > 0:
+            feed_copies[t - 1].wait_recv()
+            upper_part += feed_ring_ref[t - 1, :feed_half].astype(F32)
+            lower_part += feed_ring_ref[t - 1, feed_half:].astype(F32)
+        if t == nz - 1:
+            feed_finish(0, upper_part, lower_part)
+            return
+        feed_send_ref[t, :feed_half] = upper_part.astype(BF)
+        feed_send_ref[t, feed_half:] = lower_part.astype(BF)
+        feed_copies.append(mail.send(feed_send_ref.at[t], feed_ring_ref.at[t], above))
+
+    feed_step(0)
 
     mid_copies = {}
     for k in ring:
@@ -991,7 +1231,6 @@
             mail.send(mid_ref.at[k, :half], mid_up_ref.at[k], across_y),
             mail.send(mid_ref.at[k, half:], mid_low_ref.at[k], across_x),
         )
-    result_copy = mail.send(result_away_ref, result_got_ref, sibling)
     text_rows = text_ref.shape[0] // 2
     text_away_ref[...] = text_ref[text_rows:].astype(BF)
     text_copy = mail.send(text_away_ref, text_got_ref, sibling)
@@ -1014,28 +1253,29 @@
             if ref is away_ref:
                 core_copies.append(mail.send(away_ref.at[q], got_ref.at[q], sibling))
 
-    def feed_step(t):
-        for kind in range(2):
-            feed_copies[kind, t - 1].wait_recv()
-            total = feed_piece(kind, ring[t]) + feed_ring_ref[kind, t - 1].astype(F32)
-            if t < nz - 1:
-                feed_send_ref[kind, t] = total.astype(BF)
-                feed_copies[kind, t] = feed_send(t, kind)
-            else:
-                feed_finish(kind, total)
-
-    def feed_finish(kind, total):
-        rows = total.shape[0] // 2
-        away = jnp.where(core == 0, total[rows:], total[:rows])
-        own = jnp.where(core == 0, total[:rows], total[rows:])
-        across = total.shape[1]
+    def out_step():
+        for q in range(2):
+            out_copies[q].wait_recv()
+            out_own_ref[q] = out_ref[2 + q] + out_x_ref[q]
+            if q == 0:
+                out_copies.append(mail.send(out_own_ref.at[0], out_y_ref, across_y))
+
+    def out_last():
+        out_copies[2].wait_recv()
+        total = out_own_ref[1].astype(F32) + out_y_ref[...].astype(F32)
+        feed_finish(1, total[:feed_half], total[feed_half:])
+
+    def feed_finish(kind, even, odd):
+        away = jnp.where(core == 0, odd, even)
+        own = jnp.where(core == 0, even, odd)
+        across = own.shape[1]
         feed_away_ref[kind] = away
-        feed_copies[kind, nz] = mail.send(feed_away_ref.at[kind], feed_other_ref.at[kind], sibling)
+        feed_last_copies[kind] = mail.send(feed_away_ref.at[kind], feed_other_ref.at[kind], sibling)
         at = pl.ds(pl.multiple_of(core * across, across), across)
         feed_ref[kind, :, at] = own
 
     def feed_last(kind):
-        feed_copies[kind, nz].wait_recv()
+        feed_last_copies[kind].wait_recv()
         across = feed_other_ref.shape[2]
         at = pl.ds(pl.multiple_of((1 - core) * across, across), across)
         feed_ref[kind, :, at] = feed_other_ref[kind]
@@ -1066,6 +1306,10 @@
 
     def qkv_send(t):
         k = ring[t]
+        second[k][0].wait_recv()
+        own_ref[3, k, up] = own_ref[3, k, up] + second_y_ref[k]
+        second[k][1].wait_recv()
+        own_ref[3, k, low] = own_ref[3, k, low] + second_x_ref[k]
         if t > 0:
             qkv_ring[t - 1].wait_recv()
         if t == nz - 1:
@@ -1084,16 +1328,14 @@
     core_step(2)
     lower_first.append(mail.send(own_ref.at[2, :, low], first_y_ref.at[1], across_y))
     core_step(3)
-
-    result_copy.wait_recv()
+    out_step()
+
+    for load in loads:
+        load.wait()
     slots = tokens // 2
-    result_got_ref[...] = (result_ref[...] + result_got_ref[...].astype(F32)).astype(BF)
-    result_home = Home(ways, result_out, home_sends.at[0], home_recvs.at[0])
-    for slot in range(2):
-        result_home.send(result_got_ref.at[slot * slots : (slot + 1) * slots], slot)
     text_copy.wait_recv()
     text_got_ref[...] = (text_ref[:text_rows] + text_got_ref[...].astype(F32)).astype(BF)
-    text_home = Home(ways, text_out, home_sends.at[1], home_recvs.at[1])
+    text_home = Home(ways, text_out, home_sends.at[0], home_recvs.at[0])
     for slot in range(2):
         at = slice(slot * text_rows // 2, (slot + 1) * text_rows // 2)
         text_home.send(text_got_ref.at[at], slot)
@@ -1114,9 +1356,6 @@
         k_got_ref[at] = (first_ref[at] + grad).astype(BF)
         gain_sum += gain_part[None]
         shift_sum += shift_part[None]
-    frames_home = Home(ways, frames_out, home_sends.at[2], home_recvs.at[2])
-    for slot in range(2):
-        frames_home.send(k_got_ref.at[slot * slots : (slot + 1) * slots], slot)
     vector_out_ref[0] = vector_ref[...]
     vector_out_ref[0, 0:1] = gain_sum
     vector_out_ref[0, 1:2] = shift_sum
@@ -1133,13 +1372,21 @@
     vector_copy.wait_recv()
     vector_out_ref[2] = vector_out_ref[1] + vector_in_ref[1]
     vector_copy = mail.send(vector_out_ref.at[2], vector_in_ref.at[2], across_y)
+    out_last()
 
     upper_first[0].wait_recv()
     own_ref[2, :, up] = own_ref[2, :, up] + first_x_ref[0]
-    upper_second = mail.send(own_ref.at[2, :, up], second_y_ref, across_y)
     lower_first[0].wait_recv()
     own_ref[1, :, low] = own_ref[1, :, low] + first_y_ref[0]
-    lower_second = mail.send(own_ref.at[1, :, low], second_x_ref, across_x)
+    second = {}
+    for k in ring:
+        second[k] = (
+            mail.send(own_ref.at[2, k, up], second_y_ref.at[k], across_y),
+            mail.send(own_ref.at[1, k, low], second_x_ref.at[k], across_x),
+        )
+    frames_home = Home(ways, frames_out, home_sends.at[1], home_recvs.at[1])
+    for slot in range(2):
+        frames_home.send(k_got_ref.at[slot * slots : (slot + 1) * slots], slot)
     vector_copy.wait_recv()
     vector_out_ref[3] = vector_out_ref[2] + vector_in_ref[2]
     vector_copy = mail.send(vector_out_ref.at[3], vector_in_ref.at[3], above)
@@ -1157,13 +1404,8 @@
         if t < nz - 2:
             vector_copy = mail.send(vector_in_ref.at[3 + t], vector_in_ref.at[4 + t], above)
     sum_ref[...] = total
-    upper_second.wait_recv()
-    own_ref[3, :, up] = own_ref[3, :, up] + second_y_ref[...]
-    lower_second.wait_recv()
-    own_ref[3, :, low] = own_ref[3, :, low] + second_x_ref[...]
     for t in range(nz):
         qkv_send(t)
-    result_home.finish()
     text_home.finish()
     frames_home.finish()
     for number, copy in enumerate(mail.sent):
@@ -1171,31 +1413,38 @@
             copy.wait_send()
 
 
+FINAL_IN_PLACE = (2, 4, 8, 9)
+
+
 def final_sums(place, count, *operands):
     nz = place.nz
-    normed, weight, upper, in_keep = operands[0], operands[4], operands[10], operands[14]
-    vectors, text = operands[18], operands[21]
+    normed, weight, upper, in_up = operands[0], operands[4], operands[10], operands[14]
+    vectors, text = operands[19], operands[20]
     tokens, width = normed.shape
     block, piece = width // place.rows, weight.shape[1] // place.seq
     half, middle = block // 2, upper.shape[3]
-    feed_width = in_keep.shape[1]
+    feed_width = in_up.shape[1]
     feed_rows = width // nz
-    copies = 2 + 2 * nz + 2 * nz + 2 + 4 + 3 + nz - 1 + 4 + 2 + 2 * (nz - 1)
+    copies = 2 + 3 + nz - 1 + 2 + 2 * nz + 1 + 4 + 3 + nz - 1 + 4 + 2 * nz + 2 * (nz - 1)
     vmem = pltpu.VMEM
     return pl.pallas_call(
         functools.partial(final_kernel, nz),
-        in_specs=[WHOLE_SPEC] * 22,
-        out_specs=[WHOLE_SPEC] * 4 + [ANY_SPEC] * 3,
+        in_specs=[
+            ANY_SPEC if n in FINAL_IN_PLACE else WHOLE_SPEC for n in range(len(operands))
+        ],
+        out_specs=[WHOLE_SPEC] * 4 + [ANY_SPEC] * 2,
         out_shape=[
             jax.ShapeDtypeStruct((block, piece), F32),
             jax.ShapeDtypeStruct((block, middle), F32),
             jax.ShapeDtypeStruct((2, block, 2 * feed_width), F32),
             jax.ShapeDtypeStruct(vectors.shape, F32),
             jax.ShapeDtypeStruct((count, tokens // count, width), BF),
-            jax.ShapeDtypeStruct((count, tokens // count, width), BF),
             jax.ShapeDtypeStruct((count, text.shape[0] // 2 // count, text.shape[1]), BF),
         ],
         scratch_shapes=[
+            vmem(weight.shape, BF),
+            vmem((tokens, width), F32),
+            pltpu.SemaphoreType.DMA((2,)),
             vmem((tokens, 3 * width), BF),
             vmem((tokens, width), BF),
             vmem((tokens, width), BF),
@@ -1213,19 +1462,21 @@
             vmem((nz, block, middle), BF),
             vmem((nz - 1, block, middle), BF),
             vmem((nz - 1, block, piece), BF),
-            vmem((2, nz - 1, feed_rows, feed_width), BF),
-            vmem((2, nz - 1, feed_rows, feed_width), BF),
+            vmem((nz - 1, feed_rows, feed_width), BF),
+            vmem((nz - 1, feed_rows, feed_width), BF),
+            vmem((2, feed_rows, feed_width), BF),
+            vmem((2, feed_rows, feed_width), BF),
+            vmem((feed_rows, feed_width), BF),
             vmem((2, feed_rows // 2, feed_width), F32),
             vmem((2, feed_rows // 2, feed_width), F32),
             vmem((4,) + vectors.shape, F32),
             vmem((2 + nz,) + vectors.shape, F32),
-            vmem((tokens, width), BF),
             vmem((text.shape[0] // 2, text.shape[1]), BF),
             vmem((text.shape[0] // 2, text.shape[1]), BF),
             pltpu.SemaphoreType.DMA((copies,)),
             pltpu.SemaphoreType.DMA((copies,)),
-            pltpu.SemaphoreType.DMA((3, 2)),
-            pltpu.SemaphoreType.DMA((3, 2)),
+            pltpu.SemaphoreType.DMA((2, 2)),
+            pltpu.SemaphoreType.DMA((2, 2)),
         ],
         compiler_params=pltpu.CompilerParams(
             collective_id=1, has_side_effects=True, vmem_limit_bytes=63 * 1024 * 1024
@@ -1236,7 +1487,7 @@
     )(*operands)
 
 
-def permuted_sums(place, meta, in_half, out_half, lefts, rights, normed_self, backward_self):
+def permuted_sums(place, meta, in_up, in_low, out_sum, lefts, rights, normed_self, backward_self):
     nx, ny, nz, seq = place.nx, place.ny, place.nz, place.seq
     width = normed_self.shape[1]
     block, piece = width // place.rows, width // seq
@@ -1246,13 +1497,16 @@
     out_own, out_away = weight_parts(place, meta, lefts[4:], rights[5:])
     middle_got = place.swap_core(middle_away)
     out_got = place.swap_core(out_away)
-    grad_packed = backward_self(in_half, out_half, middle_got, out_got)
-    in_quarter = ring_sum([lambda k=k: in_half[k].astype(F32) for k in range(ny)], place.next_y)
-    out_quarter = ring_sum([lambda k=k: out_half[k].astype(F32) for k in range(nx)], place.next_x)
-    feed_quarter = jnp.stack([in_quarter, out_quarter]).astype(BF)
-    feed_quarter = feed_quarter.reshape(2, nz, -1, feed_quarter.shape[2])
-    feed_own = ring_sum([lambda k=k: feed_quarter[:, k].astype(F32) for k in range(nz)], place.next_z)
-    feed_own = feed_own.reshape(2, 2, block, -1)
+    grad_packed = backward_self(middle_got, out_got)
+    in_up = ring_sum([lambda a=in_up[k]: a.astype(F32) for k in range(ny)], place.next_y)
+    in_low = ring_sum([lambda a=in_low[k]: a.astype(F32) for k in range(nx)], place.next_x)
+    in_both = jnp.stack([in_up, in_low]).astype(BF).reshape(2, nz, block, -1)
+    in_both = ring_sum([lambda a=in_both[:, k]: a.astype(F32) for k in range(nz)], place.next_z)
+    out_sum = out_sum.reshape((nx, ny) + out_sum.shape[1:])
+    out_sum = ring_sum([lambda a=out_sum[k]: a.astype(F32) for k in range(nx)], place.next_x)
+    out_sum = out_sum.astype(BF)
+    out_sum = ring_sum([lambda a=out_sum[k]: a.astype(F32) for k in range(ny)], place.next_y)
+    feed_own = jnp.stack([in_both, out_sum.reshape(2, block, -1)])
     feed_got = place.swap_core(pick(feed_own, 1 - place.core, 1))
     feed_own = pick(feed_own, place.core, 1)
     low = jnp.where(place.core == 0, feed_own, feed_got)
@@ -1342,86 +1596,97 @@
     place = Place()
     count = frames.shape[0]
     width = frames.shape[2]
-    frame_total = frames.shape[1] * place.seq
     text_total = text_states.shape[1] * place.seq
 
+    nx, ny, nz, seq = place.nx, place.ny, place.nz, place.seq
+    block, piece = width // place.rows, width // seq
+    kernels = nx == 2 and ny == 2 and piece % 128 == 0
     lengths = jnp.concatenate([clip_lengths, text_lengths], axis=1)
-    lengths_other = place.swap_core(lengths)
+    if kernels:
+        padded = jnp.zeros((8, 128), jnp.int32).at[:count, : 2 * CLIPS].set(lengths)
+        (
+            layer_raw,
+            normed_self,
+            queries,
+            pair,
+            pair_other,
+            cotangent,
+            text_input,
+            projected,
+            text_pair,
+            lengths_other,
+        ) = entry(
+            place,
+            frames,
+            text_states,
+            grad_out,
+            padded,
+            self_gain,
+            self_shift,
+            self_qkv,
+            text_proj,
+            text_bias,
+            cross_kv,
+        )
+        lengths_other = lengths_other[:count, : 2 * CLIPS]
+        layer_input = layer_raw.astype(F32)
+    else:
+        lengths_other = place.swap_core(lengths)
+        text_half = place.to_rows(text_states)
+        layer_raw = place.to_rows(frames)
+        text_input = jnp.concatenate([text_half, place.swap_core(text_half)], axis=0)
+        cotangent = place.to_rows(grad_out)
+        projected = (dot(text_input, text_proj) + text_bias).astype(BF)
+        text_pair = dot(projected, cross_kv).astype(BF)
+        layer_input = layer_raw.astype(F32)
+        normed_self = layer_norm(layer_input, self_gain, self_shift)
+        pair = dot(normed_self, self_qkv[:, width:]).astype(BF)
+        pair_other = place.swap_core(pair)
+        queries = dot(normed_self, self_qkv[:, :width]).astype(BF)
+    cotangent_other = place.swap_core(cotangent)
     mine = place.spot // count == place.core
     row_lengths = pick(jnp.where(mine, lengths, lengths_other), place.spot % count, 0)
-    clips = clip_lengths.shape[1]
-    frame_ends = jnp.cumsum(row_lengths[:clips])
-    text_ends = jnp.cumsum(row_lengths[clips:])
-
-    def segments(positions, ends):
-        return jnp.sum((positions[:, None] >= ends[None, :]).astype(jnp.int32), axis=1)
-
-    own_segment = segments(place.positions(frame_total, place.core), frame_ends)
-    other_segment = segments(place.positions(frame_total, 1 - place.core), frame_ends)
-    text_positions = jnp.concatenate(
-        [place.positions(text_total, place.core), place.positions(text_total, 1 - place.core)]
-    )
-    text_segment = segments(text_positions, text_ends)
-    query_segment = own_segment[None, :]
-    own_segment, other_segment = own_segment[:, None], other_segment[:, None]
-    text_segment = text_segment[:, None]
-    core = place.core.reshape(1).astype(jnp.int32)
-
-    text_half = place.to_rows(text_states)
-    layer_raw = place.to_rows(frames)
-    text_input = jnp.concatenate([text_half, place.swap_core(text_half)], axis=0)
-    cotangent = place.to_rows(after(grad_out, layer_raw))
-    cotangent_other = place.swap_core(cotangent)
-    projected = (dot(text_input, text_proj) + text_bias).astype(BF)
-    text_pair = dot(projected, cross_kv).astype(BF)
-
-    layer_input = layer_raw.astype(F32)
-    normed_self = layer_norm(layer_input, self_gain, self_shift)
-    pair = dot(normed_self, self_qkv[:, width:]).astype(BF)
-    pair_other = place.swap_core(pair)
-    queries = dot(normed_self, self_qkv[:, :width]).astype(BF)
-    self_mix, self_lse = self_forward(
-        core, query_segment, own_segment, other_segment, queries, pair, pair_other
-    )
+
+    self_mix, self_lse, _ = self_forward(row_lengths, queries, pair, pair_other)
     first = layer_input + dot(self_mix, self_out)
     normed_cross = layer_norm(first, cross_gain, cross_shift)
     cross_queries = dot(normed_cross, cross_query).astype(BF)
-    cross_mix, cross_lse = cross_forward(query_segment, text_segment, cross_queries, text_pair)
+    cross_mix, cross_lse, _ = cross_forward(row_lengths, cross_queries, text_pair)
     second = first + dot(cross_mix, cross_out)
     normed_feed = layer_norm(second, feed_gain, feed_shift)
 
-    nx, ny, nz, seq = place.nx, place.ny, place.nz, place.seq
     meta = jnp.stack([place.core, place.x, place.y, place.z]).astype(jnp.int32)
     normed_other = place.swap_core(normed_feed)
     fed = feed(
         place, meta, normed_feed, normed_other, cotangent, cotangent_other, feed_in, feed_out
     )
     result, result_away, grad_normed_feed, grad_away = fed[:4]
-    grad_in, grad_out_parts = fed[4 : 4 + nx], fed[4 + nx :]
+    up_parts, low_parts, out_parts = fed[4 : 4 + nx], fed[4 + nx : 4 + nx + ny], fed[4 + nx + ny :]
     grad_normed_feed = grad_normed_feed + place.swap_core(grad_away).astype(F32)
-
-    def x_piece(k):
-        return lambda: grad_in[k].astype(F32)
-
-    def y_piece(k):
-        return lambda: grad_out_parts[k].astype(F32)
-
-    in_half = ring_sum([x_piece(k) for k in range(nx)], place.next_x).astype(BF)
-    out_half = ring_sum([y_piece(k) for k in range(ny)], place.next_y).astype(BF)
 
     grad_part, grad_feed_gain, grad_feed_shift = norm_backward(second, feed_gain, grad_normed_feed)
     grad_second = cotangent.astype(F32) + grad_part
     grad_second_branch = grad_second.astype(BF)
     grad_cross_mix = dot(grad_second_branch, cross_out, 1, 1).astype(BF)
-    grad_cross_queries, grad_text_keys, grad_text_values = cross_backward(
-        query_segment,
-        text_segment,
+    grad_cross_queries, grad_text_keys, grad_text_values, cross_mark = cross_backward(
+        row_lengths,
         cross_queries,
         text_pair,
         grad_cross_mix,
         cross_mix,
         cross_lse,
     )
+    late = cross_mark[0, 0]
+    in_up = ring_sum([lambda a=a: a.astype(F32) for a in up_parts], place.next_x)
+    in_low = ring_sum([lambda a=a: a.astype(F32) for a in low_parts], place.next_y)
+    in_up, in_low = (in_up + late).astype(BF), (in_low + late).astype(BF)
+    order = ring_order(nz)
+
+    def out_step(sent, t, mark):
+        return (out_parts[order[t]].astype(F32) + place.next_z(sent).astype(F32) + mark).astype(BF)
+
+    out_sum = out_step(out_parts[order[0]], 1, late)
+
     grad_normed_cross = dot(grad_cross_queries, cross_query, 1, 1)
     grad_part, grad_cross_gain, grad_cross_shift = norm_backward(first, cross_gain, grad_normed_cross)
     grad_first = grad_second + grad_part
@@ -1432,7 +1697,6 @@
     grad_projected = dot(grad_pair, cross_kv, 1, 1).astype(BF)
     grad_text_bias = jnp.sum(grad_projected.astype(F32), axis=0)
     grad_text = dot(grad_projected, text_proj, 1, 1)
-    block, piece = width // place.rows, width // seq
     padding = block - text_input.shape[1] // place.rows
     lefts = [cross_mix, normed_cross, projected, text_input, self_mix]
     rights = [
@@ -1447,10 +1711,7 @@
 
     def backward_self(*before):
         return self_backward(
-            core,
-            query_segment,
-            own_segment,
-            other_segment,
+            row_lengths,
             queries,
             pair,
             pair_other,
@@ -1458,7 +1719,7 @@
             self_mix,
             self_lse,
             before=before,
-        )
+        )[:5]
 
     def vector_list(grad_gain, grad_shift):
         return jnp.stack(
@@ -1474,13 +1735,18 @@
             ]
         )
 
-    if nx == 2 and ny == 2 and piece % 128 == 0:
-        send_up, send_low, keep_up, keep_low = middle_parts(place, lefts, rights)
+    if kernels:
+        send_up, send_low, keep_up, keep_low, result, middle_mark = middle_parts(
+            place, count, lefts, rights, result, result_away, (in_up[0], in_low[0], out_sum)
+        )
         up_got, low_got = place.next_x(send_up), place.next_y(send_low)
-        in_got, out_got = place.next_y(in_half[0]), place.next_x(out_half[0])
-        grads = backward_self(in_half[0], out_half[0])
+        in_up_got, in_low_got = place.next_y(in_up[0]), place.next_x(in_low[0])
+        out_sum = out_step(out_sum, 2, middle_mark[0, 0])
+        grads = backward_self(out_sum)
+        for t in range(3, nz):
+            out_sum = out_step(out_sum, t, 0.0)
         nothing = jnp.zeros_like(grad_feed_shift)
-        sum_self_qkv, spread, sum_feed, vectors, result, grad_frames, grad_text = final_sums(
+        sum_self_qkv, spread, sum_feed, vectors, grad_frames, grad_text = final_sums(
             place,
             count,
             normed_self,
@@ -1493,13 +1759,12 @@
             up_got,
             keep_low,
             low_got,
-            in_half[1],
-            in_got,
-            out_half[1],
-            out_got,
+            in_up[1],
+            in_up_got,
+            in_low[1],
+            in_low_got,
+            out_sum,
             vector_list(nothing, nothing),
-            result,
-            result_away,
             grad_text,
         )
         sum_self_out = spread[:, 5 * piece :]
@@ -1511,11 +1776,13 @@
             values = (grads[2].astype(F32) + place.swap_core(grads[4]).astype(F32)).astype(BF)
             return jnp.concatenate([grads[0], keys, values], axis=1)
 
+        for t in range(2, nz):
+            out_sum = out_step(out_sum, t, 0.0)
         text_blocks = text_input.reshape(text_total, place.rows, -1)
         text_padded = jnp.pad(text_blocks, ((0, 0), (0, 0), (0, padding))).reshape(text_total, width)
         lefts[3] = text_padded
         sum_feed, spread, sum_self_qkv, sum_self_out, grad_packed = permuted_sums(
-            place, meta, in_half, out_half, lefts, rights, normed_self, packed_self
+            place, meta, in_up, in_low, out_sum, lefts, rights, normed_self, packed_self
         )
         result = (result + place.swap_core(result_away).astype(F32)).astype(BF)
         result = place.from_rows(result, count)

time: 380 us -> 358 us (0.942)
  Pallas kernels: 232 us -> 263 us
  waiting for transfers between devices: 31.7 us -> 3.22 us
  starting transfers between devices: 26.4 us -> 12.7 us
  matrix products: 27.4 us -> 18 us
  local copies, waits for them, and re-layouts: 26.5 us -> 32.8 us
    ppermute x18 -> x12, waiting for transfers between devices: 31.7 us -> 3.22 us  [permute(): return lax.ppermute(value, (ROWS, SEQ), pairs)]
    pallas_call x2 -> x3, Pallas kernels: 123 us -> 151 us  [the longest x1 89.7 us: final_sums(): pl.pallas_call(functools.partial(final_kernel, nz), in_specs=[ANY_SPEC if...]
    ppermute x18 -> x12, starting transfers between devices: 26.4 us -> 12.7 us  [permute(): return lax.ppermute(value, (ROWS, SEQ), pairs)]
    dot_general x12 -> x8, matrix products: 27.4 us -> 18 us  [dot(): lax.dot_general(left, right, (((left_dim,), (right_dim,)), ((), ())), pre...]
    unnamed x133 -> x119, local copies, waits for them, and re-layouts: 12.8 us -> 20.8 us
    convert_element_type x2 -> x5, other arithmetic: 4.36 us -> 8.12 us  [the longest x3 5.91 us: out_step(): (out_parts[order[t]].astype(F32) + place.next_z(sent).astype(F32) + mark)...]
  transfers between devices with their start and end apart: 18 -> 12, of which waited for: 7 -> 2; matrix products, arithmetic and copies ran while one was open for 15% -> 10% of each run, Pallas kernels for 22% -> 18%
where the time goes in v2:
time: 358 us; the launch traced here: 353 us
  Pallas kernels  263 us (73%)
  local copies, waits for them, and re-layouts  32.8 us (9%)
  other arithmetic  22.7 us (6%)
  matrix products  18 us (5%)
  starting transfers between devices  12.7 us (4%)
    pallas_call x1, Pallas kernels, final_sums(): pl.pallas_call(functools.partial(final_kernel, nz), in_specs=[ANY_SPEC if...  89.7 us
    pallas_call x4, Pallas kernels, attention_call(): pl.pallas_call(kernel, grid=(pairs,), in_specs=in_specs, out_specs=out_sp...  70.3 us
    pallas_call x1, Pallas kernels, feed(): pl.pallas_call(functools.partial(feed_kernel, (nx, ny, nz, chunk)), grid_...  41.1 us
    pallas_call x1, Pallas kernels, entry(): pl.pallas_call(functools.partial(entry_kernel, place.nz), in_specs=[ANY_S...  36.6 us
    pallas_call x1, Pallas kernels, middle_parts(): pl.pallas_call(without(marked(functools.partial(middle_kernel, (nz, piece...  24.8 us
    unnamed x119, local copies, waits for them, and re-layouts  20.8 us
    dot_general x8, matrix products, dot(): lax.dot_general(left, right, (((left_dim,), (right_dim,)), ((), ())), pre...  18 us
    ppermute x12, starting transfers between devices, permute(): return lax.ppermute(value, (ROWS, SEQ), pairs)  12.7 us
  transfers between devices with their start and end apart: 12, of which 2 were waited for; matrix products, arithmetic and copies ran while one was open for 10% of the time, Pallas kernels for 18%

profile of v2, /device:TPU:0, one launch (start us, length us, event | category | flops | bytes accessed | tf_op | source)
XLA Modules:
  0.0 353.2 jit_solution(18381724383491948174)
XLA Ops:
  4.5 36.6 %shard_map.331 = (bf16[512,1024]{1,0:T(8,128)(2,1)S(1)}, bf16[512,1024]{1,0:T(8,128)(2,1)S(1)}, bf16[512,1024]{1,0:T(8,128)(2,1)S(1)}, bf16[512,2048]{1,0:T(8,12...) custom-call(bf16[2,256,1024]{2,1,0:T(8,128)(2,1)} %frames_ref.1, ...), custom_call_target="tpu_custom_call" | custom-call | flops 10737418240 | bytes 20971520 | tf_op jit(solution)/shard_map/pallas_call | solution.py:956
  41.9 1.0 copy-done.16
  44.7 2.3 copy-done.14
  47.0 1.2 copy-done.18
  48.2 18.8 %shard_map.332 = (bf16[512,1024]{1,0:T(8,128)(2,1)S(1)}, f32[8,8,512]{2,1,0:T(8,128)S(1)}, f32[8,128]{1,0:T(8,128)}) custom-call(s32[8]{0:T(128)S(1)} %fusion.3.refs_0_, bf16[512,1024]{1,0:T(8,128)(2,1)S(1)} %copy-done.18, bf16[512,2048]{1,0:T(8,128)(2,1)S(1)} %copy-done.14, bf16[512,2048]{1,0:T(8,128)(2,1)S(1)} %copy-done.14, ...), custom_call_target="tpu_custom_call" | custom-call | flops 5368709120 | bytes 8388608 | tf_op jit(solution)/shard_map/pallas_call | solution.py:454
  67.0 1.3 fusion.9
  69.6 1.2 copy-done.56
  70.7 1.3 convolution_convert_fusion.2.refs_1_
  72.3 13.1 %shard_map.333 = (bf16[512,1024]{1,0:T(8,128)(2,1)S(1)}, f32[8,8,512]{2,1,0:T(8,128)S(1)}, f32[8,128]{1,0:T(8,128)}) custom-call(s32[8]{0:T(128)S(1)} %fusion.3.refs_0_, bf16[512,1024]{1,0:T(8,128)(2,1)S(1)} %convolution_convert_fusion.2.refs_1_, bf16[256,2048]{1,0:T(8,128)(2,1)S(1)} %copy-done.12, bf16[256,2048]{1,0:T(8,128)(2,1)S(1)} %copy-done.12), custom_call_target="tpu_custom_call" | custom-call | flops 2147483648 | bytes 8388608 | tf_op jit(solution)/shard_map/pallas_call | solution.py:454
  85.4 1.3 fusion.10
  89.2 1.7 collective-permute-done.other_ref
  90.9 1.5 collective-permute-done.1.gother_ref
  92.4 41.1 %shard_map.334 = (f32[512,1024]{1,0:T(8,128)}, bf16[512,1024]{1,0:T(8,128)(2,1)}, f32[512,1024]{1,0:T(8,128)}, bf16[512,1024]{1,0:T(8,128)(2,1)}, bf16[2,512,512...) custom-call(s32[4]{0:T(128)} %pad_add_fusion.1.meta_ref, ...), custom_call_target="tpu_custom_call" | custom-call | flops 25769803776 | bytes 41943040 | tf_op jit(solution)/shard_map/pallas_call | solution.py:640
  133.6 1.6 collective-permute-start.5
  135.6 1.2 collective-permute-start.3
  136.8 3.4 multiply_reduce_fusion
  140.6 3.4 fusion.7
  144.0 1.3 convolution_convert_fusion.1.refs_4_
  145.6 12.3 %shard_map.335 = (bf16[512,1024]{1,0:T(8,128)(2,1)S(1)}, bf16[256,1024]{1,0:T(8,128)(2,1)S(1)}, bf16[256,1024]{1,0:T(8,128)(2,1)S(1)}, f32[8,128]{1,0:T(8,128)S(1)}) custom-call(s32[8]{0:T(128)S(1)} %fusion.3.refs_0_, bf16[512,1024]{1,0:T(8,128)(2,1)S(1)} %convolution_convert_fusion.2.refs_1_, bf16[256,2048]{1,0:T(8,128)(2,1)S(1)} %copy-done.13, ...), custom_call_target="tpu_custom_call" | custom-call | flops 5368709120 | bytes 8388608 | tf_op jit(solution)/shard_map/pallas_call | solution.py:454
  158.0 4.2 %multiply_reduce_fusion.1 = (f32[1024]{0:T(1024)S(1)}, f32[512]{0:T(512)S(1)}, f32[512]{0:T(512)S(1)}, f32[1024]{0:T(1024)S(1)}, f32[512,1024]{1,0:T(8,128)S(1)}) fusion(f32[512,1024]{1,0:T(8,128)S(1)} %copy-done.28, f32[512]{0:T(512)S(1)} %add_rsqrt_fusion.1, f32[512]{0:T(512)S(1)} %broadcast_multiply_fusion.5, f32[1024]{0:T(1024)S(1)} %copy-done.48, ...), kind=kOutput, calls=%fused_computation.1 | convolution fusion | flops 1078457344 | bytes 7360512 | tf_op jit(solution)/shard_map/dot_general | solution.py:24
  162.7 1.1 add_convert_fusion.3
  164.7 1.1 add_convert_fusion.4
  165.8 1.1 slice_bitcast_fusion.1
  166.9 2.4 add_convert_fusion.2.refs_15_
  169.4 1.7 collective-permute-start.6
  171.1 1.2 collective-permute-start.10
  172.3 1.2 collective-permute-start.9
  173.5 2.1 convert_reduce_fusion
  175.6 2.5 fusion.6
  178.1 24.8 %shard_map.336 = (bf16[2,4,64,1536]{3,2,1,0:T(8,128)(2,1)}, bf16[2,4,64,1536]{3,2,1,0:T(8,128)(2,1)}, bf16[2,4,64,1536]{3,2,1,0:T(8,128)(2,1)}, bf16[2,4,64,1536...) custom-call(bf16[512,1024]{1,0:T(8,128)(2,1)} %copy-done.8, bf16[512,1024]{1,0:T(8,128)(2,1)} %copy-done.34, ...), custom_call_target="tpu_custom_call" | custom-call | flops 8589934592 | bytes 25165824 | tf_op jit(solution)/shard_map/pallas_call | solution.py:1097
  202.9 1.3 slice.98
  204.2 1.0 collective-permute-start.7
  205.2 1.8 collective-permute-start.8
  207.7 2.6 fusion.11.refs_20_
  210.3 3.9 %convolution_convert_fusion.refs_6_ = bf16[512,1024]{1,0:T(8,128)(2,1)} fusion(bf16[512,1024]{1,0:T(8,128)(2,1)S(1)} %copy-done.32, bf16[1024,1024]{1,0:T(8,128)(2,1)} %param.29), kind=kOutput, calls=%fused_computation.22 | convolution fusion | flops 1074266112 | bytes 4194304 | tf_op jit(solution)/shard_map/dot_general | solution.py:24
  214.2 2.2 add_convert_fusion.1.refs_9_
  216.4 1.8 collective-permute-start.11
  218.3 26.1 %shard_map.337 = (bf16[512,1024]{1,0:T(8,128)(2,1)S(1)}, bf16[512,1024]{1,0:T(8,128)(2,1)S(1)}, bf16[512,1024]{1,0:T(8,128)(2,1)S(1)}, bf16[512,1024]{1,0:T(8,12...) custom-call(s32[8]{0:T(128)S(1)} %fusion.3.refs_0_, bf16[512,1024]{1,0:T(8,128)(2,1)} %copy-done.17, ...), custom_call_target="tpu_custom_call" | custom-call | flops 13421772800 | bytes 8388608 | tf_op jit(solution)/shard_map/pallas_call | solution.py:454
  246.3 1.0 copy-done.22
  247.3 1.0 copy-done.23
  249.3 1.3 add_convert_fusion.refs_18_
  250.6 89.7 %shard_map.338 = (f32[128,768]{1,0:T(8,128)}, f32[128,1536]{1,0:T(8,128)}, f32[2,128,1024]{2,1,0:T(8,128)}, f32[8,1024]{1,0:T(8,128)}, bf16[2,256,1024]{2,1,0:T(8,128)(2,1)}, /*index=5*/bf16[2,64,768]{2,1,0:T(8,128)(2,1)}) custom-call(bf16[512,1024]{1,0:T(8,128)(2,1)} %copy-done.16, bf16[512,1024]{1,0:T(8,128)(2,1)} %copy-done.6, ...), custom_call_target="tpu_custom_call" | custom-call | flops 96636764160 | bytes 41943040 | tf_op jit(solution)/shard_map/pallas_call | solution.py:1430
  340.3 1.9 fusion.8
  342.2 1.8 slice.109
  343.9 1.5 slice.107
  345.5 1.6 convert_element_type.118
  347.9 1.0 copy.38
  349.7 1.5 constant_dynamic-slice_fusion.6
  (149 shorter events, 19.9 us)
Async XLA Ops:
  4.4 40.2 %copy-start.51 = (s32[2,4]{1,0:T(2,128)S(1)}, s32[2,4]{1,0:T(2,128)}, u32[]{:S(2)}) copy-start(s32[2,4]{1,0:T(2,128)} %param.25) | copy-start | bytes 100
  4.5 40.2 %copy-start.52 = (s32[2,4]{1,0:T(2,128)S(1)}, s32[2,4]{1,0:T(2,128)}, u32[]{:S(2)}) copy-start(s32[2,4]{1,0:T(2,128)} %param.24) | copy-start | bytes 100
  44.6 22.4 %copy-start.6 = (bf16[512,1024]{1,0:T(8,128)(2,1)}, bf16[512,1024]{1,0:T(8,128)(2,1)S(1)}, u32[]{:S(2)}) copy-start(bf16[512,1024]{1,0:T(8,128)(2,1)S(1)} %get-tuple-element.78.refs_1_) | copy-start | bytes 3145732
  44.6 43.5 %copy-start = (bf16[512,1024]{1,0:T(8,128)(2,1)}, bf16[512,1024]{1,0:T(8,128)(2,1)S(1)}, u32[]{:S(2)}) copy-start(bf16[512,1024]{1,0:T(8,128)(2,1)S(1)} %get-tuple-element.87.gown_ref) | copy-start | bytes 3145732
  44.7 2.3 copy-start.14
  48.2 18.8 %copy-start.57 = (bf16[1024,1024]{1,0:T(8,128)(2,1)S(1)}, bf16[1024,1024]{1,0:T(8,128)(2,1)}, u32[]{:S(2)}) copy-start(bf16[1024,1024]{1,0:T(8,128)(2,1)} %param.29) | copy-start | bytes 6291460
  68.4 17.1 %copy-start.27 = (f32[512,1024]{1,0:T(8,128)}, f32[512,1024]{1,0:T(8,128)S(1)}, u32[]{:S(2)}) copy-start(f32[512,1024]{1,0:T(8,128)S(1)} %get-tuple-element.172) | copy-start | bytes 6291460
  68.8 2.0 copy-start.56
  70.7 1.6 copy-start.12
  72.3 13.1 %copy-start.54 = (bf16[1024,1024]{1,0:T(8,128)(2,1)S(1)}, bf16[1024,1024]{1,0:T(8,128)(2,1)}, u32[]{:S(2)}) copy-start(bf16[1024,1024]{1,0:T(8,128)(2,1)} %param.36) | copy-start | bytes 6291460
  85.4 1.4 copy-start.8
  88.1 4.3 %copy-start.40 = (bf16[512,1024]{1,0:T(8,128)(2,1)}, bf16[512,1024]{1,0:T(8,128)(2,1)S(1)}, u32[]{:S(2)}) copy-start(bf16[512,1024]{1,0:T(8,128)(2,1)S(1)} %add_convert_fusion.5.own_ref) | copy-start | bytes 3145732
  88.1 2.8 collective-permute-start
  88.1 4.3 %collective-permute-start.1 = (bf16[512,1024]{1,0:T(8,128)(2,1)S(1)}, bf16[512,1024]{1,0:T(8,128)(2,1)}, u32[]{:S(2)}, u32[]{:S(2)}) collective-permute-start(bf16[512,1024]{1,0:T(8,128)(2,1)S(1)} %get-tuple-element.87.gown_ref), channel_id=1, source_target_pairs={{0,4},{1,5},{2,6},{3,7},{4,0},{5,1},{6,2},{7,3},{8,12},{9,13},{10,... | collective-permute-start | bytes 3145736 | tf_op jit(solution)/shard_map/ppermute | solution.py:57
  133.5 3.3 collective-permute-start.2
  133.6 33.3 %collective-permute-start.5 = (bf16[4,256,512]{2,1,0:T(8,128)(2,1)}, bf16[4,256,512]{2,1,0:T(8,128)(2,1)S(1)}, u32[]{:S(2)}, u32[]{:S(2)}) collective-permute-start(bf16[4,256,512]{2,1,0:T(8,128)(2,1)} %get-tuple-element.102), channel_id=1, source_target_pairs={{0,8},{1,9},{2,10},{3,11},{4,12},{5,13},{6,14},{7,15},{8,16},{9,17... | collective-permute-start | bytes 3145736 | tf_op jit(solution)/shard_map/ppermute | solution.py:57
  135.2 27.5 %collective-permute-start.4 = (bf16[2,512,512]{2,1,0:T(8,128)(2,1)}, bf16[2,512,512]{2,1,0:T(8,128)(2,1)S(1)}, u32[]{:S(2)}, u32[]{:S(2)}) collective-permute-start(bf16[2,512,512]{2,1,0:T(8,128)(2,1)} %get-tuple-element.100), channel_id=1, source_target_pairs={{0,2},{1,3},{2,0},{3,1},{4,6},{5,7},{6,4},{7,5},{8,10},{9,11},{10,... | collective-permute-start | bytes 3145736 | tf_op jit(solution)/shard_map/ppermute | solution.py:57
  135.6 29.1 %collective-permute-start.3 = (bf16[2,512,512]{2,1,0:T(8,128)(2,1)}, bf16[2,512,512]{2,1,0:T(8,128)(2,1)S(1)}, u32[]{:S(2)}, u32[]{:S(2)}) collective-permute-start(bf16[2,512,512]{2,1,0:T(8,128)(2,1)} %get-tuple-element.97), channel_id=1, source_target_pairs={{0,1},{1,0},{2,3},{3,2},{4,5},{5,4},{6,7},{7,6},{8,9},{9,8},{10,11... | collective-permute-start | bytes 3145736 | tf_op jit(solution)/shard_map/ppermute | solution.py:57
  136.8 3.4 copy-start.1
  136.8 3.5 copy-start.26
  136.8 3.8 %copy-start.29 = (f32[512,1024]{1,0:T(8,128)S(1)}, f32[512,1024]{1,0:T(8,128)}, u32[]{:S(2)}) copy-start(f32[512,1024]{1,0:T(8,128)} %get-tuple-element.88) | copy-start | bytes 6291460
  140.6 3.4 copy-start.55
  144.0 1.6 copy-start.13
  145.6 12.4 %copy-start.28 = (f32[512,1024]{1,0:T(8,128)S(1)}, f32[512,1024]{1,0:T(8,128)}, u32[]{:S(2)}) copy-start(f32[512,1024]{1,0:T(8,128)} %copy-done.27) | copy-start | bytes 6291460
  158.0 4.2 %copy-start.9 = (bf16[512,1024]{1,0:T(8,128)(2,1)}, bf16[512,1024]{1,0:T(8,128)(2,1)S(1)}, u32[]{:S(2)}) copy-start(bf16[512,1024]{1,0:T(8,128)(2,1)S(1)} %get-tuple-element.91.refs_6_) | copy-start | bytes 3145732
  158.0 15.5 %copy-start.10 = (bf16[256,1024]{1,0:T(8,128)(2,1)}, bf16[256,1024]{1,0:T(8,128)(2,1)S(1)}, u32[]{:S(2)}) copy-start(bf16[256,1024]{1,0:T(8,128)(2,1)S(1)} %get-tuple-element.92.refs_7_) | copy-start | bytes 1572868
  158.0 15.5 %copy-start.11 = (bf16[256,1024]{1,0:T(8,128)(2,1)}, bf16[256,1024]{1,0:T(8,128)(2,1)S(1)}, u32[]{:S(2)}) copy-start(bf16[256,1024]{1,0:T(8,128)(2,1)S(1)} %get-tuple-element.93.refs_8_) | copy-start | bytes 1572868
  158.0 4.7 %copy-start.39 = (bf16[2,512,512]{2,1,0:T(8,128)(2,1)S(1)}, bf16[2,512,512]{2,1,0:T(8,128)(2,1)}, u32[]{:S(2)}) copy-start(bf16[2,512,512]{2,1,0:T(8,128)(2,1)} %get-tuple-element.99) | copy-start | bytes 3145732
  162.7 2.0 copy-start.38
  164.7 6.4 %copy-start.44 = (bf16[512,512]{1,0:T(8,128)(2,1)}, bf16[512,512]{1,0:T(8,128)(2,1)S(1)}, u32[]{:S(2)}) copy-start(bf16[512,512]{1,0:T(8,128)(2,1)S(1)} %get-tuple-element.158.refs_14_) | copy-start | bytes 1572868
  164.7 2.2 copy-start.37
  165.8 7.7 %copy-start.53 = (bf16[1024,2048]{1,0:T(8,128)(2,1)S(1)}, bf16[1024,2048]{1,0:T(8,128)(2,1)}, u32[]{:S(2)}) copy-start(bf16[1024,2048]{1,0:T(8,128)(2,1)} %kv_ref.1) | copy-start | bytes 12582916
  169.4 44.8 %collective-permute-start.6 = (bf16[4,256,512]{2,1,0:T(8,128)(2,1)}, bf16[4,256,512]{2,1,0:T(8,128)(2,1)}, u32[]{:S(2)}, u32[]{:S(2)}) collective-permute-start(bf16[4,256,512]{2,1,0:T(8,128)(2,1)} %add_convert_fusion.2.refs_15_), channel_id=1, source_target_pairs={{0,8},{1,9},{2,10},{3,11},{4,12},{5,13},{6,14},{7,15},{8,16},{9,17... | collective-permute-start | bytes 3145736 | tf_op jit(solution)/shard_map/ppermute | solution.py:57
  171.1 79.5 %collective-permute-start.10 = (bf16[512,512]{1,0:T(8,128)(2,1)S(1)}, bf16[512,512]{1,0:T(8,128)(2,1)}, u32[]{:S(2)}, u32[]{:S(2)}) collective-permute-start(bf16[512,512]{1,0:T(8,128)(2,1)S(1)} %get-tuple-element.158.refs_14_), channel_id=1, source_target_pairs={{0,1},{1,0},{2,3},{3,2},{4,5},{5,4},{6,7},{7,6},{8,9},{9,8},{10,11... | collective-permute-start | bytes 1572872 | tf_op jit(solution)/shard_map/ppermute | solution.py:57
  172.3 78.2 %collective-permute-start.9 = (bf16[512,512]{1,0:T(8,128)(2,1)}, bf16[512,512]{1,0:T(8,128)(2,1)}, u32[]{:S(2)}, u32[]{:S(2)}) collective-permute-start(bf16[512,512]{1,0:T(8,128)(2,1)} %get-tuple-element.160.refs_13_), channel_id=1, source_target_pairs={{0,2},{1,3},{2,0},{3,1},{4,6},{5,7},{6,4},{7,5},{8,10},{9,11},{10,... | collective-permute-start | bytes 1572872 | tf_op jit(solution)/shard_map/ppermute | solution.py:57
  178.1 29.6 %copy-start.30 = (bf16[768,1024]{1,0:T(8,128)(2,1)S(1)}, bf16[768,1024]{1,0:T(8,128)(2,1)}, u32[]{:S(2)}) copy-start(bf16[768,1024]{1,0:T(8,128)(2,1)} %proj_ref.1) | copy-start | bytes 4718596
  202.9 7.4 %copy-start.32 = (bf16[512,1024]{1,0:T(8,128)(2,1)S(1)}, bf16[512,1024]{1,0:T(8,128)(2,1)}, u32[]{:S(2)}) copy-start(bf16[512,1024]{1,0:T(8,128)(2,1)} %get-tuple-element.150.refs_10_) | copy-start | bytes 3145732
  204.2 46.4 %collective-permute-start.7 = (bf16[2,4,64,1536]{3,2,1,0:T(8,128)(2,1)}, bf16[2,4,64,1536]{3,2,1,0:T(8,128)(2,1)}, u32[]{:S(2)}, u32[]{:S(2)}) collective-permute-start(bf16[2,4,64,1536]{3,2,1,0:T(8,128)(2,1)} %get-tuple-element.114), channel_id=1, source_target_pairs={{0,1},{1,0},{2,3},{3,2},{4,5},{5,4},{6,7},{7,6},{8,9},{9,8},{10,11... | collective-permute-start | bytes 4718600 | tf_op jit(solution)/shard_map/ppermute | solution.py:57
  205.2 45.4 %collective-permute-start.8 = (bf16[2,4,64,1536]{3,2,1,0:T(8,128)(2,1)}, bf16[2,4,64,1536]{3,2,1,0:T(8,128)(2,1)}, u32[]{:S(2)}, u32[]{:S(2)}) collective-permute-start(bf16[2,4,64,1536]{3,2,1,0:T(8,128)(2,1)} %get-tuple-element.116), channel_id=1, source_target_pairs={{0,2},{1,3},{2,0},{3,1},{4,6},{5,7},{6,4},{7,5},{8,10},{9,11},{10,... | collective-permute-start | bytes 4718600 | tf_op jit(solution)/shard_map/ppermute | solution.py:57
  210.3 4.0 %copy-start.35 = (bf16[4,256,512]{2,1,0:T(8,128)(2,1)S(1)}, bf16[4,256,512]{2,1,0:T(8,128)(2,1)}, u32[]{:S(2)}) copy-start(bf16[4,256,512]{2,1,0:T(8,128)(2,1)} %get-tuple-element.106) | copy-start | bytes 3145732
  216.4 1.9 copy-start.42
  216.4 32.8 %collective-permute-start.11 = (bf16[4,256,512]{2,1,0:T(8,128)(2,1)S(1)}, bf16[4,256,512]{2,1,0:T(8,128)(2,1)S(1)}, u32[]{:S(2)}, u32[]{:S(2)}) collective-permute-start(bf16[4,256,512]{2,1,0:T(8,128)(2,1)S(1)} %add_convert_fusion.1.refs_9_), channel_id=1, source_target_pairs={{0,8},{1,9},{2,10},{3,11},{4,12},{5,13},{6,14},{7,15},{8,16},{9,17... | collective-permute-start | bytes 3145736 | tf_op jit(solution)/shard_map/ppermute | solution.py:57
  218.3 31.0 %copy-start.31 = (bf16[4,256,512]{2,1,0:T(8,128)(2,1)S(1)}, bf16[4,256,512]{2,1,0:T(8,128)(2,1)}, u32[]{:S(2)}) copy-start(bf16[4,256,512]{2,1,0:T(8,128)(2,1)} %get-tuple-element.117) | copy-start | bytes 3145732
  340.3 5.2 %copy-start.33 = (bf16[2,256,1024]{2,1,0:T(8,128)(2,1)S(1)}, bf16[2,256,1024]{2,1,0:T(8,128)(2,1)}, u32[]{:S(2)}) copy-start(bf16[2,256,1024]{2,1,0:T(8,128)(2,1)} %get-tuple-element.118) | copy-start | bytes 3145732
  342.2 4.9 %copy-start.41 = (f32[2,128,1024]{2,1,0:T(8,128)S(1)}, f32[2,128,1024]{2,1,0:T(8,128)}, u32[]{:S(2)}) copy-start(f32[2,128,1024]{2,1,0:T(8,128)} %get-tuple-element.123) | copy-start | bytes 3145732
  347.0 1.9 copy-start.46
  347.0 4.2 %copy-start.36 = (bf16[2,256,1024]{2,1,0:T(8,128)(2,1)S(1)}, bf16[2,256,1024]{2,1,0:T(8,128)(2,1)}, u32[]{:S(2)}) copy-start(bf16[2,256,1024]{2,1,0:T(8,128)(2,1)} %get-tuple-element.198) | copy-start | bytes 3145732
  347.9 4.3 %copy-start.45 = (f32[128,768]{1,0:T(8,128)S(1)}, f32[128,768]{1,0:T(8,128)}, u32[]{:S(2)}) copy-start(f32[128,768]{1,0:T(8,128)} %get-tuple-element.203) | copy-start | bytes 1179652
  (22 other events, 20.8 us)

commit v3 on v2

--- a/solution.py
+++ b/solution.py
@@ -18,6 +18,7 @@
 BF = jnp.bfloat16
 F32 = jnp.float32
 VMEM_LIMIT = 48 * 1024 * 1024
+MOST_VMEM = 62 * 1024 * 1024
 
 
 def dot(left, right, left_dim=1, right_dim=0):
@@ -434,7 +435,9 @@
     return run
 
 
-def attention_call(kernel, heads, in_specs, outs, bias_shape, flops, arguments, before=()):
+def attention_call(
+    kernel, heads, in_specs, outs, bias_shape, flops, arguments, before=(), limit=VMEM_LIMIT
+):
     pairs = heads // 2
     kernel = marked(kernel, len(arguments) + len(outs))
     kernel = without(kernel, len(arguments), len(before))
@@ -458,7 +461,7 @@
         out_specs=out_specs,
         out_shape=out_shape,
         scratch_shapes=[pltpu.VMEM(bias_shape, F32)],
-        compiler_params=pltpu.CompilerParams(vmem_limit_bytes=VMEM_LIMIT),
+        compiler_params=pltpu.CompilerParams(vmem_limit_bytes=limit),
         cost_estimate=pl.CostEstimate(flops=flops, bytes_accessed=8 << 20, transcendentals=flops >> 8),
     )(*arguments)
 
@@ -514,6 +517,7 @@
         heads * 5 * 10 * length * length * PAIR * 2,
         (lengths, queries, pair, pair, pair_other, pair_other, grads, mixed, lse),
         before,
+        MOST_VMEM,
     )
 
 
@@ -564,9 +568,21 @@
 
 def feed_kernel(shape, meta_ref, own_ref, other_ref, gown_ref, gother_ref, win_ref, wout_ref, *refs):
     nx, ny, nz, chunk = shape
-    res_ref, res_other_ref, grad_ref, grad_other_ref = refs[:4]
+    res_out, res_other_out, grad_out, grad_other_out = refs[:4]
     up_refs, low_refs, gout_refs = refs[4 : 4 + nx], refs[4 + nx : 4 + nx + ny], refs[4 + nx + ny : 4 + nx + ny + nz]
-    act_ref, pre_ref, turned_ref, gturned_ref, res_acc, grad_acc = refs[4 + nx + ny + nz :]
+    (act_ref, pre_ref, turned_ref, gturned_ref, res_acc, grad_acc) = refs[4 + nx + ny + nz : 10 + nx + ny + nz]
+    res_ref, grad_ref, res_other_ref, grad_other_ref, store_sems = refs[10 + nx + ny + nz :]
+    stores = [
+        pltpu.make_async_copy(source, target, store_sems.at[number])
+        for number, (source, target) in enumerate(
+            (
+                (res_ref, res_out),
+                (res_other_ref, res_other_out),
+                (grad_ref, grad_out),
+                (grad_other_ref, grad_other_out),
+            )
+        )
+    ]
     j, i = pl.program_id(0), pl.program_id(1)
     z = meta_ref[3]
     tokens = own_ref.shape[0]
@@ -593,6 +609,13 @@
             res[at] += dot(activated, wout_ref[...])
             grad[at] += nt(before, win_ref[...])
 
+    @pl.when((i == ny - 1) & (j == nx - 1))
+    def _():
+        res_other_ref[...] = res_acc[...].astype(BF)
+        grad_other_ref[...] = grad_acc[...].astype(BF)
+        for copy in stores:
+            copy.start()
+
     rows = turned_ref.shape[0] // nz
     half = rows // 2
     for k in range(nz):
@@ -614,8 +637,8 @@
 
     @pl.when((i == ny - 1) & (j == nx - 1))
     def _():
-        res_other_ref[...] = res_acc[...].astype(BF)
-        grad_other_ref[...] = grad_acc[...].astype(BF)
+        for copy in stores:
+            copy.wait()
 
 
 def feed(place, meta, own, other, gown, gother, feed_in, feed_out):
@@ -647,7 +670,7 @@
                 pl.BlockSpec((width, part), lambda j, i, meta: (0, unit(j, i, meta))),
                 pl.BlockSpec((part, width), lambda j, i, meta: (unit(j, i, meta), 0)),
             ],
-            out_specs=[WHOLE_SPEC] * 4
+            out_specs=[ANY_SPEC] * 4
             + [up_spec(n) for n in range(nx)]
             + [low_spec] * ny
             + [gout_spec] * nz,
@@ -658,6 +681,11 @@
                 pltpu.VMEM((width, total), BF),
                 pltpu.VMEM((tokens, width), F32),
                 pltpu.VMEM((tokens, width), F32),
+                pltpu.VMEM((tokens, width), F32),
+                pltpu.VMEM((tokens, width), F32),
+                pltpu.VMEM((tokens, width), BF),
+                pltpu.VMEM((tokens, width), BF),
+                pltpu.SemaphoreType.DMA((4,)),
             ],
         ),
         out_shape=[
@@ -827,25 +855,26 @@
         self.ways, self.source_ref, self.target_ref = ways, source_ref, target_ref
         self.send_sems, self.recv_sems = send_sems, recv_sems
         self.block = source_ref.shape[1]
-        self.started = []
-
-    def start(self):
-        ways = self.ways
+        self.copies = []
         owner = jnp.where((ways.spot == 0) | (ways.spot == 3), 0, 1)
         slot = ways.spot // 2
-        to = self.target_ref.at[pl.ds(pl.multiple_of(slot * self.block, self.block), self.block)]
+        to = target_ref.at[pl.ds(pl.multiple_of(slot * self.block, self.block), self.block)]
         for r in range(2):
             row, spot = 2 * ways.z + owner, 2 * ways.core + r
             stays = (spot == ways.spot) & (row == ways.row)
             copy = pltpu.make_async_remote_copy(
-                src_ref=self.source_ref.at[r],
+                src_ref=source_ref.at[r],
                 dst_ref=to,
-                send_sem=self.send_sems.at[r],
-                recv_sem=self.recv_sems.at[slot],
+                send_sem=send_sems.at[r],
+                recv_sem=recv_sems.at[slot],
                 device_id=(row, spot),
                 device_id_type=MESH,
             )
-            local = pltpu.make_async_copy(self.source_ref.at[r], to, self.recv_sems.at[slot])
+            local = pltpu.make_async_copy(source_ref.at[r], to, recv_sems.at[slot])
+            self.copies.append((stays, copy, local))
+
+    def start(self):
+        for stays, copy, local in self.copies:
 
             @pl.when(stays)
             def _(local=local):
@@ -855,25 +884,74 @@
             def _(copy=copy):
                 copy.start()
 
-            self.started.append((stays, copy))
-
     def arrived(self, slot):
         to = self.target_ref.at[slot * self.block : (slot + 1) * self.block]
         pltpu.make_async_copy(to, to, self.recv_sems.at[slot]).wait()
 
     def finish(self):
-        for stays, copy in self.started:
+        for stays, copy, _ in self.copies:
 
             @pl.when(jnp.logical_not(stays))
             def _(copy=copy):
                 copy.wait_send()
+
+
+def self_forward_carrying(nz, lengths_ref, *refs):
+    grads_ref, cotangent_ref = refs[5], refs[8]
+    bias_ref, sends, recvs = refs[9:]
+    gathering = Gathering(Ways(nz), grads_ref, cotangent_ref, sends, recvs)
+
+    @pl.when(pl.program_id(0) == 0)
+    def _():
+        gathering.ways.meet(gathering.ways.plane())
+        gathering.start()
+
+    self_forward_kernel(lengths_ref, *refs[:5], *refs[6:8], bias_ref)
+
+    @pl.when(pl.program_id(0) == pl.num_programs(0) - 1)
+    def _():
+        for slot in range(2):
+            gathering.arrived(slot)
+        gathering.finish()
+
+
+def self_forward_and_gather(place, lengths, queries, pair, pair_other, grads):
+    rows, width = queries.shape
+    half = width // HD // 2
+    length = rows // 2
+    return pl.pallas_call(
+        functools.partial(self_forward_carrying, place.nz),
+        grid=(half,),
+        in_specs=[
+            SMEM_SPEC,
+            column(rows),
+            column(rows),
+            column(rows, half),
+            column(rows),
+            column(rows, half),
+            ANY_SPEC,
+        ],
+        out_specs=[column(rows), lse_spec(rows), ANY_SPEC],
+        out_shape=[
+            jax.ShapeDtypeStruct((rows, width), BF),
+            jax.ShapeDtypeStruct((half, 8, rows), F32),
+            jax.ShapeDtypeStruct((rows, width), BF),
+        ],
+        scratch_shapes=[pltpu.VMEM((5, length, length), F32)]
+        + [pltpu.SemaphoreType.DMA((2,))] * 2,
+        compiler_params=pltpu.CompilerParams(
+            collective_id=4, has_side_effects=True, vmem_limit_bytes=VMEM_LIMIT
+        ),
+        cost_estimate=pl.CostEstimate(
+            flops=40 * rows * length * width, bytes_accessed=8 << 20, transcendentals=0
+        ),
+    )(lengths, queries, pair, pair, pair_other, pair_other, grads)
 
 
 def entry_kernel(
     nz,
     frames_ref,
     text_ref,
-    grad_ref,
     lengths_ref,
     gain_ref,
     shift_ref,
@@ -881,16 +959,23 @@
     proj_ref,
     bias_ref,
     kv_ref,
+    input_out,
+    normed_out,
+    queries_out,
+    pair_out,
+    pair_other_ref,
+    words_out,
+    projected_out,
+    text_pair_out,
+    lengths_other_ref,
     input_ref,
     normed_ref,
     queries_ref,
     pair_ref,
-    pair_other_ref,
-    cotangent_ref,
     words_ref,
     projected_ref,
     text_pair_ref,
-    lengths_other_ref,
+    store_sems,
     qkv_here,
     proj_here,
     kv_here,
@@ -908,12 +993,18 @@
     ]
     for load in loads:
         load.start()
+    stores = []
+
+    def store(source, target):
+        copy = pltpu.make_async_copy(source, target, store_sems.at[len(stores)])
+        copy.start()
+        stores.append(copy)
+
     ways = Ways(nz)
     ways.meet(ways.plane())
     mail = Mail(send_sems, recv_sems)
     words = Gathering(ways, text_ref, words_ref, gather_sends.at[0], gather_recvs.at[0])
     frames = Gathering(ways, frames_ref, input_ref, gather_sends.at[1], gather_recvs.at[1])
-    grads = Gathering(ways, grad_ref, cotangent_ref, gather_sends.at[2], gather_recvs.at[2])
     words.start()
     frames.start()
     lengths_copy = mail.send(lengths_ref, lengths_other_ref, ways.sibling)
@@ -921,75 +1012,116 @@
     for slot in range(2):
         words.arrived(slot)
     words_copy = mail.send(words_ref.at[:half], words_ref.at[half:], ways.sibling)
-    for load in loads:
-        load.wait()
+    loads[0].wait()
+    loads[1].wait()
     words_copy.wait_recv()
+    store(words_ref, words_out)
     projected = (dot(words_ref[...], proj_here[...]) + bias_ref[...]).astype(BF)
     projected_ref[...] = projected
+    store(projected_ref, projected_out)
     text_pair_ref[...] = dot(projected, kv_here[...]).astype(BF)
+    store(text_pair_ref, text_pair_out)
+    loads[2].wait()
     width = input_ref.shape[1]
     block = input_ref.shape[0] // 2
     copies = []
     for slot in range(2):
         frames.arrived(slot)
-        if slot == 1:
-            grads.start()
         at = slice(slot * block, (slot + 1) * block)
         normed_ref[at] = layer_norm(input_ref[at].astype(F32), gain_ref[...], shift_ref[...])
+        store(input_ref.at[at], input_out.at[at])
+        store(normed_ref.at[at], normed_out.at[at])
         pair_ref[at] = dot(normed_ref[at], qkv_here[:, width:]).astype(BF)
+        store(pair_ref.at[at], pair_out.at[at])
         copies.append(mail.send(pair_ref.at[at], pair_other_ref.at[at], ways.sibling))
     queries_ref[...] = dot(normed_ref[...], qkv_here[:, :width]).astype(BF)
+    store(queries_ref, queries_out)
     lengths_copy.wait_recv()
     for copy in copies:
         copy.wait_recv()
-    for slot in range(2):
-        grads.arrived(slot)
     mail.finish()
-    for gathering in (words, frames, grads):
+    for gathering in (words, frames):
         gathering.finish()
-
-
-def entry(place, frames, text, grads, lengths, gain, shift, qkv, proj, bias, kv):
+    for copy in stores:
+        copy.wait()
+
+
+def entry(place, frames, text, lengths, gain, shift, qkv, proj, bias, kv):
     count, block, width = frames.shape
     tokens, words = count * block, 2 * count * text.shape[1]
     shape, vmem = jax.ShapeDtypeStruct, pltpu.VMEM
     return pl.pallas_call(
         functools.partial(entry_kernel, place.nz),
-        in_specs=[ANY_SPEC] * 3 + [WHOLE_SPEC] * 3 + [ANY_SPEC] * 2 + [WHOLE_SPEC, ANY_SPEC],
-        out_specs=[WHOLE_SPEC] * 10,
+        in_specs=[ANY_SPEC] * 2 + [WHOLE_SPEC] * 3 + [ANY_SPEC] * 2 + [WHOLE_SPEC, ANY_SPEC],
+        out_specs=[ANY_SPEC] * 8 + [WHOLE_SPEC],
         out_shape=[
             shape((tokens, width), BF),
             shape((tokens, width), BF),
             shape((tokens, width), BF),
             shape((tokens, 2 * width), BF),
             shape((tokens, 2 * width), BF),
-            shape((tokens, width), BF),
             shape((words, text.shape[2]), BF),
             shape((words, width), BF),
             shape((words, 2 * width), BF),
             shape(lengths.shape, jnp.int32),
         ],
         scratch_shapes=[
+            vmem((tokens, width), BF),
+            vmem((tokens, width), BF),
+            vmem((tokens, width), BF),
+            vmem((tokens, 2 * width), BF),
+            vmem((words, text.shape[2]), BF),
+            vmem((words, width), BF),
+            vmem((words, 2 * width), BF),
+            pltpu.SemaphoreType.DMA((10,)),
             vmem(qkv.shape, BF),
             vmem(proj.shape, BF),
             vmem(kv.shape, BF),
             pltpu.SemaphoreType.DMA((3,)),
             pltpu.SemaphoreType.DMA((4,)),
             pltpu.SemaphoreType.DMA((4,)),
-            pltpu.SemaphoreType.DMA((3, 2)),
-            pltpu.SemaphoreType.DMA((3, 2)),
+            pltpu.SemaphoreType.DMA((2, 2)),
+            pltpu.SemaphoreType.DMA((2, 2)),
         ],
         compiler_params=pltpu.CompilerParams(
-            collective_id=3, has_side_effects=True, vmem_limit_bytes=VMEM_LIMIT
+            collective_id=3, has_side_effects=True, vmem_limit_bytes=MOST_VMEM
         ),
         cost_estimate=pl.CostEstimate(
             flops=20 * tokens * width * width, bytes_accessed=20 << 20, transcendentals=0
         ),
-    )(frames, text, grads, lengths, gain[None], shift[None], qkv, proj, bias[None], kv)
+    )(frames, text, lengths, gain[None], shift[None], qkv, proj, bias[None], kv)
+
+
+def with_loads(kernel, count, late):
+    def run(*refs):
+        inputs, rest = list(refs[:count]), refs[count:]
+        here, sems = rest[-len(late) - 1 : -1], rest[-1]
+        copies = []
+        for number, which in enumerate(late):
+            copy = pltpu.make_async_copy(inputs[which], here[number], sems.at[number])
+            copy.start()
+            inputs[which] = here[number]
+            copies.append(copy)
+        open_copies = dict(zip(map(id, here), copies))
+
+        def wait(*wanted):
+            for ref in wanted:
+                open_copies.pop(id(ref)).wait()
+
+        kernel(wait, *inputs, *rest[: -len(late) - 1])
+
+    return run
+
+
+def load_scratch(operands, late):
+    return [pltpu.VMEM(operands[n].shape, operands[n].dtype) for n in late] + [
+        pltpu.SemaphoreType.DMA((len(late),))
+    ]
 
 
 def middle_kernel(
     shape,
+    wait,
     mixed_ref,
     normed_ref,
     projected_ref,
@@ -1003,11 +1135,25 @@
     g_first_ref,
     result_ref,
     result_away_ref,
+    in_up_ref,
+    in_up_got_ref,
+    in_low_ref,
+    in_low_got_ref,
+    out_one_ref,
+    out_one_got_ref,
+    out_zero_ref,
+    self_weight_ref,
     send_up_ref,
     send_low_ref,
     keep_up_ref,
     keep_low_ref,
     result_out,
+    in_up_keep,
+    in_up_next,
+    in_low_keep,
+    in_low_next,
+    out_next,
+    g_mix_ref,
     mixed_t,
     normed_t,
     projected_t,
@@ -1017,6 +1163,9 @@
     away_ref,
     got_ref,
     result_got_ref,
+    in_send_ref,
+    out_send_ref,
+    out_came_ref,
     send_sems,
     recv_sems,
     home_sends,
@@ -1024,12 +1173,26 @@
 ):
     nz, piece = shape
     ways = Ways(nz)
-    ways.meet(ways.plane())
+    ways.meet(ways.plane() + [ways.above, ways.below])
     mail = Mail(send_sems, recv_sems)
     result_copy = mail.send(result_away_ref, result_got_ref, ways.sibling)
+    wait(out_one_ref, out_one_got_ref)
+    out_send_ref[...] = out_one_ref[...] + out_one_got_ref[...]
+    out_copy = mail.send(out_send_ref, out_came_ref, ways.above)
+    wait(in_up_ref, in_up_got_ref, in_low_ref, in_low_got_ref)
+    in_send_ref[0] = in_up_ref[0] + in_up_got_ref[0]
+    in_send_ref[1] = in_low_ref[0] + in_low_got_ref[0]
+    in_copies = [
+        mail.send(in_send_ref.at[0], in_up_next, ways.across_y),
+        mail.send(in_send_ref.at[1], in_low_next, ways.across_x),
+    ]
+    in_up_keep[...] = in_up_ref[1] + in_up_got_ref[1]
+    in_low_keep[...] = in_low_ref[1] + in_low_got_ref[1]
     home = Home(ways, result_out, home_sends, home_recvs)
     for left, to in ((mixed_ref, mixed_t), (normed_ref, normed_t), (projected_ref, projected_t), (self_ref, self_t)):
+        wait(left)
         to[...] = turned(left[...])
+    wait(text_ref)
     turned_text = turned(text_ref[...])
     block = own_ref.shape[2]
     count = 2 * nz
@@ -1046,6 +1209,7 @@
         (keep_up_ref.at[1], keep_low_ref.at[1]),
     )
     copies = []
+    wait(g_second_ref, g_query_ref, g_keys_ref, g_values_ref, g_projected_ref, g_first_ref)
 
     def settle(q):
         copies[q].wait_recv()
@@ -1075,6 +1239,7 @@
             if ref is away_ref:
                 copies.append(mail.send(away_ref.at[q], got_ref.at[q], ways.sibling))
         if q == 0:
+            wait(result_ref)
             result_copy.wait_recv()
             result_got_ref[...] = (result_ref[...] + result_got_ref[...].astype(F32)).astype(BF)
             slots = result_ref.shape[0] // 2
@@ -1082,39 +1247,53 @@
                 home.send(result_got_ref.at[slot * slots : (slot + 1) * slots], slot)
         else:
             settle(q - 1)
+    wait(self_weight_ref)
+    g_mix_ref[...] = nt(g_first_ref[...], self_weight_ref[...]).astype(BF)
     settle(3)
+    for copy in in_copies:
+        copy.wait_recv()
+    out_copy.wait_recv()
+    wait(out_zero_ref)
+    out_next[...] = out_zero_ref[...] + out_came_ref[...]
     mail.finish()
     home.finish()
 
 
-def middle_parts(place, count, lefts, rights, result, result_away, before):
+def middle_parts(place, count, lefts, rights, result, result_away, feeds, weight):
     nz = place.nz
     depth, width = lefts[0].shape[1], rights[0].shape[1]
     piece, block = width // place.seq, depth // place.rows
     columns = piece * len(rights)
     out = jax.ShapeDtypeStruct((2, nz, block // 2, columns), BF)
     big = pltpu.VMEM((4, nz, block, columns), BF)
+    operands = [*lefts, *rights, result, result_away, *feeds, weight]
+    late = (17, 18, 13, 14, 15, 16, 0, 1, 2, 4, 3, 5, 6, 7, 8, 9, 10, 11, 20, 19)
     return pl.pallas_call(
-        without(marked(functools.partial(middle_kernel, (nz, piece)), 18), 13, len(before)),
-        in_specs=[WHOLE_SPEC] * 12 + [ANY_SPEC] * (1 + len(before)),
-        out_specs=[WHOLE_SPEC] * 4 + [ANY_SPEC, WHOLE_SPEC],
+        with_loads(functools.partial(middle_kernel, (nz, piece)), len(operands), late),
+        in_specs=[ANY_SPEC] * len(operands),
+        out_specs=[WHOLE_SPEC] * 4
+        + [ANY_SPEC, WHOLE_SPEC, ANY_SPEC, WHOLE_SPEC, ANY_SPEC, WHOLE_SPEC, WHOLE_SPEC],
         out_shape=[out] * 4
-        + [jax.ShapeDtypeStruct((count, result.shape[0] // count, width), BF), MARK],
+        + [jax.ShapeDtypeStruct((count, result.shape[0] // count, width), BF)]
+        + [jax.ShapeDtypeStruct(feeds[0].shape[1:], BF)] * 4
+        + [jax.ShapeDtypeStruct(feeds[4].shape, BF), jax.ShapeDtypeStruct(result.shape, BF)],
         scratch_shapes=[pltpu.VMEM((depth, left.shape[0]), BF) for left in lefts]
         + [big] * 3
-        + [pltpu.VMEM(result.shape, BF)]
-        + [pltpu.SemaphoreType.DMA((5,))] * 2
-        + [pltpu.SemaphoreType.DMA((2,))] * 2,
+        + [pltpu.VMEM(result.shape, BF), pltpu.VMEM(feeds[0].shape, BF)]
+        + [pltpu.VMEM(feeds[4].shape, BF)] * 2
+        + [pltpu.SemaphoreType.DMA((8,))] * 2
+        + [pltpu.SemaphoreType.DMA((2,))] * 2
+        + load_scratch(operands, late),
         compiler_params=pltpu.CompilerParams(
-            collective_id=2, has_side_effects=True, vmem_limit_bytes=60 * 1024 * 1024
+            collective_id=2, has_side_effects=True, vmem_limit_bytes=63 * 1024 * 1024
         ),
         cost_estimate=pl.CostEstimate(
             flops=2 * 8 * 512 * depth * width, bytes_accessed=24 << 20, transcendentals=0
         ),
-    )(*lefts, *rights, result, result_away, *before)
-
-
-def final_kernel(nz, *refs):
+    )(*operands)
+
+
+def final_kernel(nz, wait, *refs):
     (
         normed_ref,
         input_ref,
@@ -1134,15 +1313,16 @@
         in_up_got_ref,
         in_low_ref,
         in_low_got_ref,
+        out_last_ref,
+        out_got_ref,
+        vector_ref,
+        projected_ref,
+        proj_ref,
+    ) = refs[:23]
+    (qkv_ref, middle_ref, feed_ref, sum_ref, frames_out, text_out) = refs[23:29]
+    (
         out_ref,
-        vector_ref,
         text_ref,
-    ) = refs[:21]
-    (qkv_ref, middle_ref, feed_ref, sum_ref, frames_out, text_out) = refs[21:27]
-    (
-        weight_here,
-        first_here,
-        load_sems,
         packed_ref,
         k_got_ref,
         v_got_ref,
@@ -1175,16 +1355,7 @@
         recv_sems,
         home_sends,
         home_recvs,
-    ) = refs[27:]
-    loads = [
-        pltpu.make_async_copy(source, target, load_sems.at[number])
-        for number, (source, target) in enumerate(
-            ((weight_ref, weight_here), (first_ref, first_here))
-        )
-    ]
-    for load in loads:
-        load.start()
-    weight_ref, first_ref = weight_here, first_here
+    ) = refs[29:]
     ways = Ways(nz)
     core, z = ways.core, ways.z
     sibling, across_x, across_y, above = ways.sibling, ways.across_x, ways.across_y, ways.above
@@ -1198,6 +1369,8 @@
     k_copy = mail.send(k_away_ref, k_got_ref, sibling)
     v_copy = mail.send(v_away_ref, v_got_ref, sibling)
 
+    wait(out_last_ref, out_got_ref)
+    out_ref[...] = out_last_ref[...] + out_got_ref[...]
     out_copies = [mail.send(out_ref.at[q], out_x_ref.at[q], across_x) for q in range(2)]
     feed_copies, feed_last_copies = [], {}
 
@@ -1221,9 +1394,11 @@
         feed_send_ref[t, feed_half:] = lower_part.astype(BF)
         feed_copies.append(mail.send(feed_send_ref.at[t], feed_ring_ref.at[t], above))
 
+    wait(in_up_ref, in_up_got_ref, in_low_ref, in_low_got_ref)
     feed_step(0)
 
     mid_copies = {}
+    wait(upper_ref, upper_got_ref, lower_ref, lower_got_ref)
     for k in ring:
         mid_ref[k, :half] = upper_ref[0, k] + upper_got_ref[0, k]
         mid_ref[k, half:] = lower_ref[0, k] + lower_got_ref[0, k]
@@ -1231,10 +1406,7 @@
             mail.send(mid_ref.at[k, :half], mid_up_ref.at[k], across_y),
             mail.send(mid_ref.at[k, half:], mid_low_ref.at[k], across_x),
         )
-    text_rows = text_ref.shape[0] // 2
-    text_away_ref[...] = text_ref[text_rows:].astype(BF)
-    text_copy = mail.send(text_away_ref, text_got_ref, sibling)
-
+    wait(normed_ref, gq_ref, gk_ref, gv_ref)
     turned_ref[...] = turned(normed_ref[...])
     packed_ref[:, :width] = gq_ref[...]
     k_copy.wait_recv()
@@ -1279,6 +1451,12 @@
         across = feed_other_ref.shape[2]
         at = pl.ds(pl.multiple_of((1 - core) * across, across), across)
         feed_ref[kind, :, at] = feed_other_ref[kind]
+
+    wait(projected_ref, proj_ref)
+    text_ref[...] = nt(projected_ref[...], proj_ref[...])
+    text_rows = text_ref.shape[0] // 2
+    text_away_ref[...] = text_ref[text_rows:].astype(BF)
+    text_copy = mail.send(text_away_ref, text_got_ref, sibling)
 
     def core_step(q):
         core_copies[q].wait_recv()
@@ -1330,8 +1508,6 @@
     core_step(3)
     out_step()
 
-    for load in loads:
-        load.wait()
     slots = tokens // 2
     text_copy.wait_recv()
     text_got_ref[...] = (text_ref[:text_rows] + text_got_ref[...].astype(F32)).astype(BF)
@@ -1340,11 +1516,13 @@
         at = slice(slot * text_rows // 2, (slot + 1) * text_rows // 2)
         text_home.send(text_got_ref.at[at], slot)
 
+    wait(weight_ref)
     acc_ref[...] = nt(packed_ref[:, :width], weight_ref[:, :width])
     acc_ref[...] += nt(packed_ref[:, width : 2 * width], weight_ref[:, width : 2 * width])
     mid_send(0)
     feed_step(1)
     acc_ref[...] += nt(packed_ref[:, 2 * width :], weight_ref[:, 2 * width :])
+    wait(input_ref, first_ref, gain_ref)
     gain_sum = jnp.zeros((1, width), F32)
     shift_sum = jnp.zeros((1, width), F32)
     chunk = min(128, tokens)
@@ -1356,6 +1534,7 @@
         k_got_ref[at] = (first_ref[at] + grad).astype(BF)
         gain_sum += gain_part[None]
         shift_sum += shift_part[None]
+    wait(vector_ref)
     vector_out_ref[0] = vector_ref[...]
     vector_out_ref[0, 0:1] = gain_sum
     vector_out_ref[0, 1:2] = shift_sum
@@ -1413,13 +1592,14 @@
             copy.wait_send()
 
 
-FINAL_IN_PLACE = (2, 4, 8, 9)
+FINAL_LOADS = (18, 19, 14, 15, 16, 17, 10, 11, 12, 13, 0, 5, 6, 7, 21, 22, 4, 1, 2, 3, 20)
 
 
 def final_sums(place, count, *operands):
     nz = place.nz
     normed, weight, upper, in_up = operands[0], operands[4], operands[10], operands[14]
-    vectors, text = operands[19], operands[20]
+    vectors, projected, proj = operands[20], operands[21], operands[22]
+    words, text_width = projected.shape[0], proj.shape[0]
     tokens, width = normed.shape
     block, piece = width // place.rows, weight.shape[1] // place.seq
     half, middle = block // 2, upper.shape[3]
@@ -1428,10 +1608,8 @@
     copies = 2 + 3 + nz - 1 + 2 + 2 * nz + 1 + 4 + 3 + nz - 1 + 4 + 2 * nz + 2 * (nz - 1)
     vmem = pltpu.VMEM
     return pl.pallas_call(
-        functools.partial(final_kernel, nz),
-        in_specs=[
-            ANY_SPEC if n in FINAL_IN_PLACE else WHOLE_SPEC for n in range(len(operands))
-        ],
+        with_loads(functools.partial(final_kernel, nz), len(operands), FINAL_LOADS),
+        in_specs=[ANY_SPEC] * len(operands),
         out_specs=[WHOLE_SPEC] * 4 + [ANY_SPEC] * 2,
         out_shape=[
             jax.ShapeDtypeStruct((block, piece), F32),
@@ -1439,12 +1617,11 @@
             jax.ShapeDtypeStruct((2, block, 2 * feed_width), F32),
             jax.ShapeDtypeStruct(vectors.shape, F32),
             jax.ShapeDtypeStruct((count, tokens // count, width), BF),
-            jax.ShapeDtypeStruct((count, text.shape[0] // 2 // count, text.shape[1]), BF),
+            jax.ShapeDtypeStruct((count, words // 2 // count, text_width), BF),
         ],
         scratch_shapes=[
-            vmem(weight.shape, BF),
-            vmem((tokens, width), F32),
-            pltpu.SemaphoreType.DMA((2,)),
+            vmem((4, feed_rows, feed_width), BF),
+            vmem((words, text_width), F32),
             vmem((tokens, 3 * width), BF),
             vmem((tokens, width), BF),
             vmem((tokens, width), BF),
@@ -1471,13 +1648,14 @@
             vmem((2, feed_rows // 2, feed_width), F32),
             vmem((4,) + vectors.shape, F32),
             vmem((2 + nz,) + vectors.shape, F32),
-            vmem((text.shape[0] // 2, text.shape[1]), BF),
-            vmem((text.shape[0] // 2, text.shape[1]), BF),
+            vmem((words // 2, text_width), BF),
+            vmem((words // 2, text_width), BF),
             pltpu.SemaphoreType.DMA((copies,)),
             pltpu.SemaphoreType.DMA((copies,)),
             pltpu.SemaphoreType.DMA((2, 2)),
             pltpu.SemaphoreType.DMA((2, 2)),
-        ],
+        ]
+        + load_scratch(operands, FINAL_LOADS),
         compiler_params=pltpu.CompilerParams(
             collective_id=1, has_side_effects=True, vmem_limit_bytes=63 * 1024 * 1024
         ),
@@ -1485,6 +1663,44 @@
             flops=60 * tokens * width * weight.shape[1], bytes_accessed=40 << 20, transcendentals=0
         ),
     )(*operands)
+
+
+def last_kernel(padding, qkv_ref, middle_ref, feed_ref, frames_ref, text_ref, *outs):
+    frames_out, text_out, qkv_out, self_out, query_out, proj_out, kv_out, cross_out, in_out, out_out = outs
+    piece = self_out.shape[1]
+    frames_out[...] = frames_ref[...].astype(F32)
+    text_out[...] = text_ref[...].astype(F32)
+    qkv_out[...] = qkv_ref[...]
+    cross_out[...] = middle_ref[:, :piece]
+    query_out[...] = middle_ref[:, piece : 2 * piece]
+    kv_out[...] = middle_ref[:, 2 * piece : 4 * piece]
+    proj_out[...] = middle_ref[: proj_out.shape[0], 4 * piece : 5 * piece]
+    self_out[...] = middle_ref[:, 5 * piece :]
+    in_out[...] = feed_ref[0]
+    out_out[...] = jnp.swapaxes(feed_ref[1], 0, 1)
+
+
+def last_step(padding, piece, qkv, middle, feed_sums, frames, text):
+    block, across = qkv.shape[0], feed_sums.shape[2]
+    shapes = [
+        frames.shape,
+        text.shape,
+        qkv.shape,
+        (block, piece),
+        (block, piece),
+        (block - padding, piece),
+        (block, 2 * piece),
+        (block, piece),
+        (block, across),
+        (across, block),
+    ]
+    return pl.pallas_call(
+        functools.partial(last_kernel, padding),
+        in_specs=[WHOLE_SPEC] * 5,
+        out_specs=[WHOLE_SPEC] * len(shapes),
+        out_shape=[jax.ShapeDtypeStruct(shape, F32) for shape in shapes],
+        compiler_params=pltpu.CompilerParams(vmem_limit_bytes=MOST_VMEM),
+    )(qkv, middle, feed_sums, frames, text)
 
 
 def permuted_sums(place, meta, in_up, in_low, out_sum, lefts, rights, normed_self, backward_self):
@@ -1600,7 +1816,7 @@
 
     nx, ny, nz, seq = place.nx, place.ny, place.nz, place.seq
     block, piece = width // place.rows, width // seq
-    kernels = nx == 2 and ny == 2 and piece % 128 == 0
+    kernels = nx == 2 and ny == 2 and nz == 4 and piece % 128 == 0
     lengths = jnp.concatenate([clip_lengths, text_lengths], axis=1)
     if kernels:
         padded = jnp.zeros((8, 128), jnp.int32).at[:count, : 2 * CLIPS].set(lengths)
@@ -1610,7 +1826,6 @@
             queries,
             pair,
             pair_other,
-            cotangent,
             text_input,
             projected,
             text_pair,
@@ -1619,7 +1834,6 @@
             place,
             frames,
             text_states,
-            grad_out,
             padded,
             self_gain,
             self_shift,
@@ -1643,11 +1857,16 @@
         pair = dot(normed_self, self_qkv[:, width:]).astype(BF)
         pair_other = place.swap_core(pair)
         queries = dot(normed_self, self_qkv[:, :width]).astype(BF)
-    cotangent_other = place.swap_core(cotangent)
     mine = place.spot // count == place.core
     row_lengths = pick(jnp.where(mine, lengths, lengths_other), place.spot % count, 0)
 
-    self_mix, self_lse, _ = self_forward(row_lengths, queries, pair, pair_other)
+    if kernels:
+        self_mix, self_lse, cotangent = self_forward_and_gather(
+            place, row_lengths, queries, pair, pair_other, grad_out
+        )
+    else:
+        self_mix, self_lse, _ = self_forward(row_lengths, queries, pair, pair_other)
+    cotangent_other = place.swap_core(cotangent)
     first = layer_input + dot(self_mix, self_out)
     normed_cross = layer_norm(first, cross_gain, cross_shift)
     cross_queries = dot(normed_cross, cross_query).astype(BF)
@@ -1668,7 +1887,7 @@
     grad_second = cotangent.astype(F32) + grad_part
     grad_second_branch = grad_second.astype(BF)
     grad_cross_mix = dot(grad_second_branch, cross_out, 1, 1).astype(BF)
-    grad_cross_queries, grad_text_keys, grad_text_values, cross_mark = cross_backward(
+    grad_cross_queries, grad_text_keys, grad_text_values, _ = cross_backward(
         row_lengths,
         cross_queries,
         text_pair,
@@ -1676,27 +1895,14 @@
         cross_mix,
         cross_lse,
     )
-    late = cross_mark[0, 0]
-    in_up = ring_sum([lambda a=a: a.astype(F32) for a in up_parts], place.next_x)
-    in_low = ring_sum([lambda a=a: a.astype(F32) for a in low_parts], place.next_y)
-    in_up, in_low = (in_up + late).astype(BF), (in_low + late).astype(BF)
-    order = ring_order(nz)
-
-    def out_step(sent, t, mark):
-        return (out_parts[order[t]].astype(F32) + place.next_z(sent).astype(F32) + mark).astype(BF)
-
-    out_sum = out_step(out_parts[order[0]], 1, late)
-
     grad_normed_cross = dot(grad_cross_queries, cross_query, 1, 1)
     grad_part, grad_cross_gain, grad_cross_shift = norm_backward(first, cross_gain, grad_normed_cross)
     grad_first = grad_second + grad_part
     grad_first_branch = grad_first.astype(BF)
-    grad_self_mix = dot(grad_first_branch, self_out, 1, 1).astype(BF)
 
     grad_pair = jnp.concatenate([grad_text_keys, grad_text_values], axis=1)
     grad_projected = dot(grad_pair, cross_kv, 1, 1).astype(BF)
     grad_text_bias = jnp.sum(grad_projected.astype(F32), axis=0)
-    grad_text = dot(grad_projected, text_proj, 1, 1)
     padding = block - text_input.shape[1] // place.rows
     lefts = [cross_mix, normed_cross, projected, text_input, self_mix]
     rights = [
@@ -1709,7 +1915,7 @@
     ]
     result = second + result
 
-    def backward_self(*before):
+    def backward_self(grad_self_mix, *before):
         return self_backward(
             row_lengths,
             queries,
@@ -1736,15 +1942,39 @@
         )
 
     if kernels:
-        send_up, send_low, keep_up, keep_low, result, middle_mark = middle_parts(
-            place, count, lefts, rights, result, result_away, (in_up[0], in_low[0], out_sum)
+        (
+            send_up,
+            send_low,
+            keep_up,
+            keep_low,
+            result,
+            in_up,
+            in_up_got,
+            in_low,
+            in_low_got,
+            out_sum,
+            grad_self_mix,
+        ) = middle_parts(
+            place,
+            count,
+            lefts,
+            rights,
+            result,
+            result_away,
+            (
+                up_parts[1],
+                place.next_x(up_parts[0]),
+                low_parts[1],
+                place.next_y(low_parts[0]),
+                out_parts[1],
+                place.next_z(out_parts[2]),
+                out_parts[0],
+            ),
+            self_out,
         )
         up_got, low_got = place.next_x(send_up), place.next_y(send_low)
-        in_up_got, in_low_got = place.next_y(in_up[0]), place.next_x(in_low[0])
-        out_sum = out_step(out_sum, 2, middle_mark[0, 0])
-        grads = backward_self(out_sum)
-        for t in range(3, nz):
-            out_sum = out_step(out_sum, t, 0.0)
+        out_got = place.next_z(out_sum)
+        grads = backward_self(grad_self_mix)
         nothing = jnp.zeros_like(grad_feed_shift)
         sum_self_qkv, spread, sum_feed, vectors, grad_frames, grad_text = final_sums(
             place,
@@ -1759,25 +1989,40 @@
             up_got,
             keep_low,
             low_got,
-            in_up[1],
+            in_up,
             in_up_got,
-            in_low[1],
+            in_low,
             in_low_got,
-            out_sum,
+            out_parts[3],
+            out_got,
             vector_list(nothing, nothing),
+            grad_projected,
+            text_proj,
+        )
+        (
+            grad_frames,
             grad_text,
-        )
-        sum_self_out = spread[:, 5 * piece :]
+            sum_self_qkv,
+            sum_self_out,
+            sum_cross_query,
+            sum_text_proj,
+            sum_cross_kv,
+            sum_cross_out,
+            sum_feed_in,
+            sum_feed_out,
+        ) = last_step(padding, piece, sum_self_qkv, spread, sum_feed, grad_frames, grad_text)
     else:
 
         def packed_self(*before):
-            grads = backward_self(*before)
+            grads = backward_self(dot(grad_first_branch, self_out, 1, 1).astype(BF), *before)
             keys = (grads[1].astype(F32) + place.swap_core(grads[3]).astype(F32)).astype(BF)
             values = (grads[2].astype(F32) + place.swap_core(grads[4]).astype(F32)).astype(BF)
             return jnp.concatenate([grads[0], keys, values], axis=1)
 
-        for t in range(2, nz):
-            out_sum = out_step(out_sum, t, 0.0)
+        in_up = ring_sum([lambda a=a: a.astype(F32) for a in up_parts], place.next_x).astype(BF)
+        in_low = ring_sum([lambda a=a: a.astype(F32) for a in low_parts], place.next_y).astype(BF)
+        out_sum = ring_sum([lambda a=a: a.astype(F32) for a in out_parts], place.next_z).astype(BF)
+        grad_text = dot(grad_projected, text_proj, 1, 1)
         text_blocks = text_input.reshape(text_total, place.rows, -1)
         text_padded = jnp.pad(text_blocks, ((0, 0), (0, 0), (0, padding))).reshape(text_total, width)
         lefts[3] = text_padded
@@ -1794,14 +2039,16 @@
         grad_text = (grad_text[:half] + text_away.astype(F32)).astype(BF)
         grad_text = place.from_rows(grad_text, count)
         vectors = place.vector_sum(vector_list(grad_gain, grad_shift))
-    sum_cross_out, sum_cross_query = spread[:, :piece], spread[:, piece : 2 * piece]
-    sum_cross_kv, sum_text_proj = spread[:, 2 * piece : 4 * piece], spread[:, 4 * piece : 5 * piece]
-    sum_text_proj = sum_text_proj[: block - padding]
+        sum_cross_out, sum_cross_query = spread[:, :piece], spread[:, piece : 2 * piece]
+        sum_cross_kv, sum_text_proj = spread[:, 2 * piece : 4 * piece], spread[:, 4 * piece : 5 * piece]
+        sum_text_proj = sum_text_proj[: block - padding]
+        sum_feed_in, sum_feed_out = sum_feed[0], jnp.swapaxes(sum_feed[1], 0, 1)
+        grad_frames, grad_text = grad_frames.astype(F32), grad_text.astype(F32)
     vectors = pick(vectors.reshape(8, seq, width // seq), place.spot, 1)
     return (
         result,
-        grad_frames.astype(F32),
-        grad_text.astype(F32),
+        grad_frames,
+        grad_text,
         vectors[0],
         vectors[1],
         sum_self_qkv,
@@ -1815,8 +2062,8 @@
         sum_cross_out,
         vectors[5],
         vectors[6],
-        sum_feed[0],
-        jnp.swapaxes(sum_feed[1], 0, 1),
+        sum_feed_in,
+        sum_feed_out,
     )
 
 

time: 358 us -> 316 us (0.88)
  local copies, waits for them, and re-layouts: 32.8 us -> 8.22 us
  other arithmetic: 22.7 us -> 11.9 us
  waiting for transfers between devices: 3.22 us -> 11.9 us
  matrix products: 18 us -> 11.6 us
  starting transfers between devices: 12.7 us -> 6.66 us
    pallas_call x2 -> x4, Pallas kernels: 115 us -> 144 us  [the longest x1 86.3 us: final_sums(): pl.pallas_call(with_loads(functools.partial(final_kernel, nz), len(operan...]
    pallas_call x4 -> x3, Pallas kernels: 70.3 us -> 51.4 us  [attention_call(): pl.pallas_call(kernel, grid=(pairs,), in_specs=in_specs, out_specs=out_sp...]
    unnamed x119 -> x69, local copies, waits for them, and re-layouts: 20.8 us -> 5.4 us
    pallas_call x1, Pallas kernels: 36.6 us -> 26.1 us  [entry(): pl.pallas_call(functools.partial(entry_kernel, place.nz), in_specs=[ANY_S...]
    convert_element_type x7 -> x0, other arithmetic: 10.5 us -> none  [the longest x3 5.91 us: out_step(): (out_parts[order[t]].astype(F32) + place.next_z(sent).astype(F32) + mark)...]
    ppermute x12 -> x9, waiting for transfers between devices: 3.22 us -> 11.9 us  [permute(): return lax.ppermute(value, (ROWS, SEQ), pairs)]
    slice x5 -> x0, local copies, waits for them, and re-layouts: 6.96 us -> none  [the longest x1 1.87 us: shards(): spread[:, :piece]]
    dot_general x8 -> x6, matrix products: 18 us -> 11.6 us  [dot(): lax.dot_general(left, right, (((left_dim,), (right_dim,)), ((), ())), pre...]
  transfers between devices with their start and end apart: 12 -> 9, of which waited for: 2 -> 3; matrix products, arithmetic and copies ran while one was open for 10% -> 5% of each run, Pallas kernels for 18% -> 12%
where the time goes in v3:
time: 316 us; the launch traced here: 312 us
  Pallas kernels  260 us (82%)
  other arithmetic  11.9 us (4%)
  waiting for transfers between devices  11.9 us (4%)
  matrix products  11.6 us (4%)
  local copies, waits for them, and re-layouts  8.22 us (3%)
  starting transfers between devices  6.66 us (2%)
    pallas_call x1, Pallas kernels, final_sums(): pl.pallas_call(with_loads(functools.partial(final_kernel, nz), len(operan...  86.3 us
    pallas_call x3, Pallas kernels, attention_call(): pl.pallas_call(kernel, grid=(pairs,), in_specs=in_specs, out_specs=out_sp...  51.4 us
    pallas_call x1, Pallas kernels, feed(): pl.pallas_call(functools.partial(feed_kernel, (nx, ny, nz, chunk)), grid_...  39.1 us
    pallas_call x1, Pallas kernels, middle_parts(): pl.pallas_call(with_loads(functools.partial(middle_kernel, (nz, piece)),...  32.5 us
    pallas_call x1, Pallas kernels, entry(): pl.pallas_call(functools.partial(entry_kernel, place.nz), in_specs=[ANY_S...  26.1 us
    pallas_call x1, Pallas kernels, self_forward_and_gather(): pl.pallas_call(functools.partial(self_forward_carrying, place.nz), grid=(...  20.5 us
    ppermute x9, waiting for transfers between devices, permute(): return lax.ppermute(value, (ROWS, SEQ), pairs)  11.9 us
    dot_general x6, matrix products, dot(): lax.dot_general(left, right, (((left_dim,), (right_dim,)), ((), ())), pre...  11.6 us
  transfers between devices with their start and end apart: 9, of which 3 were waited for; matrix products, arithmetic and copies ran while one was open for 5% of the time, Pallas kernels for 12%

profile of v3, /device:TPU:0, one launch (start us, length us, event | category | flops | bytes accessed | tf_op | source)
XLA Modules:
  0.0 311.8 jit_solution(13256067826921892326)
XLA Ops:
  0.7 0.8 pad_add_fusion
  1.5 0.6 scatter.4.lengths_ref
  2.1 26.1 %shard_map.331 = (bf16[512,1024]{1,0:T(8,128)(2,1)}, bf16[512,1024]{1,0:T(8,128)(2,1)}, bf16[512,1024]{1,0:T(8,128)(2,1)}, bf16[512,2048]{1,0:T(8,128)(2,1)}, bf...) custom-call(bf16[2,256,1024]{2,1,0:T(8,128)(2,1)} %frames_ref.1, ...), custom_call_target="tpu_custom_call" | custom-call | flops 10737418240 | bytes 20971520 | tf_op jit(solution)/shard_map/pallas_call | solution.py:1053
  28.2 0.8 slice_select_fusion
  29.0 1.2 copy-done.11
  30.2 20.5 %shard_map.332 = (bf16[512,1024]{1,0:T(8,128)(2,1)S(1)}, f32[8,8,512]{2,1,0:T(8,128)S(1)}, bf16[512,1024]{1,0:T(8,128)(2,1)S(1)}) custom-call(s32[8]{0:T(128)S(1)} %fusion.3.lengths_ref.refs_0_, bf16[512,1024]{1,0:T(8,128)(2,1)S(1)} %copy-done.11, bf16[512,2048]{1,0:T(8,128)(2,1)} %get-tuple-element.94.refs_1_.refs_2_.refs_3_, ...), custom_call_target="tpu_custom_call" | custom-call | flops 5368709120 | bytes 8388608 | tf_op jit(solution)/shard_map/pallas_call | solution.py:922
  50.8 1.4 fusion.8
  52.2 0.3 multiply_reduce_fusion.5
  52.6 0.3 copy-done.23
  52.9 0.4 add_convert_fusion.1.refs_1_
  53.3 1.2 copy-done.31
  54.5 1.3 convolution_convert_fusion.1.refs_1_
  55.8 0.3 copy-done.12
  56.1 13.1 %shard_map.333 = (bf16[512,1024]{1,0:T(8,128)(2,1)S(1)}, f32[8,8,512]{2,1,0:T(8,128)S(1)}, f32[8,128]{1,0:T(8,128)}) custom-call(s32[8]{0:T(128)S(1)} %fusion.3.lengths_ref.refs_0_, bf16[512,1024]{1,0:T(8,128)(2,1)S(1)} %convolution_convert_fusion.1.refs_1_, bf16[256,2048]{1,0:T(8,128)(2,1)S(1)} %copy-done.12, bf16[256,2048]{1,0:T(8,128)(2,1)S(1)} %copy-done.12), custom_call_target="tpu_custom_call" | custom-call | flops 2147483648 | bytes 8388608 | tf_op jit(solution)/shard_map/pallas_call | solution.py:457
  69.2 1.4 fusion.9
  70.6 0.3 multiply_reduce_fusion.4
  71.0 0.3 copy-done.22
  71.3 1.5 add_convert_fusion.own_ref
  72.8 0.5 collective-permute-start.1
  73.3 0.6 pad_add_fusion.1.meta_ref
  73.8 3.3 %collective-permute-done.other_ref = bf16[512,1024]{1,0:T(8,128)(2,1)} collective-permute-done((bf16[512,1024]{1,0:T(8,128)(2,1)}, bf16[512,1024]{1,0:T(8,128)(2,1)}, u32[]{:S(2)}, u32[]{:S(2)}) %collective-permute-start) | collective-permute-done | bytes 1048608 | tf_op jit(solution)/shard_map/ppermute | solution.py:58
  77.2 39.1 %shard_map.334 = (f32[512,1024]{1,0:T(8,128)}, bf16[512,1024]{1,0:T(8,128)(2,1)}, f32[512,1024]{1,0:T(8,128)}, bf16[512,1024]{1,0:T(8,128)(2,1)}, bf16[2,512,512...) custom-call(s32[4]{0:T(128)} %pad_add_fusion.1.meta_ref, ...), custom_call_target="tpu_custom_call" | custom-call | flops 25769803776 | bytes 41943040 | tf_op jit(solution)/shard_map/pallas_call | solution.py:663
  116.2 0.2 collective-permute-start.2
  116.5 1.0 collective-permute-start.3
  117.5 0.6 collective-permute-start.4
  118.1 1.6 collective-permute-start.5
  119.6 2.8 multiply_reduce_fusion
  122.5 0.3 copy-done.18
  122.8 2.0 fusion.7
  124.8 1.3 convolution_convert_fusion.refs_4_
  126.2 0.3 copy-done.8
  126.4 0.3 copy-done.13
  126.7 13.3 %shard_map.335 = (bf16[512,1024]{1,0:T(8,128)(2,1)S(1)}, bf16[256,1024]{1,0:T(8,128)(2,1)S(1)}, bf16[256,1024]{1,0:T(8,128)(2,1)S(1)}, f32[8,128]{1,0:T(8,128)}) custom-call(s32[8]{0:T(128)S(1)} %fusion.3.lengths_ref.refs_0_, bf16[512,1024]{1,0:T(8,128)(2,1)S(1)} %copy-done.8, bf16[256,2048]{1,0:T(8,128)(2,1)S(1)} %copy-done.13, ...), custom_call_target="tpu_custom_call" | custom-call | flops 5368709120 | bytes 8388608 | tf_op jit(solution)/shard_map/pallas_call | solution.py:457
  140.1 4.2 %multiply_reduce_fusion.1 = (f32[1024]{0:T(1024)S(1)}, f32[512]{0:T(512)S(1)}, f32[512]{0:T(512)S(1)}, f32[1024]{0:T(1024)S(1)}, f32[512,1024]{1,0:T(8,128)S(1)}) fusion(f32[512,1024]{1,0:T(8,128)S(1)} %copy-done.16, f32[512]{0:T(512)S(1)} %add_rsqrt_fusion.1, f32[512]{0:T(512)S(1)} %broadcast_multiply_fusion.5, f32[1024]{0:T(1024)S(1)} %copy-done.23, ...), kind=kOutput, calls=%fused_computation.1 | convolution fusion | flops 1078457344 | bytes 7360512 | tf_op jit(solution)/shard_map/dot_general | solution.py:25
  144.4 2.1 convert_reduce_fusion
  146.5 2.4 fusion.6
  148.9 32.5 %shard_map.336 = (bf16[2,4,64,1536]{3,2,1,0:T(8,128)(2,1)}, bf16[2,4,64,1536]{3,2,1,0:T(8,128)(2,1)}, bf16[2,4,64,1536]{3,2,1,0:T(8,128)(2,1)}, bf16[2,4,64,1536...) custom-call(bf16[512,1024]{1,0:T(8,128)(2,1)} %copy-done.5, ...), custom_call_target="tpu_custom_call" | custom-call | flops 8589934592 | bytes 25165824 | tf_op jit(solution)/shard_map/pallas_call | solution.py:1271
  181.4 1.1 collective-permute-start.6
  182.5 1.0 collective-permute-start.7
  183.5 0.7 collective-permute-start.8
  184.2 0.7 stack.47.refs_20_
  184.8 25.0 %shard_map.337 = (bf16[512,1024]{1,0:T(8,128)(2,1)}, bf16[512,1024]{1,0:T(8,128)(2,1)}, bf16[512,1024]{1,0:T(8,128)(2,1)}, bf16[512,1024]{1,0:T(8,128)(2,1)}, bf...) custom-call(s32[8]{0:T(128)} %copy-done.3, bf16[512,1024]{1,0:T(8,128)(2,1)} %get-tuple-element.93.refs_0_.refs_1_, ...), custom_call_target="tpu_custom_call" | custom-call | flops 13421772800 | bytes 8388608 | tf_op jit(solution)/shard_map/pallas_call | solution.py:457
  209.9 7.8 %collective-permute-done.6.refs_11_ = bf16[2,4,64,1536]{3,2,1,0:T(8,128)(2,1)} collective-permute-done((bf16[2,4,64,1536]{3,2,1,0:T(8,128)(2,1)}, bf16[2,4,64,1536]{3,2,1,0:T(8,128)(2,1)}, u32[]{:S(2)}, u32[]{:S(2)}) %collective-permute-start.6) | collective-permute-done | bytes 1572896 | tf_op jit(solution)/shard_map/ppermute | solution.py:58
  217.7 0.7 collective-permute-done.7.refs_13_
  218.4 86.3 %shard_map.338 = (f32[128,768]{1,0:T(8,128)}, f32[128,1536]{1,0:T(8,128)}, f32[2,128,1024]{2,1,0:T(8,128)}, f32[8,1024]{1,0:T(8,128)}, bf16[2,256,1024]{2,1,0:T(8,128)(2,1)}, /*index=5*/bf16[2,64,768]{2,1,0:T(8,128)(2,1)}) custom-call(bf16[512,1024]{1,0:T(8,128)(2,1)} %get-tuple-element.118.refs_0_, bf16[512,1024]{1,0:T(8,128)(2,1)} %get-tuple-element.92.refs_1_, ...), custom_call_target="tpu_custom_call" | custom-call | flops 96636764160 | bytes 41943040 | tf_op jit(solution)/shard_map/pallas_call | solution.py:1610
  304.8 4.3 %shard_map.339 = (f32[2,256,1024]{2,1,0:T(8,128)}, f32[2,64,768]{2,1,0:T(8,128)}, f32[128,768]{1,0:T(8,128)}, f32[128,256]{1,0:T(8,128)}, f32[128,256]{1,0:T(8,1...) custom-call(f32[128,768]{1,0:T(8,128)} %get-tuple-element.136.qkv_re, ...), custom_call_target="tpu_custom_call" | custom-call | tf_op jit(solution)/shard_map/pallas_call | solution.py:1697
  309.1 1.5 constant_dynamic-slice_fusion.6
  310.7 1.0 copy.39
  (77 shorter events, 0.3 us)
Async XLA Ops:
  2.0 26.1 %copy-start.26 = (s32[2,4]{1,0:T(2,128)S(1)}, s32[2,4]{1,0:T(2,128)}, u32[]{:S(2)}) copy-start(s32[2,4]{1,0:T(2,128)} %param.25) | copy-start | bytes 100
  2.1 26.1 %copy-start.27 = (s32[2,4]{1,0:T(2,128)S(1)}, s32[2,4]{1,0:T(2,128)}, u32[]{:S(2)}) copy-start(s32[2,4]{1,0:T(2,128)} %param.24) | copy-start | bytes 100
  2.1 26.9 %copy-start.2 = (bf16[2,256,1024]{2,1,0:T(8,128)(2,1)S(1)}, bf16[2,256,1024]{2,1,0:T(8,128)(2,1)}, u32[]{:S(2)}) copy-start(bf16[2,256,1024]{2,1,0:T(8,128)(2,1)} %refs_5_.1) | copy-start | bytes 3145732
  29.0 97.2 %copy-start.3 = (s32[8]{0:T(128)}, s32[8]{0:T(128)S(1)}, u32[]{:S(2)}) copy-start(s32[8]{0:T(128)S(1)} %fusion.3.lengths_ref.refs_0_) | copy-start | bytes 100
  29.0 1.2 copy-start.11
  30.2 20.6 %copy-start.32 = (bf16[1024,1024]{1,0:T(8,128)(2,1)S(1)}, bf16[1024,1024]{1,0:T(8,128)(2,1)}, u32[]{:S(2)}) copy-start(bf16[1024,1024]{1,0:T(8,128)(2,1)} %refs_20_.1) | copy-start | bytes 6291460
  30.2 20.6 %copy-start.33 = (bf16[512,1024]{1,0:T(8,128)(2,1)S(1)}, bf16[512,1024]{1,0:T(8,128)(2,1)}, u32[]{:S(2)}) copy-start(bf16[512,1024]{1,0:T(8,128)(2,1)} %get-tuple-element.92.refs_1_) | copy-start | bytes 3145732
  50.7 1.4 copy-start.4
  50.7 1.4 copy-start.14
  50.7 22.0 %copy-start = (bf16[512,1024]{1,0:T(8,128)(2,1)}, bf16[512,1024]{1,0:T(8,128)(2,1)S(1)}, u32[]{:S(2)}) copy-start(bf16[512,1024]{1,0:T(8,128)(2,1)S(1)} %get-tuple-element.101.gown_ref) | copy-start | bytes 3145732
  52.1 17.1 %copy-start.15 = (f32[512,1024]{1,0:T(8,128)}, f32[512,1024]{1,0:T(8,128)S(1)}, u32[]{:S(2)}) copy-start(f32[512,1024]{1,0:T(8,128)S(1)} %get-tuple-element.173) | copy-start | bytes 6291460
  52.2 0.7 copy-start.23
  52.2 0.8 copy-start.24
  52.5 2.0 copy-start.31
  54.5 1.3 copy-start.19
  54.5 1.6 copy-start.12
  55.8 13.4 %copy-start.7 = (bf16[512,1024]{1,0:T(8,128)(2,1)}, bf16[512,1024]{1,0:T(8,128)(2,1)S(1)}, u32[]{:S(2)}) copy-start(bf16[512,1024]{1,0:T(8,128)(2,1)S(1)} %convolution_convert_fusion.1.refs_1_) | copy-start | bytes 3145732
  56.1 13.1 %copy-start.29 = (bf16[1024,1024]{1,0:T(8,128)(2,1)S(1)}, bf16[1024,1024]{1,0:T(8,128)(2,1)}, u32[]{:S(2)}) copy-start(bf16[1024,1024]{1,0:T(8,128)(2,1)} %param.36) | copy-start | bytes 6291460
  69.2 1.4 copy-start.5
  70.6 0.7 copy-start.22
  70.6 0.7 copy-start.25
  72.7 4.4 %collective-permute-start = (bf16[512,1024]{1,0:T(8,128)(2,1)}, bf16[512,1024]{1,0:T(8,128)(2,1)}, u32[]{:S(2)}, u32[]{:S(2)}) collective-permute-start(bf16[512,1024]{1,0:T(8,128)(2,1)} %add_convert_fusion.own_ref), channel_id=1, source_target_pairs={{0,4},{1,5},{2,6},{3,7},{4,0},{5,1},{6,2},{7,3},{8,12},{9,13},{10,... | collective-permute-start | bytes 3145736 | tf_op jit(solution)/shard_map/ppermute | solution.py:58
  72.8 4.4 %collective-permute-start.1 = (bf16[512,1024]{1,0:T(8,128)(2,1)S(1)}, bf16[512,1024]{1,0:T(8,128)(2,1)}, u32[]{:S(2)}, u32[]{:S(2)}) collective-permute-start(bf16[512,1024]{1,0:T(8,128)(2,1)S(1)} %get-tuple-element.101.gown_ref), channel_id=1, source_target_pairs={{0,4},{1,5},{2,6},{3,7},{4,0},{5,1},{6,2},{7,3},{8,12},{9,13},{10,... | collective-permute-start | bytes 3145736 | tf_op jit(solution)/shard_map/ppermute | solution.py:58
  116.2 3.4 %collective-permute-start.2 = (bf16[512,1024]{1,0:T(8,128)(2,1)}, bf16[512,1024]{1,0:T(8,128)(2,1)S(1)}, u32[]{:S(2)}, u32[]{:S(2)}) collective-permute-start(bf16[512,1024]{1,0:T(8,128)(2,1)} %get-tuple-element.103), channel_id=1, source_target_pairs={{0,4},{1,5},{2,6},{3,7},{4,0},{5,1},{6,2},{7,3},{8,12},{9,13},{10,... | collective-permute-start | bytes 3145736 | tf_op jit(solution)/shard_map/ppermute | solution.py:58
  116.5 32.4 %collective-permute-start.3 = (bf16[2,512,512]{2,1,0:T(8,128)(2,1)}, bf16[2,512,512]{2,1,0:T(8,128)(2,1)}, u32[]{:S(2)}, u32[]{:S(2)}) collective-permute-start(bf16[2,512,512]{2,1,0:T(8,128)(2,1)} %get-tuple-element.111), channel_id=1, source_target_pairs={{0,1},{1,0},{2,3},{3,2},{4,5},{5,4},{6,7},{7,6},{8,9},{9,8},{10,11... | collective-permute-start | bytes 3145736 | tf_op jit(solution)/shard_map/ppermute | solution.py:58
  117.5 31.4 %collective-permute-start.4 = (bf16[2,512,512]{2,1,0:T(8,128)(2,1)}, bf16[2,512,512]{2,1,0:T(8,128)(2,1)}, u32[]{:S(2)}, u32[]{:S(2)}) collective-permute-start(bf16[2,512,512]{2,1,0:T(8,128)(2,1)} %get-tuple-element.113), channel_id=1, source_target_pairs={{0,2},{1,3},{2,0},{3,1},{4,6},{5,7},{6,4},{7,5},{8,10},{9,11},{10,... | collective-permute-start | bytes 3145736 | tf_op jit(solution)/shard_map/ppermute | solution.py:58
  118.1 30.8 %collective-permute-start.5 = (bf16[4,256,512]{2,1,0:T(8,128)(2,1)}, bf16[4,256,512]{2,1,0:T(8,128)(2,1)}, u32[]{:S(2)}, u32[]{:S(2)}) collective-permute-start(bf16[4,256,512]{2,1,0:T(8,128)(2,1)} %get-tuple-element.115), channel_id=1, source_target_pairs={{0,8},{1,9},{2,10},{3,11},{4,12},{5,13},{6,14},{7,15},{8,16},{9,17... | collective-permute-start | bytes 3145736 | tf_op jit(solution)/shard_map/ppermute | solution.py:58
  119.6 2.8 copy-start.1
  119.6 2.8 copy-start.17
  119.6 3.2 %copy-start.18 = (f32[512,1024]{1,0:T(8,128)S(1)}, f32[512,1024]{1,0:T(8,128)}, u32[]{:S(2)}) copy-start(f32[512,1024]{1,0:T(8,128)} %get-tuple-element.108) | copy-start | bytes 6291460
  122.8 2.0 copy-start.30
  124.8 1.3 copy-start.21
  124.8 1.6 copy-start.8
  124.8 1.9 copy-start.13
  126.7 13.4 %copy-start.16 = (f32[512,1024]{1,0:T(8,128)S(1)}, f32[512,1024]{1,0:T(8,128)}, u32[]{:S(2)}) copy-start(f32[512,1024]{1,0:T(8,128)} %copy-done.15) | copy-start | bytes 6291460
  140.1 4.2 %copy-start.6 = (bf16[512,1024]{1,0:T(8,128)(2,1)}, bf16[512,1024]{1,0:T(8,128)(2,1)S(1)}, u32[]{:S(2)}) copy-start(bf16[512,1024]{1,0:T(8,128)(2,1)S(1)} %get-tuple-element.105.refs_6_) | copy-start | bytes 3145732
  140.1 4.2 %copy-start.9 = (bf16[256,1024]{1,0:T(8,128)(2,1)}, bf16[256,1024]{1,0:T(8,128)(2,1)S(1)}, u32[]{:S(2)}) copy-start(bf16[256,1024]{1,0:T(8,128)(2,1)S(1)} %get-tuple-element.106.refs_7_) | copy-start | bytes 1572868
  140.1 4.2 %copy-start.10 = (bf16[256,1024]{1,0:T(8,128)(2,1)}, bf16[256,1024]{1,0:T(8,128)(2,1)S(1)}, u32[]{:S(2)}) copy-start(bf16[256,1024]{1,0:T(8,128)(2,1)S(1)} %get-tuple-element.107.refs_8_) | copy-start | bytes 1572868
  140.1 4.2 %copy-start.28 = (bf16[1024,2048]{1,0:T(8,128)(2,1)S(1)}, bf16[1024,2048]{1,0:T(8,128)(2,1)}, u32[]{:S(2)}) copy-start(bf16[1024,2048]{1,0:T(8,128)(2,1)} %kv_ref.1) | copy-start | bytes 12582916
  181.4 36.3 %collective-permute-start.6 = (bf16[2,4,64,1536]{3,2,1,0:T(8,128)(2,1)}, bf16[2,4,64,1536]{3,2,1,0:T(8,128)(2,1)}, u32[]{:S(2)}, u32[]{:S(2)}) collective-permute-start(bf16[2,4,64,1536]{3,2,1,0:T(8,128)(2,1)} %get-tuple-element.127), channel_id=1, source_target_pairs={{0,1},{1,0},{2,3},{3,2},{4,5},{5,4},{6,7},{7,6},{8,9},{9,8},{10,11... | collective-permute-start | bytes 4718600 | tf_op jit(solution)/shard_map/ppermute | solution.py:58
  182.5 36.0 %collective-permute-start.7 = (bf16[2,4,64,1536]{3,2,1,0:T(8,128)(2,1)}, bf16[2,4,64,1536]{3,2,1,0:T(8,128)(2,1)}, u32[]{:S(2)}, u32[]{:S(2)}) collective-permute-start(bf16[2,4,64,1536]{3,2,1,0:T(8,128)(2,1)} %get-tuple-element.129), channel_id=1, source_target_pairs={{0,2},{1,3},{2,0},{3,1},{4,6},{5,7},{6,4},{7,5},{8,10},{9,11},{10,... | collective-permute-start | bytes 4718600 | tf_op jit(solution)/shard_map/ppermute | solution.py:58
  183.5 26.4 %collective-permute-start.8 = (bf16[4,256,512]{2,1,0:T(8,128)(2,1)}, bf16[4,256,512]{2,1,0:T(8,128)(2,1)}, u32[]{:S(2)}, u32[]{:S(2)}) collective-permute-start(bf16[4,256,512]{2,1,0:T(8,128)(2,1)} %get-tuple-element.135), channel_id=1, source_target_pairs={{0,8},{1,9},{2,10},{3,11},{4,12},{5,13},{6,14},{7,15},{8,16},{9,17... | collective-permute-start | bytes 3145736 | tf_op jit(solution)/shard_map/ppermute | solution.py:58
  304.8 5.9 %copy-start.20 = (bf16[2,256,1024]{2,1,0:T(8,128)(2,1)S(1)}, bf16[2,256,1024]{2,1,0:T(8,128)(2,1)}, u32[]{:S(2)}) copy-start(bf16[2,256,1024]{2,1,0:T(8,128)(2,1)} %get-tuple-element.199) | copy-start | bytes 3145732

commit v4 on v3

--- a/solution.py
+++ b/solution.py
@@ -278,12 +278,12 @@
 
 
 def self_forward_kernel(
-    lengths_ref, q_ref, k_ref, v_ref, ko_ref, vo_ref, o_ref, lse_ref, bias_ref
+    lengths_ref, q_ref, k_ref, v_ref, ko_ref, vo_ref, o_ref, lse_ref, bias_ref, fresh=True
 ):
     core = lax.axis_index(ROWS) % 2
     length = bias_ref.shape[1]
 
-    @pl.when(pl.program_id(0) == 0)
+    @pl.when((pl.program_id(0) == 0) & fresh)
     def _():
         self_biases(core, lengths_ref, bias_ref)
 
@@ -323,11 +323,12 @@
     dko_ref,
     dvo_ref,
     bias_ref,
+    fresh=True,
 ):
     core = lax.axis_index(ROWS) % 2
     length = bias_ref.shape[1]
 
-    @pl.when(pl.program_id(0) == 0)
+    @pl.when((pl.program_id(0) == 0) & fresh)
     def _():
         self_biases(core, lengths_ref, bias_ref)
 
@@ -363,10 +364,10 @@
                         ref[where] = value.astype(BF)
 
 
-def cross_forward_kernel(lengths_ref, q_ref, k_ref, v_ref, o_ref, lse_ref, bias_ref):
+def cross_forward_kernel(lengths_ref, q_ref, k_ref, v_ref, o_ref, lse_ref, bias_ref, fresh=True):
     length = q_ref.shape[0] // 2
 
-    @pl.when(pl.program_id(0) == 0)
+    @pl.when((pl.program_id(0) == 0) & fresh)
     def _():
         cross_bias(lengths_ref, bias_ref)
 
@@ -389,10 +390,11 @@
     dk_ref,
     dv_ref,
     bias_ref,
+    fresh=True,
 ):
     length = q_ref.shape[0] // 2
 
-    @pl.when(pl.program_id(0) == 0)
+    @pl.when((pl.program_id(0) == 0) & fresh)
     def _():
         cross_bias(lengths_ref, bias_ref)
 
@@ -406,8 +408,26 @@
     dv_ref[...] = sums[1].astype(BF)
 
 
+GROUP = 2
+
+
 def column(rows, first=0):
-    return pl.BlockSpec((rows, PAIR), lambda i: (0, first + i))
+    return pl.BlockSpec((rows, GROUP * PAIR), lambda i: (0, first // GROUP + i))
+
+
+def grouped(kernel):
+    def part(ref, pair):
+        if len(ref.shape) == 2 and ref.shape[1] == GROUP * PAIR and ref.dtype == BF:
+            return ref.at[:, pair * PAIR : (pair + 1) * PAIR]
+        if len(ref.shape) == 3 and ref.shape[:2] == (GROUP, 8):
+            return ref.at[pair : pair + 1]
+        return ref
+
+    def run(*refs):
+        for pair in range(GROUP):
+            kernel(*[part(ref, pair) for ref in refs], fresh=pair == 0)
+
+    return run
 
 
 SMEM_SPEC = pl.BlockSpec(memory_space=pltpu.SMEM)
@@ -439,7 +459,7 @@
     kernel, heads, in_specs, outs, bias_shape, flops, arguments, before=(), limit=VMEM_LIMIT
 ):
     pairs = heads // 2
-    kernel = marked(kernel, len(arguments) + len(outs))
+    kernel = marked(grouped(kernel), len(arguments) + len(outs))
     kernel = without(kernel, len(arguments), len(before))
     in_specs = list(in_specs) + [ANY_SPEC] * len(before)
     arguments = tuple(arguments) + tuple(before)
@@ -448,7 +468,7 @@
         if rows is None:
             queries = outs[0]
             out_shape.append(jax.ShapeDtypeStruct((pairs, 8, queries), F32))
-            out_specs.append(pl.BlockSpec((1, 8, queries), lambda i: (i, 0, 0)))
+            out_specs.append(lse_spec(queries))
         else:
             out_shape.append(jax.ShapeDtypeStruct((rows, pairs * PAIR), BF))
             out_specs.append(column(rows))
@@ -456,7 +476,7 @@
     out_specs.append(pl.BlockSpec((8, 128), lambda i: (0, 0)))
     return pl.pallas_call(
         kernel,
-        grid=(pairs,),
+        grid=(pairs // GROUP,),
         in_specs=in_specs,
         out_specs=out_specs,
         out_shape=out_shape,
@@ -467,7 +487,7 @@
 
 
 def lse_spec(queries):
-    return pl.BlockSpec((1, 8, queries), lambda i: (i, 0, 0))
+    return pl.BlockSpec((GROUP, 8, queries), lambda i: (i, 0, 0))
 
 
 def self_forward(lengths, queries, pair, pair_other):
@@ -566,12 +586,24 @@
     return values * inside, inside + values * bell
 
 
-def feed_kernel(shape, meta_ref, own_ref, other_ref, gown_ref, gother_ref, win_ref, wout_ref, *refs):
+def feed_kernel(shape, meta_ref, own_in, other_in, gown_in, gother_in, win_ref, wout_ref, *refs):
     nx, ny, nz, chunk = shape
     res_out, res_other_out, grad_out, grad_other_out = refs[:4]
     up_refs, low_refs, gout_refs = refs[4 : 4 + nx], refs[4 + nx : 4 + nx + ny], refs[4 + nx + ny : 4 + nx + ny + nz]
-    (act_ref, pre_ref, turned_ref, gturned_ref, res_acc, grad_acc) = refs[4 + nx + ny + nz : 10 + nx + ny + nz]
-    res_ref, grad_ref, res_other_ref, grad_other_ref, store_sems = refs[10 + nx + ny + nz :]
+    scratch = refs[4 + nx + ny + nz :]
+    act_ref, pre_ref, own_ref, other_ref, gown_ref, gother_ref, res_acc, grad_acc = scratch[:8]
+    res_ref, grad_ref, res_other_ref, grad_other_ref, load_sems, store_sems = scratch[8:]
+    loads = [
+        pltpu.make_async_copy(source, target, load_sems.at[number])
+        for number, (source, target) in enumerate(
+            (
+                (own_in, own_ref),
+                (gown_in, gown_ref),
+                (other_in, other_ref),
+                (gother_in, gother_ref),
+            )
+        )
+    ]
     stores = [
         pltpu.make_async_copy(source, target, store_sems.at[number])
         for number, (source, target) in enumerate(
@@ -588,16 +620,23 @@
     tokens = own_ref.shape[0]
     sources = ((own_ref, gown_ref, res_ref, grad_ref), (other_ref, gother_ref, res_acc, grad_acc))
 
-    @pl.when((i == 0) & (j == 0))
+    first = (i == 0) & (j == 0)
+
+    @pl.when(first)
     def _():
-        for side, (values, grads, res, grad) in enumerate(sources):
-            at = slice(side * tokens, (side + 1) * tokens)
-            turned_ref[:, at] = turned(values[...])
-            gturned_ref[:, at] = turned(grads[...])
+        for load in loads:
+            load.start()
+        for _, _, res, grad in sources:
             res[...] = jnp.zeros_like(res)
             grad[...] = jnp.zeros_like(grad)
 
     for side, (values, grads, res, grad) in enumerate(sources):
+
+        @pl.when(first)
+        def _(side=side):
+            loads[2 * side].wait()
+            loads[2 * side + 1].wait()
+
         for m in range(tokens // chunk):
             at = slice(m * chunk, (m + 1) * chunk)
             activated, slope = gelu_and_slope(dot(values[at], win_ref[...]))
@@ -616,12 +655,17 @@
         for copy in stores:
             copy.start()
 
-    rows = turned_ref.shape[0] // nz
+    rows = own_ref.shape[1] // nz
     half = rows // 2
+
+    def both(one, two, right):
+        low, high = right[:tokens], right[tokens:]
+        return (dot(one, low, 0, 0) + dot(two, high, 0, 0)).astype(BF)
+
     for k in range(nz):
-        source = pl.ds(pl.multiple_of((z + 1 + k) % nz * rows, rows), rows)
-        gin = dot(turned_ref[source], pre_ref[...]).astype(BF)
-        gout_refs[k][0] = dot(gturned_ref[source], act_ref[...]).astype(BF)
+        at = pl.ds(pl.multiple_of((z + 1 + k) % nz * rows, rows), rows)
+        gin = both(own_ref[:, at], other_ref[:, at], pre_ref)
+        gout_refs[k][0] = both(gown_ref[:, at], gother_ref[:, at], act_ref)
         to = slice(k * half, (k + 1) * half)
         for number, ref in enumerate(up_refs):
 
@@ -665,7 +709,7 @@
         grid_spec=pltpu.PrefetchScalarGridSpec(
             num_scalar_prefetch=1,
             grid=(nx, ny),
-            in_specs=[WHOLE_SPEC] * 4
+            in_specs=[ANY_SPEC] * 4
             + [
                 pl.BlockSpec((width, part), lambda j, i, meta: (0, unit(j, i, meta))),
                 pl.BlockSpec((part, width), lambda j, i, meta: (unit(j, i, meta), 0)),
@@ -677,14 +721,17 @@
             scratch_shapes=[
                 pltpu.VMEM((total, part), BF),
                 pltpu.VMEM((total, part), BF),
-                pltpu.VMEM((width, total), BF),
-                pltpu.VMEM((width, total), BF),
+                pltpu.VMEM((tokens, width), BF),
+                pltpu.VMEM((tokens, width), BF),
+                pltpu.VMEM((tokens, width), BF),
+                pltpu.VMEM((tokens, width), BF),
                 pltpu.VMEM((tokens, width), F32),
                 pltpu.VMEM((tokens, width), F32),
                 pltpu.VMEM((tokens, width), F32),
                 pltpu.VMEM((tokens, width), F32),
                 pltpu.VMEM((tokens, width), BF),
                 pltpu.VMEM((tokens, width), BF),
+                pltpu.SemaphoreType.DMA((4,)),
                 pltpu.SemaphoreType.DMA((4,)),
             ],
         ),
@@ -906,7 +953,7 @@
         gathering.ways.meet(gathering.ways.plane())
         gathering.start()
 
-    self_forward_kernel(lengths_ref, *refs[:5], *refs[6:8], bias_ref)
+    grouped(self_forward_kernel)(lengths_ref, *refs[:5], *refs[6:8], bias_ref)
 
     @pl.when(pl.program_id(0) == pl.num_programs(0) - 1)
     def _():
@@ -921,7 +968,7 @@
     length = rows // 2
     return pl.pallas_call(
         functools.partial(self_forward_carrying, place.nz),
-        grid=(half,),
+        grid=(half // GROUP,),
         in_specs=[
             SMEM_SPEC,
             column(rows),
@@ -1369,9 +1416,6 @@
     k_copy = mail.send(k_away_ref, k_got_ref, sibling)
     v_copy = mail.send(v_away_ref, v_got_ref, sibling)
 
-    wait(out_last_ref, out_got_ref)
-    out_ref[...] = out_last_ref[...] + out_got_ref[...]
-    out_copies = [mail.send(out_ref.at[q], out_x_ref.at[q], across_x) for q in range(2)]
     feed_copies, feed_last_copies = [], {}
 
     def feed_piece(t):
@@ -1506,7 +1550,9 @@
     core_step(2)
     lower_first.append(mail.send(own_ref.at[2, :, low], first_y_ref.at[1], across_y))
     core_step(3)
-    out_step()
+    wait(out_last_ref, out_got_ref)
+    out_ref[...] = out_last_ref[...] + out_got_ref[...]
+    out_copies = [mail.send(out_ref.at[q], out_x_ref.at[q], across_x) for q in range(2)]
 
     slots = tokens // 2
     text_copy.wait_recv()
@@ -1551,7 +1597,6 @@
     vector_copy.wait_recv()
     vector_out_ref[2] = vector_out_ref[1] + vector_in_ref[1]
     vector_copy = mail.send(vector_out_ref.at[2], vector_in_ref.at[2], across_y)
-    out_last()
 
     upper_first[0].wait_recv()
     own_ref[2, :, up] = own_ref[2, :, up] + first_x_ref[0]
@@ -1573,9 +1618,9 @@
     own_ref[3, :, up] = own_ref[3, :, up] + first_x_ref[1]
     lower_first[1].wait_recv()
     own_ref[3, :, low] = own_ref[3, :, low] + first_y_ref[1]
+    out_step()
     mid_send(nz - 1)
-    for kind in range(2):
-        feed_last(kind)
+    feed_last(0)
     total = vector_out_ref[3]
     for t in range(nz - 1):
         vector_copy.wait_recv()
@@ -1585,6 +1630,8 @@
     sum_ref[...] = total
     for t in range(nz):
         qkv_send(t)
+    out_last()
+    feed_last(1)
     text_home.finish()
     frames_home.finish()
     for number, copy in enumerate(mail.sent):
@@ -1592,7 +1639,7 @@
             copy.wait_send()
 
 
-FINAL_LOADS = (18, 19, 14, 15, 16, 17, 10, 11, 12, 13, 0, 5, 6, 7, 21, 22, 4, 1, 2, 3, 20)
+FINAL_LOADS = (14, 15, 16, 17, 10, 11, 12, 13, 0, 5, 6, 7, 18, 19, 21, 22, 4, 1, 2, 3, 20)
 
 
 def final_sums(place, count, *operands):

time: 316 us -> 312 us (0.987)
  Pallas kernels: 260 us -> 255 us
where the time goes in v4:
time: 312 us; the launch traced here: 306 us
  Pallas kernels  255 us (82%)
  other arithmetic  11.9 us (4%)
  matrix products  11.6 us (4%)
  waiting for transfers between devices  11.6 us (4%)
  local copies, waits for them, and re-layouts  8.22 us (3%)
  starting transfers between devices  6.61 us (2%)
    pallas_call x1, Pallas kernels, final_sums(): pl.pallas_call(with_loads(functools.partial(final_kernel, nz), len(operan...  84.4 us
    pallas_call x3, Pallas kernels, attention_call(): pl.pallas_call(kernel, grid=(pairs // GROUP,), in_specs=in_specs, out_spe...  49 us
    pallas_call x1, Pallas kernels, feed(): pl.pallas_call(functools.partial(feed_kernel, (nx, ny, nz, chunk)), grid_...  38.6 us
    pallas_call x1, Pallas kernels, middle_parts(): pl.pallas_call(with_loads(functools.partial(middle_kernel, (nz, piece)),...  32.5 us
    pallas_call x1, Pallas kernels, entry(): pl.pallas_call(functools.partial(entry_kernel, place.nz), in_specs=[ANY_S...  26.1 us
    pallas_call x1, Pallas kernels, self_forward_and_gather(): pl.pallas_call(functools.partial(self_forward_carrying, place.nz), grid=(...  19.6 us
    ppermute x9, waiting for transfers between devices, permute(): return lax.ppermute(value, (ROWS, SEQ), pairs)  11.6 us
    dot_general x6, matrix products, dot(): lax.dot_general(left, right, (((left_dim,), (right_dim,)), ((), ())), pre...  11.6 us
  transfers between devices with their start and end apart: 9, of which 3 were waited for; matrix products, arithmetic and copies ran while one was open for 5% of the time, Pallas kernels for 12%

profile of v4, /device:TPU:0, one launch (start us, length us, event | category | flops | bytes accessed | tf_op | source)
XLA Modules:
  0.0 306.2 jit_solution(7093645341872872199)
XLA Ops:
  0.7 0.8 pad_add_fusion
  1.5 0.6 scatter.4.lengths_ref
  2.1 26.1 %shard_map.331 = (bf16[512,1024]{1,0:T(8,128)(2,1)}, bf16[512,1024]{1,0:T(8,128)(2,1)}, bf16[512,1024]{1,0:T(8,128)(2,1)}, bf16[512,2048]{1,0:T(8,128)(2,1)}, bf...) custom-call(bf16[2,256,1024]{2,1,0:T(8,128)(2,1)} %frames_ref.1, ...), custom_call_target="tpu_custom_call" | custom-call | flops 10737418240 | bytes 20971520 | tf_op jit(solution)/shard_map/pallas_call | solution.py:1100
  28.2 0.8 slice_select_fusion
  29.0 1.2 copy-done.11
  30.2 19.6 %shard_map.332 = (bf16[512,1024]{1,0:T(8,128)(2,1)S(1)}, f32[8,8,512]{2,1,0:T(8,128)S(1)}, bf16[512,1024]{1,0:T(8,128)(2,1)S(1)}) custom-call(s32[8]{0:T(128)S(1)} %fusion.3.lengths_ref.refs_0_, bf16[512,1024]{1,0:T(8,128)(2,1)S(1)} %copy-done.11, bf16[512,2048]{1,0:T(8,128)(2,1)} %get-tuple-element.94.refs_1_.refs_2_.refs_3_, ...), custom_call_target="tpu_custom_call" | custom-call | flops 5368709120 | bytes 8388608 | tf_op jit(solution)/shard_map/pallas_call | solution.py:969
  49.9 1.4 fusion.8
  51.3 0.3 multiply_reduce_fusion.5
  51.7 0.3 copy-done.23
  52.0 0.4 add_convert_fusion.1.refs_1_
  52.5 1.2 copy-done.31
  53.6 1.3 convolution_convert_fusion.1.refs_1_
  54.9 0.3 copy-done.12
  55.2 12.2 %shard_map.333 = (bf16[512,1024]{1,0:T(8,128)(2,1)S(1)}, f32[8,8,512]{2,1,0:T(8,128)S(1)}, f32[8,128]{1,0:T(8,128)}) custom-call(s32[8]{0:T(128)S(1)} %fusion.3.lengths_ref.refs_0_, bf16[512,1024]{1,0:T(8,128)(2,1)S(1)} %convolution_convert_fusion.1.refs_1_, bf16[256,2048]{1,0:T(8,128)(2,1)S(1)} %copy-done.12, bf16[256,2048]{1,0:T(8,128)(2,1)S(1)} %copy-done.12), custom_call_target="tpu_custom_call" | custom-call | flops 2147483648 | bytes 8388608 | tf_op jit(solution)/shard_map/pallas_call | solution.py:477
  67.5 1.4 fusion.9
  68.9 0.3 multiply_reduce_fusion.4
  69.3 0.3 copy-done.22
  69.6 1.5 add_convert_fusion.own_in
  71.1 0.5 collective-permute-start.1
  71.6 0.6 pad_add_fusion.1.meta_ref
  72.2 3.3 %collective-permute-done.other_in = bf16[512,1024]{1,0:T(8,128)(2,1)} collective-permute-done((bf16[512,1024]{1,0:T(8,128)(2,1)}, bf16[512,1024]{1,0:T(8,128)(2,1)}, u32[]{:S(2)}, u32[]{:S(2)}) %collective-permute-start) | collective-permute-done | bytes 1048608 | tf_op jit(solution)/shard_map/ppermute | solution.py:58
  75.5 38.6 %shard_map.334 = (f32[512,1024]{1,0:T(8,128)}, bf16[512,1024]{1,0:T(8,128)(2,1)}, f32[512,1024]{1,0:T(8,128)}, bf16[512,1024]{1,0:T(8,128)(2,1)}, bf16[2,512,512...) custom-call(s32[4]{0:T(128)} %pad_add_fusion.1.meta_ref, ...), custom_call_target="tpu_custom_call" | custom-call | flops 25769803776 | bytes 41943040 | tf_op jit(solution)/shard_map/pallas_call | solution.py:707
  114.1 0.2 collective-permute-start.2
  114.3 1.0 collective-permute-start.3
  115.3 0.6 collective-permute-start.4
  115.9 1.6 collective-permute-start.5
  117.4 2.8 multiply_reduce_fusion
  120.3 0.3 copy-done.18
  120.6 2.0 fusion.7
  122.6 1.3 convolution_convert_fusion.refs_4_
  124.0 0.3 copy-done.8
  124.2 0.3 copy-done.13
  124.5 11.5 %shard_map.335 = (bf16[512,1024]{1,0:T(8,128)(2,1)S(1)}, bf16[256,1024]{1,0:T(8,128)(2,1)S(1)}, bf16[256,1024]{1,0:T(8,128)(2,1)S(1)}, f32[8,128]{1,0:T(8,128)}) custom-call(s32[8]{0:T(128)S(1)} %fusion.3.lengths_ref.refs_0_, bf16[512,1024]{1,0:T(8,128)(2,1)S(1)} %copy-done.8, bf16[256,2048]{1,0:T(8,128)(2,1)S(1)} %copy-done.13, ...), custom_call_target="tpu_custom_call" | custom-call | flops 5368709120 | bytes 8388608 | tf_op jit(solution)/shard_map/pallas_call | solution.py:477
  136.1 4.2 %multiply_reduce_fusion.1 = (f32[1024]{0:T(1024)S(1)}, f32[512]{0:T(512)S(1)}, f32[512]{0:T(512)S(1)}, f32[1024]{0:T(1024)S(1)}, f32[512,1024]{1,0:T(8,128)S(1)}) fusion(f32[512,1024]{1,0:T(8,128)S(1)} %copy-done.16, f32[512]{0:T(512)S(1)} %add_rsqrt_fusion.1, f32[512]{0:T(512)S(1)} %broadcast_multiply_fusion.5, f32[1024]{0:T(1024)S(1)} %copy-done.23, ...), kind=kOutput, calls=%fused_computation.1 | convolution fusion | flops 1078457344 | bytes 7360512 | tf_op jit(solution)/shard_map/dot_general | solution.py:25
  140.3 2.1 convert_reduce_fusion
  142.4 2.4 fusion.6
  144.8 32.5 %shard_map.336 = (bf16[2,4,64,1536]{3,2,1,0:T(8,128)(2,1)}, bf16[2,4,64,1536]{3,2,1,0:T(8,128)(2,1)}, bf16[2,4,64,1536]{3,2,1,0:T(8,128)(2,1)}, bf16[2,4,64,1536...) custom-call(bf16[512,1024]{1,0:T(8,128)(2,1)} %copy-done.5, ...), custom_call_target="tpu_custom_call" | custom-call | flops 8589934592 | bytes 25165824 | tf_op jit(solution)/shard_map/pallas_call | solution.py:1318
  177.4 1.1 collective-permute-start.6
  178.4 1.1 collective-permute-start.7
  179.5 0.7 collective-permute-start.8
  180.2 0.7 stack.47.refs_20_
  180.8 25.3 %shard_map.337 = (bf16[512,1024]{1,0:T(8,128)(2,1)}, bf16[512,1024]{1,0:T(8,128)(2,1)}, bf16[512,1024]{1,0:T(8,128)(2,1)}, bf16[512,1024]{1,0:T(8,128)(2,1)}, bf...) custom-call(s32[8]{0:T(128)} %copy-done.3, bf16[512,1024]{1,0:T(8,128)(2,1)} %get-tuple-element.93.refs_0_.refs_1_, ...), custom_call_target="tpu_custom_call" | custom-call | flops 13421772800 | bytes 8388608 | tf_op jit(solution)/shard_map/pallas_call | solution.py:477
  206.1 7.5 %collective-permute-done.6.refs_11_ = bf16[2,4,64,1536]{3,2,1,0:T(8,128)(2,1)} collective-permute-done((bf16[2,4,64,1536]{3,2,1,0:T(8,128)(2,1)}, bf16[2,4,64,1536]{3,2,1,0:T(8,128)(2,1)}, u32[]{:S(2)}, u32[]{:S(2)}) %collective-permute-start.6) | collective-permute-done | bytes 1572896 | tf_op jit(solution)/shard_map/ppermute | solution.py:58
  213.7 0.8 collective-permute-done.7.refs_13_
  214.4 84.4 %shard_map.338 = (f32[128,768]{1,0:T(8,128)}, f32[128,1536]{1,0:T(8,128)}, f32[2,128,1024]{2,1,0:T(8,128)}, f32[8,1024]{1,0:T(8,128)}, bf16[2,256,1024]{2,1,0:T(8,128)(2,1)}, /*index=5*/bf16[2,64,768]{2,1,0:T(8,128)(2,1)}) custom-call(bf16[512,1024]{1,0:T(8,128)(2,1)} %get-tuple-element.118.refs_0_, bf16[512,1024]{1,0:T(8,128)(2,1)} %get-tuple-element.92.refs_1_, ...), custom_call_target="tpu_custom_call" | custom-call | flops 96636764160 | bytes 41943040 | tf_op jit(solution)/shard_map/pallas_call | solution.py:1657
  298.9 4.3 %shard_map.339 = (f32[2,256,1024]{2,1,0:T(8,128)}, f32[2,64,768]{2,1,0:T(8,128)}, f32[128,768]{1,0:T(8,128)}, f32[128,256]{1,0:T(8,128)}, f32[128,256]{1,0:T(8,1...) custom-call(f32[128,768]{1,0:T(8,128)} %get-tuple-element.136.qkv_re, ...), custom_call_target="tpu_custom_call" | custom-call | tf_op jit(solution)/shard_map/pallas_call | solution.py:1744
  303.2 1.5 constant_dynamic-slice_fusion.6
  304.7 1.0 copy.39
  (77 shorter events, 0.3 us)
Async XLA Ops:
  2.0 26.1 %copy-start.26 = (s32[2,4]{1,0:T(2,128)S(1)}, s32[2,4]{1,0:T(2,128)}, u32[]{:S(2)}) copy-start(s32[2,4]{1,0:T(2,128)} %param.25) | copy-start | bytes 100
  2.1 26.1 %copy-start.27 = (s32[2,4]{1,0:T(2,128)S(1)}, s32[2,4]{1,0:T(2,128)}, u32[]{:S(2)}) copy-start(s32[2,4]{1,0:T(2,128)} %param.24) | copy-start | bytes 100
  2.1 26.9 %copy-start.2 = (bf16[2,256,1024]{2,1,0:T(8,128)(2,1)S(1)}, bf16[2,256,1024]{2,1,0:T(8,128)(2,1)}, u32[]{:S(2)}) copy-start(bf16[2,256,1024]{2,1,0:T(8,128)(2,1)} %refs_5_.1) | copy-start | bytes 3145732
  29.0 95.0 %copy-start.3 = (s32[8]{0:T(128)}, s32[8]{0:T(128)S(1)}, u32[]{:S(2)}) copy-start(s32[8]{0:T(128)S(1)} %fusion.3.lengths_ref.refs_0_) | copy-start | bytes 100
  29.0 1.2 copy-start.11
  30.2 19.7 %copy-start.32 = (bf16[1024,1024]{1,0:T(8,128)(2,1)S(1)}, bf16[1024,1024]{1,0:T(8,128)(2,1)}, u32[]{:S(2)}) copy-start(bf16[1024,1024]{1,0:T(8,128)(2,1)} %refs_20_.1) | copy-start | bytes 6291460
  30.2 19.7 %copy-start.33 = (bf16[512,1024]{1,0:T(8,128)(2,1)S(1)}, bf16[512,1024]{1,0:T(8,128)(2,1)}, u32[]{:S(2)}) copy-start(bf16[512,1024]{1,0:T(8,128)(2,1)} %get-tuple-element.92.refs_1_) | copy-start | bytes 3145732
  49.8 1.4 copy-start.4
  49.8 1.4 copy-start.14
  49.8 21.2 %copy-start = (bf16[512,1024]{1,0:T(8,128)(2,1)}, bf16[512,1024]{1,0:T(8,128)(2,1)S(1)}, u32[]{:S(2)}) copy-start(bf16[512,1024]{1,0:T(8,128)(2,1)S(1)} %get-tuple-element.101.gown_in) | copy-start | bytes 3145732
  51.3 16.2 %copy-start.15 = (f32[512,1024]{1,0:T(8,128)}, f32[512,1024]{1,0:T(8,128)S(1)}, u32[]{:S(2)}) copy-start(f32[512,1024]{1,0:T(8,128)S(1)} %get-tuple-element.173) | copy-start | bytes 6291460
  51.3 0.7 copy-start.23
  51.3 0.8 copy-start.24
  51.6 2.0 copy-start.31
  53.6 1.3 copy-start.19
  53.6 1.6 copy-start.12
  54.9 12.6 %copy-start.7 = (bf16[512,1024]{1,0:T(8,128)(2,1)}, bf16[512,1024]{1,0:T(8,128)(2,1)S(1)}, u32[]{:S(2)}) copy-start(bf16[512,1024]{1,0:T(8,128)(2,1)S(1)} %convolution_convert_fusion.1.refs_1_) | copy-start | bytes 3145732
  55.2 12.3 %copy-start.29 = (bf16[1024,1024]{1,0:T(8,128)(2,1)S(1)}, bf16[1024,1024]{1,0:T(8,128)(2,1)}, u32[]{:S(2)}) copy-start(bf16[1024,1024]{1,0:T(8,128)(2,1)} %param.36) | copy-start | bytes 6291460
  67.5 1.4 copy-start.5
  68.9 0.7 copy-start.22
  68.9 0.7 copy-start.25
  71.1 4.4 %collective-permute-start = (bf16[512,1024]{1,0:T(8,128)(2,1)}, bf16[512,1024]{1,0:T(8,128)(2,1)}, u32[]{:S(2)}, u32[]{:S(2)}) collective-permute-start(bf16[512,1024]{1,0:T(8,128)(2,1)} %add_convert_fusion.own_in), channel_id=1, source_target_pairs={{0,4},{1,5},{2,6},{3,7},{4,0},{5,1},{6,2},{7,3},{8,12},{9,13},{10,... | collective-permute-start | bytes 3145736 | tf_op jit(solution)/shard_map/ppermute | solution.py:58
  71.1 4.4 %collective-permute-start.1 = (bf16[512,1024]{1,0:T(8,128)(2,1)S(1)}, bf16[512,1024]{1,0:T(8,128)(2,1)}, u32[]{:S(2)}, u32[]{:S(2)}) collective-permute-start(bf16[512,1024]{1,0:T(8,128)(2,1)S(1)} %get-tuple-element.101.gown_in), channel_id=1, source_target_pairs={{0,4},{1,5},{2,6},{3,7},{4,0},{5,1},{6,2},{7,3},{8,12},{9,13},{10,... | collective-permute-start | bytes 3145736 | tf_op jit(solution)/shard_map/ppermute | solution.py:58
  114.1 3.3 %collective-permute-start.2 = (bf16[512,1024]{1,0:T(8,128)(2,1)}, bf16[512,1024]{1,0:T(8,128)(2,1)S(1)}, u32[]{:S(2)}, u32[]{:S(2)}) collective-permute-start(bf16[512,1024]{1,0:T(8,128)(2,1)} %get-tuple-element.103), channel_id=1, source_target_pairs={{0,4},{1,5},{2,6},{3,7},{4,0},{5,1},{6,2},{7,3},{8,12},{9,13},{10,... | collective-permute-start | bytes 3145736 | tf_op jit(solution)/shard_map/ppermute | solution.py:58
  114.3 30.5 %collective-permute-start.3 = (bf16[2,512,512]{2,1,0:T(8,128)(2,1)}, bf16[2,512,512]{2,1,0:T(8,128)(2,1)}, u32[]{:S(2)}, u32[]{:S(2)}) collective-permute-start(bf16[2,512,512]{2,1,0:T(8,128)(2,1)} %get-tuple-element.111), channel_id=1, source_target_pairs={{0,1},{1,0},{2,3},{3,2},{4,5},{5,4},{6,7},{7,6},{8,9},{9,8},{10,11... | collective-permute-start | bytes 3145736 | tf_op jit(solution)/shard_map/ppermute | solution.py:58
  115.3 29.5 %collective-permute-start.4 = (bf16[2,512,512]{2,1,0:T(8,128)(2,1)}, bf16[2,512,512]{2,1,0:T(8,128)(2,1)}, u32[]{:S(2)}, u32[]{:S(2)}) collective-permute-start(bf16[2,512,512]{2,1,0:T(8,128)(2,1)} %get-tuple-element.113), channel_id=1, source_target_pairs={{0,2},{1,3},{2,0},{3,1},{4,6},{5,7},{6,4},{7,5},{8,10},{9,11},{10,... | collective-permute-start | bytes 3145736 | tf_op jit(solution)/shard_map/ppermute | solution.py:58
  115.9 29.0 %collective-permute-start.5 = (bf16[4,256,512]{2,1,0:T(8,128)(2,1)}, bf16[4,256,512]{2,1,0:T(8,128)(2,1)}, u32[]{:S(2)}, u32[]{:S(2)}) collective-permute-start(bf16[4,256,512]{2,1,0:T(8,128)(2,1)} %get-tuple-element.115), channel_id=1, source_target_pairs={{0,8},{1,9},{2,10},{3,11},{4,12},{5,13},{6,14},{7,15},{8,16},{9,17... | collective-permute-start | bytes 3145736 | tf_op jit(solution)/shard_map/ppermute | solution.py:58
  117.4 2.8 copy-start.1
  117.4 2.8 copy-start.17
  117.4 3.2 %copy-start.18 = (f32[512,1024]{1,0:T(8,128)S(1)}, f32[512,1024]{1,0:T(8,128)}, u32[]{:S(2)}) copy-start(f32[512,1024]{1,0:T(8,128)} %get-tuple-element.108) | copy-start | bytes 6291460
  120.6 2.0 copy-start.30
  122.6 1.3 copy-start.21
  122.6 1.6 copy-start.8
  122.6 1.9 copy-start.13
  124.5 11.5 %copy-start.16 = (f32[512,1024]{1,0:T(8,128)S(1)}, f32[512,1024]{1,0:T(8,128)}, u32[]{:S(2)}) copy-start(f32[512,1024]{1,0:T(8,128)} %copy-done.15) | copy-start | bytes 6291460
  136.0 4.2 %copy-start.6 = (bf16[512,1024]{1,0:T(8,128)(2,1)}, bf16[512,1024]{1,0:T(8,128)(2,1)S(1)}, u32[]{:S(2)}) copy-start(bf16[512,1024]{1,0:T(8,128)(2,1)S(1)} %get-tuple-element.105.refs_6_) | copy-start | bytes 3145732
  136.0 4.2 %copy-start.9 = (bf16[256,1024]{1,0:T(8,128)(2,1)}, bf16[256,1024]{1,0:T(8,128)(2,1)S(1)}, u32[]{:S(2)}) copy-start(bf16[256,1024]{1,0:T(8,128)(2,1)S(1)} %get-tuple-element.106.refs_7_) | copy-start | bytes 1572868
  136.0 4.2 %copy-start.10 = (bf16[256,1024]{1,0:T(8,128)(2,1)}, bf16[256,1024]{1,0:T(8,128)(2,1)S(1)}, u32[]{:S(2)}) copy-start(bf16[256,1024]{1,0:T(8,128)(2,1)S(1)} %get-tuple-element.107.refs_8_) | copy-start | bytes 1572868
  136.1 4.2 %copy-start.28 = (bf16[1024,2048]{1,0:T(8,128)(2,1)S(1)}, bf16[1024,2048]{1,0:T(8,128)(2,1)}, u32[]{:S(2)}) copy-start(bf16[1024,2048]{1,0:T(8,128)(2,1)} %kv_ref.1) | copy-start | bytes 12582916
  177.4 36.3 %collective-permute-start.6 = (bf16[2,4,64,1536]{3,2,1,0:T(8,128)(2,1)}, bf16[2,4,64,1536]{3,2,1,0:T(8,128)(2,1)}, u32[]{:S(2)}, u32[]{:S(2)}) collective-permute-start(bf16[2,4,64,1536]{3,2,1,0:T(8,128)(2,1)} %get-tuple-element.127), channel_id=1, source_target_pairs={{0,1},{1,0},{2,3},{3,2},{4,5},{5,4},{6,7},{7,6},{8,9},{9,8},{10,11... | collective-permute-start | bytes 4718600 | tf_op jit(solution)/shard_map/ppermute | solution.py:58
  178.4 36.0 %collective-permute-start.7 = (bf16[2,4,64,1536]{3,2,1,0:T(8,128)(2,1)}, bf16[2,4,64,1536]{3,2,1,0:T(8,128)(2,1)}, u32[]{:S(2)}, u32[]{:S(2)}) collective-permute-start(bf16[2,4,64,1536]{3,2,1,0:T(8,128)(2,1)} %get-tuple-element.129), channel_id=1, source_target_pairs={{0,2},{1,3},{2,0},{3,1},{4,6},{5,7},{6,4},{7,5},{8,10},{9,11},{10,... | collective-permute-start | bytes 4718600 | tf_op jit(solution)/shard_map/ppermute | solution.py:58
  179.5 26.6 %collective-permute-start.8 = (bf16[4,256,512]{2,1,0:T(8,128)(2,1)}, bf16[4,256,512]{2,1,0:T(8,128)(2,1)}, u32[]{:S(2)}, u32[]{:S(2)}) collective-permute-start(bf16[4,256,512]{2,1,0:T(8,128)(2,1)} %get-tuple-element.135), channel_id=1, source_target_pairs={{0,8},{1,9},{2,10},{3,11},{4,12},{5,13},{6,14},{7,15},{8,16},{9,17... | collective-permute-start | bytes 3145736 | tf_op jit(solution)/shard_map/ppermute | solution.py:58
  298.9 5.9 %copy-start.20 = (bf16[2,256,1024]{2,1,0:T(8,128)(2,1)S(1)}, bf16[2,256,1024]{2,1,0:T(8,128)(2,1)}, u32[]{:S(2)}) copy-start(bf16[2,256,1024]{2,1,0:T(8,128)(2,1)} %get-tuple-element.199) | copy-start | bytes 3145732

commit v5 on v4

--- a/solution.py
+++ b/solution.py
@@ -1469,17 +1469,39 @@
             if ref is away_ref:
                 core_copies.append(mail.send(away_ref.at[q], got_ref.at[q], sibling))
 
+    even_rows, odd_rows = slice(0, feed_half), slice(feed_half, 2 * feed_half)
+
+    def out_first():
+        for n in range(2):
+            out_copies.append(
+                (
+                    mail.send(out_ref.at[n, even_rows], out_x_ref.at[n], across_x),
+                    mail.send(out_ref.at[2 * n, odd_rows], out_y_ref.at[n], across_y),
+                )
+            )
+
     def out_step():
-        for q in range(2):
-            out_copies[q].wait_recv()
-            out_own_ref[q] = out_ref[2 + q] + out_x_ref[q]
-            if q == 0:
-                out_copies.append(mail.send(out_own_ref.at[0], out_y_ref, across_y))
+        for n in range(2):
+            for copy in out_copies[n]:
+                copy.wait_recv()
+            out_own_ref[0, n] = out_ref[2 + n, even_rows] + out_x_ref[n]
+            out_own_ref[1, n] = out_ref[1 + 2 * n, odd_rows] + out_y_ref[n]
+            if n == 0:
+                out_copies.append(
+                    (
+                        mail.send(out_own_ref.at[0, 0], out_x_ref.at[2], across_y),
+                        mail.send(out_own_ref.at[1, 0], out_y_ref.at[2], across_x),
+                    )
+                )
 
     def out_last():
-        out_copies[2].wait_recv()
-        total = out_own_ref[1].astype(F32) + out_y_ref[...].astype(F32)
-        feed_finish(1, total[:feed_half], total[feed_half:])
+        for copy in out_copies[2]:
+            copy.wait_recv()
+        feed_finish(
+            1,
+            out_own_ref[0, 1].astype(F32) + out_x_ref[2].astype(F32),
+            out_own_ref[1, 1].astype(F32) + out_y_ref[2].astype(F32),
+        )
 
     def feed_finish(kind, even, odd):
         away = jnp.where(core == 0, odd, even)
@@ -1552,7 +1574,8 @@
     core_step(3)
     wait(out_last_ref, out_got_ref)
     out_ref[...] = out_last_ref[...] + out_got_ref[...]
-    out_copies = [mail.send(out_ref.at[q], out_x_ref.at[q], across_x) for q in range(2)]
+    out_copies = []
+    out_first()
 
     slots = tokens // 2
     text_copy.wait_recv()
@@ -1652,7 +1675,7 @@
     half, middle = block // 2, upper.shape[3]
     feed_width = in_up.shape[1]
     feed_rows = width // nz
-    copies = 2 + 3 + nz - 1 + 2 + 2 * nz + 1 + 4 + 3 + nz - 1 + 4 + 2 * nz + 2 * (nz - 1)
+    copies = 2 + 6 + nz - 1 + 2 + 2 * nz + 1 + 4 + 3 + nz - 1 + 4 + 2 * nz + 2 * (nz - 1)
     vmem = pltpu.VMEM
     return pl.pallas_call(
         with_loads(functools.partial(final_kernel, nz), len(operands), FINAL_LOADS),
@@ -1688,9 +1711,9 @@
             vmem((nz - 1, block, piece), BF),
             vmem((nz - 1, feed_rows, feed_width), BF),
             vmem((nz - 1, feed_rows, feed_width), BF),
-            vmem((2, feed_rows, feed_width), BF),
-            vmem((2, feed_rows, feed_width), BF),
-            vmem((feed_rows, feed_width), BF),
+            vmem((3, feed_rows // 2, feed_width), BF),
+            vmem((2, 2, feed_rows // 2, feed_width), BF),
+            vmem((3, feed_rows // 2, feed_width), BF),
             vmem((2, feed_rows // 2, feed_width), F32),
             vmem((2, feed_rows // 2, feed_width), F32),
             vmem((4,) + vectors.shape, F32),

time: 312 us -> 309 us (level)
  no operation moved by 1% of the time
where the time goes in v5:
time: 309 us; the launch traced here: 304 us
  Pallas kernels  253 us (82%)
  other arithmetic  11.9 us (4%)
  matrix products  11.6 us (4%)
  waiting for transfers between devices  11.6 us (4%)
  local copies, waits for them, and re-layouts  8.22 us (3%)
  starting transfers between devices  6.61 us (2%)
    pallas_call x1, Pallas kernels, final_sums(): pl.pallas_call(with_loads(functools.partial(final_kernel, nz), len(operan...  82.5 us
    pallas_call x3, Pallas kernels, attention_call(): pl.pallas_call(kernel, grid=(pairs // GROUP,), in_specs=in_specs, out_spe...  49 us
    pallas_call x1, Pallas kernels, feed(): pl.pallas_call(functools.partial(feed_kernel, (nx, ny, nz, chunk)), grid_...  38.6 us
    pallas_call x1, Pallas kernels, middle_parts(): pl.pallas_call(with_loads(functools.partial(middle_kernel, (nz, piece)),...  32.5 us
    pallas_call x1, Pallas kernels, entry(): pl.pallas_call(functools.partial(entry_kernel, place.nz), in_specs=[ANY_S...  26.1 us
    pallas_call x1, Pallas kernels, self_forward_and_gather(): pl.pallas_call(functools.partial(self_forward_carrying, place.nz), grid=(...  19.6 us
    ppermute x9, waiting for transfers between devices, permute(): return lax.ppermute(value, (ROWS, SEQ), pairs)  11.6 us
    dot_general x6, matrix products, dot(): lax.dot_general(left, right, (((left_dim,), (right_dim,)), ((), ())), pre...  11.6 us
  transfers between devices with their start and end apart: 9, of which 3 were waited for; matrix products, arithmetic and copies ran while one was open for 5% of the time, Pallas kernels for 12%

profile of v5, /device:TPU:0, one launch (start us, length us, event | category | flops | bytes accessed | tf_op | source)
XLA Modules:
  0.0 304.2 jit_solution(18086088239484519532)
XLA Ops:
  0.7 0.8 pad_add_fusion
  1.5 0.6 scatter.4.lengths_ref
  2.1 26.1 %shard_map.331 = (bf16[512,1024]{1,0:T(8,128)(2,1)}, bf16[512,1024]{1,0:T(8,128)(2,1)}, bf16[512,1024]{1,0:T(8,128)(2,1)}, bf16[512,2048]{1,0:T(8,128)(2,1)}, bf...) custom-call(bf16[2,256,1024]{2,1,0:T(8,128)(2,1)} %frames_ref.1, ...), custom_call_target="tpu_custom_call" | custom-call | flops 10737418240 | bytes 20971520 | tf_op jit(solution)/shard_map/pallas_call | solution.py:1100
  28.2 0.8 slice_select_fusion
  29.0 1.2 copy-done.11
  30.2 19.6 %shard_map.332 = (bf16[512,1024]{1,0:T(8,128)(2,1)S(1)}, f32[8,8,512]{2,1,0:T(8,128)S(1)}, bf16[512,1024]{1,0:T(8,128)(2,1)S(1)}) custom-call(s32[8]{0:T(128)S(1)} %fusion.3.lengths_ref.refs_0_, bf16[512,1024]{1,0:T(8,128)(2,1)S(1)} %copy-done.11, bf16[512,2048]{1,0:T(8,128)(2,1)} %get-tuple-element.94.refs_1_.refs_2_.refs_3_, ...), custom_call_target="tpu_custom_call" | custom-call | flops 5368709120 | bytes 8388608 | tf_op jit(solution)/shard_map/pallas_call | solution.py:969
  49.9 1.4 fusion.8
  51.3 0.3 multiply_reduce_fusion.5
  51.7 0.3 copy-done.23
  52.0 0.4 add_convert_fusion.1.refs_1_
  52.5 1.2 copy-done.31
  53.6 1.3 convolution_convert_fusion.1.refs_1_
  54.9 0.3 copy-done.12
  55.2 12.2 %shard_map.333 = (bf16[512,1024]{1,0:T(8,128)(2,1)S(1)}, f32[8,8,512]{2,1,0:T(8,128)S(1)}, f32[8,128]{1,0:T(8,128)}) custom-call(s32[8]{0:T(128)S(1)} %fusion.3.lengths_ref.refs_0_, bf16[512,1024]{1,0:T(8,128)(2,1)S(1)} %convolution_convert_fusion.1.refs_1_, bf16[256,2048]{1,0:T(8,128)(2,1)S(1)} %copy-done.12, bf16[256,2048]{1,0:T(8,128)(2,1)S(1)} %copy-done.12), custom_call_target="tpu_custom_call" | custom-call | flops 2147483648 | bytes 8388608 | tf_op jit(solution)/shard_map/pallas_call | solution.py:477
  67.5 1.4 fusion.9
  68.9 0.3 multiply_reduce_fusion.4
  69.3 0.3 copy-done.22
  69.6 1.5 add_convert_fusion.own_in
  71.1 0.5 collective-permute-start.1
  71.6 0.6 pad_add_fusion.1.meta_ref
  72.2 3.3 %collective-permute-done.other_in = bf16[512,1024]{1,0:T(8,128)(2,1)} collective-permute-done((bf16[512,1024]{1,0:T(8,128)(2,1)}, bf16[512,1024]{1,0:T(8,128)(2,1)}, u32[]{:S(2)}, u32[]{:S(2)}) %collective-permute-start) | collective-permute-done | bytes 1048608 | tf_op jit(solution)/shard_map/ppermute | solution.py:58
  75.5 38.6 %shard_map.334 = (f32[512,1024]{1,0:T(8,128)}, bf16[512,1024]{1,0:T(8,128)(2,1)}, f32[512,1024]{1,0:T(8,128)}, bf16[512,1024]{1,0:T(8,128)(2,1)}, bf16[2,512,512...) custom-call(s32[4]{0:T(128)} %pad_add_fusion.1.meta_ref, ...), custom_call_target="tpu_custom_call" | custom-call | flops 25769803776 | bytes 41943040 | tf_op jit(solution)/shard_map/pallas_call | solution.py:707
  114.1 0.2 collective-permute-start.2
  114.3 1.0 collective-permute-start.3
  115.3 0.6 collective-permute-start.4
  115.9 1.6 collective-permute-start.5
  117.4 2.8 multiply_reduce_fusion
  120.3 0.3 copy-done.18
  120.6 2.0 fusion.7
  122.6 1.3 convolution_convert_fusion.refs_4_
  124.0 0.3 copy-done.8
  124.2 0.3 copy-done.13
  124.5 11.5 %shard_map.335 = (bf16[512,1024]{1,0:T(8,128)(2,1)S(1)}, bf16[256,1024]{1,0:T(8,128)(2,1)S(1)}, bf16[256,1024]{1,0:T(8,128)(2,1)S(1)}, f32[8,128]{1,0:T(8,128)}) custom-call(s32[8]{0:T(128)S(1)} %fusion.3.lengths_ref.refs_0_, bf16[512,1024]{1,0:T(8,128)(2,1)S(1)} %copy-done.8, bf16[256,2048]{1,0:T(8,128)(2,1)S(1)} %copy-done.13, ...), custom_call_target="tpu_custom_call" | custom-call | flops 5368709120 | bytes 8388608 | tf_op jit(solution)/shard_map/pallas_call | solution.py:477
  136.1 4.2 %multiply_reduce_fusion.1 = (f32[1024]{0:T(1024)S(1)}, f32[512]{0:T(512)S(1)}, f32[512]{0:T(512)S(1)}, f32[1024]{0:T(1024)S(1)}, f32[512,1024]{1,0:T(8,128)S(1)}) fusion(f32[512,1024]{1,0:T(8,128)S(1)} %copy-done.16, f32[512]{0:T(512)S(1)} %add_rsqrt_fusion.1, f32[512]{0:T(512)S(1)} %broadcast_multiply_fusion.5, f32[1024]{0:T(1024)S(1)} %copy-done.23, ...), kind=kOutput, calls=%fused_computation.1 | convolution fusion | flops 1078457344 | bytes 7360512 | tf_op jit(solution)/shard_map/dot_general | solution.py:25
  140.3 2.1 convert_reduce_fusion
  142.4 2.4 fusion.6
  144.8 32.5 %shard_map.336 = (bf16[2,4,64,1536]{3,2,1,0:T(8,128)(2,1)}, bf16[2,4,64,1536]{3,2,1,0:T(8,128)(2,1)}, bf16[2,4,64,1536]{3,2,1,0:T(8,128)(2,1)}, bf16[2,4,64,1536...) custom-call(bf16[512,1024]{1,0:T(8,128)(2,1)} %copy-done.5, ...), custom_call_target="tpu_custom_call" | custom-call | flops 8589934592 | bytes 25165824 | tf_op jit(solution)/shard_map/pallas_call | solution.py:1318
  177.4 1.1 collective-permute-start.6
  178.4 1.1 collective-permute-start.7
  179.5 0.7 collective-permute-start.8
  180.2 0.7 stack.47.refs_20_
  180.8 25.3 %shard_map.337 = (bf16[512,1024]{1,0:T(8,128)(2,1)}, bf16[512,1024]{1,0:T(8,128)(2,1)}, bf16[512,1024]{1,0:T(8,128)(2,1)}, bf16[512,1024]{1,0:T(8,128)(2,1)}, bf...) custom-call(s32[8]{0:T(128)} %copy-done.3, bf16[512,1024]{1,0:T(8,128)(2,1)} %get-tuple-element.93.refs_0_.refs_1_, ...), custom_call_target="tpu_custom_call" | custom-call | flops 13421772800 | bytes 8388608 | tf_op jit(solution)/shard_map/pallas_call | solution.py:477
  206.1 7.5 %collective-permute-done.6.refs_11_ = bf16[2,4,64,1536]{3,2,1,0:T(8,128)(2,1)} collective-permute-done((bf16[2,4,64,1536]{3,2,1,0:T(8,128)(2,1)}, bf16[2,4,64,1536]{3,2,1,0:T(8,128)(2,1)}, u32[]{:S(2)}, u32[]{:S(2)}) %collective-permute-start.6) | collective-permute-done | bytes 1572896 | tf_op jit(solution)/shard_map/ppermute | solution.py:58
  213.7 0.8 collective-permute-done.7.refs_13_
  214.4 82.5 %shard_map.338 = (f32[128,768]{1,0:T(8,128)}, f32[128,1536]{1,0:T(8,128)}, f32[2,128,1024]{2,1,0:T(8,128)}, f32[8,1024]{1,0:T(8,128)}, bf16[2,256,1024]{2,1,0:T(8,128)(2,1)}, /*index=5*/bf16[2,64,768]{2,1,0:T(8,128)(2,1)}) custom-call(bf16[512,1024]{1,0:T(8,128)(2,1)} %get-tuple-element.118.refs_0_, bf16[512,1024]{1,0:T(8,128)(2,1)} %get-tuple-element.92.refs_1_, ...), custom_call_target="tpu_custom_call" | custom-call | flops 96636764160 | bytes 41943040 | tf_op jit(solution)/shard_map/pallas_call | solution.py:1680
  296.9 4.3 %shard_map.339 = (f32[2,256,1024]{2,1,0:T(8,128)}, f32[2,64,768]{2,1,0:T(8,128)}, f32[128,768]{1,0:T(8,128)}, f32[128,256]{1,0:T(8,128)}, f32[128,256]{1,0:T(8,1...) custom-call(f32[128,768]{1,0:T(8,128)} %get-tuple-element.136.qkv_re, ...), custom_call_target="tpu_custom_call" | custom-call | tf_op jit(solution)/shard_map/pallas_call | solution.py:1767
  301.3 1.5 constant_dynamic-slice_fusion.6
  302.8 1.0 copy.39
  (77 shorter events, 0.3 us)
Async XLA Ops:
  2.0 26.1 %copy-start.26 = (s32[2,4]{1,0:T(2,128)S(1)}, s32[2,4]{1,0:T(2,128)}, u32[]{:S(2)}) copy-start(s32[2,4]{1,0:T(2,128)} %param.25) | copy-start | bytes 100
  2.1 26.1 %copy-start.27 = (s32[2,4]{1,0:T(2,128)S(1)}, s32[2,4]{1,0:T(2,128)}, u32[]{:S(2)}) copy-start(s32[2,4]{1,0:T(2,128)} %param.24) | copy-start | bytes 100
  2.1 26.9 %copy-start.2 = (bf16[2,256,1024]{2,1,0:T(8,128)(2,1)S(1)}, bf16[2,256,1024]{2,1,0:T(8,128)(2,1)}, u32[]{:S(2)}) copy-start(bf16[2,256,1024]{2,1,0:T(8,128)(2,1)} %refs_5_.1) | copy-start | bytes 3145732
  29.0 95.0 %copy-start.3 = (s32[8]{0:T(128)}, s32[8]{0:T(128)S(1)}, u32[]{:S(2)}) copy-start(s32[8]{0:T(128)S(1)} %fusion.3.lengths_ref.refs_0_) | copy-start | bytes 100
  29.0 1.2 copy-start.11
  30.2 19.7 %copy-start.32 = (bf16[1024,1024]{1,0:T(8,128)(2,1)S(1)}, bf16[1024,1024]{1,0:T(8,128)(2,1)}, u32[]{:S(2)}) copy-start(bf16[1024,1024]{1,0:T(8,128)(2,1)} %refs_20_.1) | copy-start | bytes 6291460
  30.2 19.7 %copy-start.33 = (bf16[512,1024]{1,0:T(8,128)(2,1)S(1)}, bf16[512,1024]{1,0:T(8,128)(2,1)}, u32[]{:S(2)}) copy-start(bf16[512,1024]{1,0:T(8,128)(2,1)} %get-tuple-element.92.refs_1_) | copy-start | bytes 3145732
  49.8 1.4 copy-start.4
  49.8 1.4 copy-start.14
  49.8 21.2 %copy-start = (bf16[512,1024]{1,0:T(8,128)(2,1)}, bf16[512,1024]{1,0:T(8,128)(2,1)S(1)}, u32[]{:S(2)}) copy-start(bf16[512,1024]{1,0:T(8,128)(2,1)S(1)} %get-tuple-element.101.gown_in) | copy-start | bytes 3145732
  51.3 16.2 %copy-start.15 = (f32[512,1024]{1,0:T(8,128)}, f32[512,1024]{1,0:T(8,128)S(1)}, u32[]{:S(2)}) copy-start(f32[512,1024]{1,0:T(8,128)S(1)} %get-tuple-element.173) | copy-start | bytes 6291460
  51.3 0.7 copy-start.23
  51.3 0.8 copy-start.24
  51.6 2.0 copy-start.31
  53.6 1.3 copy-start.19
  53.6 1.6 copy-start.12
  54.9 12.6 %copy-start.7 = (bf16[512,1024]{1,0:T(8,128)(2,1)}, bf16[512,1024]{1,0:T(8,128)(2,1)S(1)}, u32[]{:S(2)}) copy-start(bf16[512,1024]{1,0:T(8,128)(2,1)S(1)} %convolution_convert_fusion.1.refs_1_) | copy-start | bytes 3145732
  55.2 12.3 %copy-start.29 = (bf16[1024,1024]{1,0:T(8,128)(2,1)S(1)}, bf16[1024,1024]{1,0:T(8,128)(2,1)}, u32[]{:S(2)}) copy-start(bf16[1024,1024]{1,0:T(8,128)(2,1)} %param.36) | copy-start | bytes 6291460
  67.5 1.4 copy-start.5
  68.9 0.7 copy-start.22
  68.9 0.7 copy-start.25
  71.1 4.4 %collective-permute-start = (bf16[512,1024]{1,0:T(8,128)(2,1)}, bf16[512,1024]{1,0:T(8,128)(2,1)}, u32[]{:S(2)}, u32[]{:S(2)}) collective-permute-start(bf16[512,1024]{1,0:T(8,128)(2,1)} %add_convert_fusion.own_in), channel_id=1, source_target_pairs={{0,4},{1,5},{2,6},{3,7},{4,0},{5,1},{6,2},{7,3},{8,12},{9,13},{10,... | collective-permute-start | bytes 3145736 | tf_op jit(solution)/shard_map/ppermute | solution.py:58
  71.1 4.4 %collective-permute-start.1 = (bf16[512,1024]{1,0:T(8,128)(2,1)S(1)}, bf16[512,1024]{1,0:T(8,128)(2,1)}, u32[]{:S(2)}, u32[]{:S(2)}) collective-permute-start(bf16[512,1024]{1,0:T(8,128)(2,1)S(1)} %get-tuple-element.101.gown_in), channel_id=1, source_target_pairs={{0,4},{1,5},{2,6},{3,7},{4,0},{5,1},{6,2},{7,3},{8,12},{9,13},{10,... | collective-permute-start | bytes 3145736 | tf_op jit(solution)/shard_map/ppermute | solution.py:58
  114.1 3.3 %collective-permute-start.2 = (bf16[512,1024]{1,0:T(8,128)(2,1)}, bf16[512,1024]{1,0:T(8,128)(2,1)S(1)}, u32[]{:S(2)}, u32[]{:S(2)}) collective-permute-start(bf16[512,1024]{1,0:T(8,128)(2,1)} %get-tuple-element.103), channel_id=1, source_target_pairs={{0,4},{1,5},{2,6},{3,7},{4,0},{5,1},{6,2},{7,3},{8,12},{9,13},{10,... | collective-permute-start | bytes 3145736 | tf_op jit(solution)/shard_map/ppermute | solution.py:58
  114.3 30.5 %collective-permute-start.3 = (bf16[2,512,512]{2,1,0:T(8,128)(2,1)}, bf16[2,512,512]{2,1,0:T(8,128)(2,1)}, u32[]{:S(2)}, u32[]{:S(2)}) collective-permute-start(bf16[2,512,512]{2,1,0:T(8,128)(2,1)} %get-tuple-element.111), channel_id=1, source_target_pairs={{0,1},{1,0},{2,3},{3,2},{4,5},{5,4},{6,7},{7,6},{8,9},{9,8},{10,11... | collective-permute-start | bytes 3145736 | tf_op jit(solution)/shard_map/ppermute | solution.py:58
  115.3 29.5 %collective-permute-start.4 = (bf16[2,512,512]{2,1,0:T(8,128)(2,1)}, bf16[2,512,512]{2,1,0:T(8,128)(2,1)}, u32[]{:S(2)}, u32[]{:S(2)}) collective-permute-start(bf16[2,512,512]{2,1,0:T(8,128)(2,1)} %get-tuple-element.113), channel_id=1, source_target_pairs={{0,2},{1,3},{2,0},{3,1},{4,6},{5,7},{6,4},{7,5},{8,10},{9,11},{10,... | collective-permute-start | bytes 3145736 | tf_op jit(solution)/shard_map/ppermute | solution.py:58
  115.9 29.0 %collective-permute-start.5 = (bf16[4,256,512]{2,1,0:T(8,128)(2,1)}, bf16[4,256,512]{2,1,0:T(8,128)(2,1)}, u32[]{:S(2)}, u32[]{:S(2)}) collective-permute-start(bf16[4,256,512]{2,1,0:T(8,128)(2,1)} %get-tuple-element.115), channel_id=1, source_target_pairs={{0,8},{1,9},{2,10},{3,11},{4,12},{5,13},{6,14},{7,15},{8,16},{9,17... | collective-permute-start | bytes 3145736 | tf_op jit(solution)/shard_map/ppermute | solution.py:58
  117.4 2.8 copy-start.1
  117.4 2.8 copy-start.17
  117.4 3.2 %copy-start.18 = (f32[512,1024]{1,0:T(8,128)S(1)}, f32[512,1024]{1,0:T(8,128)}, u32[]{:S(2)}) copy-start(f32[512,1024]{1,0:T(8,128)} %get-tuple-element.108) | copy-start | bytes 6291460
  120.6 2.0 copy-start.30
  122.6 1.3 copy-start.21
  122.6 1.6 copy-start.8
  122.6 1.9 copy-start.13
  124.5 11.5 %copy-start.16 = (f32[512,1024]{1,0:T(8,128)S(1)}, f32[512,1024]{1,0:T(8,128)}, u32[]{:S(2)}) copy-start(f32[512,1024]{1,0:T(8,128)} %copy-done.15) | copy-start | bytes 6291460
  136.0 4.2 %copy-start.6 = (bf16[512,1024]{1,0:T(8,128)(2,1)}, bf16[512,1024]{1,0:T(8,128)(2,1)S(1)}, u32[]{:S(2)}) copy-start(bf16[512,1024]{1,0:T(8,128)(2,1)S(1)} %get-tuple-element.105.refs_6_) | copy-start | bytes 3145732
  136.0 4.2 %copy-start.9 = (bf16[256,1024]{1,0:T(8,128)(2,1)}, bf16[256,1024]{1,0:T(8,128)(2,1)S(1)}, u32[]{:S(2)}) copy-start(bf16[256,1024]{1,0:T(8,128)(2,1)S(1)} %get-tuple-element.106.refs_7_) | copy-start | bytes 1572868
  136.0 4.2 %copy-start.10 = (bf16[256,1024]{1,0:T(8,128)(2,1)}, bf16[256,1024]{1,0:T(8,128)(2,1)S(1)}, u32[]{:S(2)}) copy-start(bf16[256,1024]{1,0:T(8,128)(2,1)S(1)} %get-tuple-element.107.refs_8_) | copy-start | bytes 1572868
  136.1 4.2 %copy-start.28 = (bf16[1024,2048]{1,0:T(8,128)(2,1)S(1)}, bf16[1024,2048]{1,0:T(8,128)(2,1)}, u32[]{:S(2)}) copy-start(bf16[1024,2048]{1,0:T(8,128)(2,1)} %kv_ref.1) | copy-start | bytes 12582916
  177.4 36.3 %collective-permute-start.6 = (bf16[2,4,64,1536]{3,2,1,0:T(8,128)(2,1)}, bf16[2,4,64,1536]{3,2,1,0:T(8,128)(2,1)}, u32[]{:S(2)}, u32[]{:S(2)}) collective-permute-start(bf16[2,4,64,1536]{3,2,1,0:T(8,128)(2,1)} %get-tuple-element.127), channel_id=1, source_target_pairs={{0,1},{1,0},{2,3},{3,2},{4,5},{5,4},{6,7},{7,6},{8,9},{9,8},{10,11... | collective-permute-start | bytes 4718600 | tf_op jit(solution)/shard_map/ppermute | solution.py:58
  178.4 36.0 %collective-permute-start.7 = (bf16[2,4,64,1536]{3,2,1,0:T(8,128)(2,1)}, bf16[2,4,64,1536]{3,2,1,0:T(8,128)(2,1)}, u32[]{:S(2)}, u32[]{:S(2)}) collective-permute-start(bf16[2,4,64,1536]{3,2,1,0:T(8,128)(2,1)} %get-tuple-element.129), channel_id=1, source_target_pairs={{0,2},{1,3},{2,0},{3,1},{4,6},{5,7},{6,4},{7,5},{8,10},{9,11},{10,... | collective-permute-start | bytes 4718600 | tf_op jit(solution)/shard_map/ppermute | solution.py:58
  179.5 26.6 %collective-permute-start.8 = (bf16[4,256,512]{2,1,0:T(8,128)(2,1)}, bf16[4,256,512]{2,1,0:T(8,128)(2,1)}, u32[]{:S(2)}, u32[]{:S(2)}) collective-permute-start(bf16[4,256,512]{2,1,0:T(8,128)(2,1)} %get-tuple-element.135), channel_id=1, source_target_pairs={{0,8},{1,9},{2,10},{3,11},{4,12},{5,13},{6,14},{7,15},{8,16},{9,17... | collective-permute-start | bytes 3145736 | tf_op jit(solution)/shard_map/ppermute | solution.py:58
  296.9 5.9 %copy-start.20 = (bf16[2,256,1024]{2,1,0:T(8,128)(2,1)S(1)}, bf16[2,256,1024]{2,1,0:T(8,128)(2,1)}, u32[]{:S(2)}) copy-start(bf16[2,256,1024]{2,1,0:T(8,128)(2,1)} %get-tuple-element.199) | copy-start | bytes 3145732

commit v6 on v5

--- a/solution.py
+++ b/solution.py
@@ -408,7 +408,7 @@
     dv_ref[...] = sums[1].astype(BF)
 
 
-GROUP = 2
+GROUP = 4
 
 
 def column(rows, first=0):

time: 309 us -> 308 us (level)
  no operation moved by 1% of the time
where the time goes in v6:
time: 308 us; the launch traced here: 303 us
  Pallas kernels  252 us (82%)
  other arithmetic  12.1 us (4%)
  matrix products  11.6 us (4%)
  waiting for transfers between devices  10.8 us (4%)
  local copies, waits for them, and re-layouts  8.22 us (3%)
  starting transfers between devices  6.64 us (2%)
    pallas_call x1, Pallas kernels, final_sums(): pl.pallas_call(with_loads(functools.partial(final_kernel, nz), len(operan...  82.2 us
    pallas_call x3, Pallas kernels, attention_call(): pl.pallas_call(kernel, grid=(pairs // GROUP,), in_specs=in_specs, out_spe...  48.3 us
    pallas_call x1, Pallas kernels, feed(): pl.pallas_call(functools.partial(feed_kernel, (nx, ny, nz, chunk)), grid_...  39.1 us
    pallas_call x1, Pallas kernels, middle_parts(): pl.pallas_call(with_loads(functools.partial(middle_kernel, (nz, piece)),...  32.5 us
    pallas_call x1, Pallas kernels, entry(): pl.pallas_call(functools.partial(entry_kernel, place.nz), in_specs=[ANY_S...  26.1 us
    pallas_call x1, Pallas kernels, self_forward_and_gather(): pl.pallas_call(functools.partial(self_forward_carrying, place.nz), grid=(...  19.9 us
    dot_general x6, matrix products, dot(): lax.dot_general(left, right, (((left_dim,), (right_dim,)), ((), ())), pre...  11.6 us
    ppermute x9, waiting for transfers between devices, permute(): return lax.ppermute(value, (ROWS, SEQ), pairs)  10.8 us
  transfers between devices with their start and end apart: 9, of which 3 were waited for; matrix products, arithmetic and copies ran while one was open for 5% of the time, Pallas kernels for 12%

profile of v6, /device:TPU:0, one launch (start us, length us, event | category | flops | bytes accessed | tf_op | source)
XLA Modules:
  0.0 303.3 jit_solution(4913673380715103629)
XLA Ops:
  0.7 0.8 pad_add_fusion
  1.5 0.6 scatter.4.lengths_ref
  2.1 26.1 %shard_map.331 = (bf16[512,1024]{1,0:T(8,128)(2,1)}, bf16[512,1024]{1,0:T(8,128)(2,1)}, bf16[512,1024]{1,0:T(8,128)(2,1)}, bf16[512,2048]{1,0:T(8,128)(2,1)}, bf...) custom-call(bf16[2,256,1024]{2,1,0:T(8,128)(2,1)} %frames_ref.1, ...), custom_call_target="tpu_custom_call" | custom-call | flops 10737418240 | bytes 20971520 | tf_op jit(solution)/shard_map/pallas_call | solution.py:1100
  28.2 0.8 slice_select_fusion
  29.0 1.2 copy-done.11
  30.2 19.9 %shard_map.332 = (bf16[512,1024]{1,0:T(8,128)(2,1)S(1)}, f32[8,8,512]{2,1,0:T(8,128)S(1)}, bf16[512,1024]{1,0:T(8,128)(2,1)S(1)}) custom-call(s32[8]{0:T(128)S(1)} %fusion.3.lengths_ref.refs_0_, bf16[512,1024]{1,0:T(8,128)(2,1)S(1)} %copy-done.11, bf16[512,2048]{1,0:T(8,128)(2,1)} %get-tuple-element.94.refs_1_.refs_2_.refs_3_, ...), custom_call_target="tpu_custom_call" | custom-call | flops 5368709120 | bytes 8388608 | tf_op jit(solution)/shard_map/pallas_call | solution.py:969
  50.2 1.4 fusion.8
  51.6 0.3 multiply_reduce_fusion.5
  52.0 0.3 copy-done.23
  52.4 0.4 add_convert_fusion.1.refs_1_
  52.8 1.2 copy-done.31
  53.9 1.3 convolution_convert_fusion.1.refs_1_
  55.2 0.3 copy-done.12
  55.5 11.2 %shard_map.333 = (bf16[512,1024]{1,0:T(8,128)(2,1)S(1)}, f32[8,8,512]{2,1,0:T(8,128)S(1)}, f32[8,128]{1,0:T(8,128)}) custom-call(s32[8]{0:T(128)S(1)} %fusion.3.lengths_ref.refs_0_, bf16[512,1024]{1,0:T(8,128)(2,1)S(1)} %convolution_convert_fusion.1.refs_1_, bf16[256,2048]{1,0:T(8,128)(2,1)S(1)} %copy-done.12, bf16[256,2048]{1,0:T(8,128)(2,1)S(1)} %copy-done.12), custom_call_target="tpu_custom_call" | custom-call | flops 2147483648 | bytes 8388608 | tf_op jit(solution)/shard_map/pallas_call | solution.py:477
  66.7 1.4 fusion.9
  68.1 0.3 multiply_reduce_fusion.4
  68.5 0.3 copy-done.22
  68.8 1.5 add_convert_fusion.own_in
  70.3 0.5 collective-permute-start.1
  70.8 0.6 pad_add_fusion.1.meta_ref
  71.4 3.3 %collective-permute-done.other_in = bf16[512,1024]{1,0:T(8,128)(2,1)} collective-permute-done((bf16[512,1024]{1,0:T(8,128)(2,1)}, bf16[512,1024]{1,0:T(8,128)(2,1)}, u32[]{:S(2)}, u32[]{:S(2)}) %collective-permute-start) | collective-permute-done | bytes 1048608 | tf_op jit(solution)/shard_map/ppermute | solution.py:58
  74.7 39.1 %shard_map.334 = (f32[512,1024]{1,0:T(8,128)}, bf16[512,1024]{1,0:T(8,128)(2,1)}, f32[512,1024]{1,0:T(8,128)}, bf16[512,1024]{1,0:T(8,128)(2,1)}, bf16[2,512,512...) custom-call(s32[4]{0:T(128)} %pad_add_fusion.1.meta_ref, ...), custom_call_target="tpu_custom_call" | custom-call | flops 25769803776 | bytes 41943040 | tf_op jit(solution)/shard_map/pallas_call | solution.py:707
  113.8 0.2 collective-permute-start.2
  114.0 1.0 collective-permute-start.3
  115.0 0.6 collective-permute-start.4
  115.6 1.6 collective-permute-start.5
  117.1 2.8 multiply_reduce_fusion
  120.0 0.3 copy-done.18
  120.3 2.2 fusion.7
  122.5 1.3 convolution_convert_fusion.refs_4_
  123.8 0.3 copy-done.8
  124.1 0.3 copy-done.13
  124.4 11.0 %shard_map.335 = (bf16[512,1024]{1,0:T(8,128)(2,1)S(1)}, bf16[256,1024]{1,0:T(8,128)(2,1)S(1)}, bf16[256,1024]{1,0:T(8,128)(2,1)S(1)}, f32[8,128]{1,0:T(8,128)}) custom-call(s32[8]{0:T(128)S(1)} %fusion.3.lengths_ref.refs_0_, bf16[512,1024]{1,0:T(8,128)(2,1)S(1)} %copy-done.8, bf16[256,2048]{1,0:T(8,128)(2,1)S(1)} %copy-done.13, ...), custom_call_target="tpu_custom_call" | custom-call | flops 5368709120 | bytes 8388608 | tf_op jit(solution)/shard_map/pallas_call | solution.py:477
  135.5 4.2 %multiply_reduce_fusion.1 = (f32[1024]{0:T(1024)S(1)}, f32[512]{0:T(512)S(1)}, f32[512]{0:T(512)S(1)}, f32[1024]{0:T(1024)S(1)}, f32[512,1024]{1,0:T(8,128)S(1)}) fusion(f32[512,1024]{1,0:T(8,128)S(1)} %copy-done.16, f32[512]{0:T(512)S(1)} %add_rsqrt_fusion.1, f32[512]{0:T(512)S(1)} %broadcast_multiply_fusion.5, f32[1024]{0:T(1024)S(1)} %copy-done.23, ...), kind=kOutput, calls=%fused_computation.1 | convolution fusion | flops 1078457344 | bytes 7360512 | tf_op jit(solution)/shard_map/dot_general | solution.py:25
  139.7 2.1 convert_reduce_fusion
  141.8 2.4 fusion.6
  144.2 32.5 %shard_map.336 = (bf16[2,4,64,1536]{3,2,1,0:T(8,128)(2,1)}, bf16[2,4,64,1536]{3,2,1,0:T(8,128)(2,1)}, bf16[2,4,64,1536]{3,2,1,0:T(8,128)(2,1)}, bf16[2,4,64,1536...) custom-call(bf16[512,1024]{1,0:T(8,128)(2,1)} %copy-done.5, ...), custom_call_target="tpu_custom_call" | custom-call | flops 8589934592 | bytes 25165824 | tf_op jit(solution)/shard_map/pallas_call | solution.py:1318
  176.7 1.1 collective-permute-start.6
  177.8 1.0 collective-permute-start.7
  178.8 0.7 collective-permute-start.8
  179.5 0.7 stack.47.refs_20_
  180.2 26.2 %shard_map.337 = (bf16[512,1024]{1,0:T(8,128)(2,1)}, bf16[512,1024]{1,0:T(8,128)(2,1)}, bf16[512,1024]{1,0:T(8,128)(2,1)}, bf16[512,1024]{1,0:T(8,128)(2,1)}, bf...) custom-call(s32[8]{0:T(128)} %copy-done.3, bf16[512,1024]{1,0:T(8,128)(2,1)} %get-tuple-element.93.refs_0_.refs_1_, ...), custom_call_target="tpu_custom_call" | custom-call | flops 13421772800 | bytes 8388608 | tf_op jit(solution)/shard_map/pallas_call | solution.py:477
  206.4 6.7 %collective-permute-done.6.refs_11_ = bf16[2,4,64,1536]{3,2,1,0:T(8,128)(2,1)} collective-permute-done((bf16[2,4,64,1536]{3,2,1,0:T(8,128)(2,1)}, bf16[2,4,64,1536]{3,2,1,0:T(8,128)(2,1)}, u32[]{:S(2)}, u32[]{:S(2)}) %collective-permute-start.6) | collective-permute-done | bytes 1572896 | tf_op jit(solution)/shard_map/ppermute | solution.py:58
  213.1 0.7 collective-permute-done.7.refs_13_
  213.8 82.2 %shard_map.338 = (f32[128,768]{1,0:T(8,128)}, f32[128,1536]{1,0:T(8,128)}, f32[2,128,1024]{2,1,0:T(8,128)}, f32[8,1024]{1,0:T(8,128)}, bf16[2,256,1024]{2,1,0:T(8,128)(2,1)}, /*index=5*/bf16[2,64,768]{2,1,0:T(8,128)(2,1)}) custom-call(bf16[512,1024]{1,0:T(8,128)(2,1)} %get-tuple-element.118.refs_0_, bf16[512,1024]{1,0:T(8,128)(2,1)} %get-tuple-element.92.refs_1_, ...), custom_call_target="tpu_custom_call" | custom-call | flops 96636764160 | bytes 41943040 | tf_op jit(solution)/shard_map/pallas_call | solution.py:1680
  296.0 4.3 %shard_map.339 = (f32[2,256,1024]{2,1,0:T(8,128)}, f32[2,64,768]{2,1,0:T(8,128)}, f32[128,768]{1,0:T(8,128)}, f32[128,256]{1,0:T(8,128)}, f32[128,256]{1,0:T(8,1...) custom-call(f32[128,768]{1,0:T(8,128)} %get-tuple-element.136.qkv_re, ...), custom_call_target="tpu_custom_call" | custom-call | tf_op jit(solution)/shard_map/pallas_call | solution.py:1767
  300.4 1.5 constant_dynamic-slice_fusion.6
  301.9 1.0 copy.39
  (77 shorter events, 0.3 us)
Async XLA Ops:
  2.0 26.1 %copy-start.26 = (s32[2,4]{1,0:T(2,128)S(1)}, s32[2,4]{1,0:T(2,128)}, u32[]{:S(2)}) copy-start(s32[2,4]{1,0:T(2,128)} %param.25) | copy-start | bytes 100
  2.1 26.1 %copy-start.27 = (s32[2,4]{1,0:T(2,128)S(1)}, s32[2,4]{1,0:T(2,128)}, u32[]{:S(2)}) copy-start(s32[2,4]{1,0:T(2,128)} %param.24) | copy-start | bytes 100
  2.1 26.9 %copy-start.2 = (bf16[2,256,1024]{2,1,0:T(8,128)(2,1)S(1)}, bf16[2,256,1024]{2,1,0:T(8,128)(2,1)}, u32[]{:S(2)}) copy-start(bf16[2,256,1024]{2,1,0:T(8,128)(2,1)} %refs_5_.1) | copy-start | bytes 3145732
  29.0 94.9 %copy-start.3 = (s32[8]{0:T(128)}, s32[8]{0:T(128)S(1)}, u32[]{:S(2)}) copy-start(s32[8]{0:T(128)S(1)} %fusion.3.lengths_ref.refs_0_) | copy-start | bytes 100
  29.0 1.2 copy-start.11
  30.2 20.0 %copy-start.32 = (bf16[1024,1024]{1,0:T(8,128)(2,1)S(1)}, bf16[1024,1024]{1,0:T(8,128)(2,1)}, u32[]{:S(2)}) copy-start(bf16[1024,1024]{1,0:T(8,128)(2,1)} %refs_20_.1) | copy-start | bytes 6291460
  30.2 20.0 %copy-start.33 = (bf16[512,1024]{1,0:T(8,128)(2,1)S(1)}, bf16[512,1024]{1,0:T(8,128)(2,1)}, u32[]{:S(2)}) copy-start(bf16[512,1024]{1,0:T(8,128)(2,1)} %get-tuple-element.92.refs_1_) | copy-start | bytes 3145732
  50.1 1.4 copy-start.4
  50.1 1.4 copy-start.14
  50.2 20.1 %copy-start = (bf16[512,1024]{1,0:T(8,128)(2,1)}, bf16[512,1024]{1,0:T(8,128)(2,1)S(1)}, u32[]{:S(2)}) copy-start(bf16[512,1024]{1,0:T(8,128)(2,1)S(1)} %get-tuple-element.101.gown_in) | copy-start | bytes 3145732
  51.6 15.2 %copy-start.15 = (f32[512,1024]{1,0:T(8,128)}, f32[512,1024]{1,0:T(8,128)S(1)}, u32[]{:S(2)}) copy-start(f32[512,1024]{1,0:T(8,128)S(1)} %get-tuple-element.173) | copy-start | bytes 6291460
  51.6 0.7 copy-start.23
  51.6 0.8 copy-start.24
  52.0 2.0 copy-start.31
  53.9 1.3 copy-start.19
  53.9 1.6 copy-start.12
  55.2 11.5 %copy-start.7 = (bf16[512,1024]{1,0:T(8,128)(2,1)}, bf16[512,1024]{1,0:T(8,128)(2,1)S(1)}, u32[]{:S(2)}) copy-start(bf16[512,1024]{1,0:T(8,128)(2,1)S(1)} %convolution_convert_fusion.1.refs_1_) | copy-start | bytes 3145732
  55.5 11.2 %copy-start.29 = (bf16[1024,1024]{1,0:T(8,128)(2,1)S(1)}, bf16[1024,1024]{1,0:T(8,128)(2,1)}, u32[]{:S(2)}) copy-start(bf16[1024,1024]{1,0:T(8,128)(2,1)} %param.36) | copy-start | bytes 6291460
  66.7 1.4 copy-start.5
  68.1 0.7 copy-start.22
  68.1 0.7 copy-start.25
  70.3 4.4 %collective-permute-start = (bf16[512,1024]{1,0:T(8,128)(2,1)}, bf16[512,1024]{1,0:T(8,128)(2,1)}, u32[]{:S(2)}, u32[]{:S(2)}) collective-permute-start(bf16[512,1024]{1,0:T(8,128)(2,1)} %add_convert_fusion.own_in), channel_id=1, source_target_pairs={{0,4},{1,5},{2,6},{3,7},{4,0},{5,1},{6,2},{7,3},{8,12},{9,13},{10,... | collective-permute-start | bytes 3145736 | tf_op jit(solution)/shard_map/ppermute | solution.py:58
  70.3 4.4 %collective-permute-start.1 = (bf16[512,1024]{1,0:T(8,128)(2,1)S(1)}, bf16[512,1024]{1,0:T(8,128)(2,1)}, u32[]{:S(2)}, u32[]{:S(2)}) collective-permute-start(bf16[512,1024]{1,0:T(8,128)(2,1)S(1)} %get-tuple-element.101.gown_in), channel_id=1, source_target_pairs={{0,4},{1,5},{2,6},{3,7},{4,0},{5,1},{6,2},{7,3},{8,12},{9,13},{10,... | collective-permute-start | bytes 3145736 | tf_op jit(solution)/shard_map/ppermute | solution.py:58
  113.8 3.4 %collective-permute-start.2 = (bf16[512,1024]{1,0:T(8,128)(2,1)}, bf16[512,1024]{1,0:T(8,128)(2,1)S(1)}, u32[]{:S(2)}, u32[]{:S(2)}) collective-permute-start(bf16[512,1024]{1,0:T(8,128)(2,1)} %get-tuple-element.103), channel_id=1, source_target_pairs={{0,4},{1,5},{2,6},{3,7},{4,0},{5,1},{6,2},{7,3},{8,12},{9,13},{10,... | collective-permute-start | bytes 3145736 | tf_op jit(solution)/shard_map/ppermute | solution.py:58
  114.0 30.2 %collective-permute-start.3 = (bf16[2,512,512]{2,1,0:T(8,128)(2,1)}, bf16[2,512,512]{2,1,0:T(8,128)(2,1)}, u32[]{:S(2)}, u32[]{:S(2)}) collective-permute-start(bf16[2,512,512]{2,1,0:T(8,128)(2,1)} %get-tuple-element.111), channel_id=1, source_target_pairs={{0,1},{1,0},{2,3},{3,2},{4,5},{5,4},{6,7},{7,6},{8,9},{9,8},{10,11... | collective-permute-start | bytes 3145736 | tf_op jit(solution)/shard_map/ppermute | solution.py:58
  115.0 29.2 %collective-permute-start.4 = (bf16[2,512,512]{2,1,0:T(8,128)(2,1)}, bf16[2,512,512]{2,1,0:T(8,128)(2,1)}, u32[]{:S(2)}, u32[]{:S(2)}) collective-permute-start(bf16[2,512,512]{2,1,0:T(8,128)(2,1)} %get-tuple-element.113), channel_id=1, source_target_pairs={{0,2},{1,3},{2,0},{3,1},{4,6},{5,7},{6,4},{7,5},{8,10},{9,11},{10,... | collective-permute-start | bytes 3145736 | tf_op jit(solution)/shard_map/ppermute | solution.py:58
  115.6 28.7 %collective-permute-start.5 = (bf16[4,256,512]{2,1,0:T(8,128)(2,1)}, bf16[4,256,512]{2,1,0:T(8,128)(2,1)}, u32[]{:S(2)}, u32[]{:S(2)}) collective-permute-start(bf16[4,256,512]{2,1,0:T(8,128)(2,1)} %get-tuple-element.115), channel_id=1, source_target_pairs={{0,8},{1,9},{2,10},{3,11},{4,12},{5,13},{6,14},{7,15},{8,16},{9,17... | collective-permute-start | bytes 3145736 | tf_op jit(solution)/shard_map/ppermute | solution.py:58
  117.1 2.8 copy-start.1
  117.1 2.8 copy-start.17
  117.1 3.2 %copy-start.18 = (f32[512,1024]{1,0:T(8,128)S(1)}, f32[512,1024]{1,0:T(8,128)}, u32[]{:S(2)}) copy-start(f32[512,1024]{1,0:T(8,128)} %get-tuple-element.108) | copy-start | bytes 6291460
  120.3 2.2 copy-start.30
  122.5 1.3 copy-start.21
  122.5 1.6 copy-start.8
  122.5 1.9 copy-start.13
  124.4 11.0 %copy-start.16 = (f32[512,1024]{1,0:T(8,128)S(1)}, f32[512,1024]{1,0:T(8,128)}, u32[]{:S(2)}) copy-start(f32[512,1024]{1,0:T(8,128)} %copy-done.15) | copy-start | bytes 6291460
  135.4 4.2 %copy-start.6 = (bf16[512,1024]{1,0:T(8,128)(2,1)}, bf16[512,1024]{1,0:T(8,128)(2,1)S(1)}, u32[]{:S(2)}) copy-start(bf16[512,1024]{1,0:T(8,128)(2,1)S(1)} %get-tuple-element.105.refs_6_) | copy-start | bytes 3145732
  135.4 4.2 %copy-start.9 = (bf16[256,1024]{1,0:T(8,128)(2,1)}, bf16[256,1024]{1,0:T(8,128)(2,1)S(1)}, u32[]{:S(2)}) copy-start(bf16[256,1024]{1,0:T(8,128)(2,1)S(1)} %get-tuple-element.106.refs_7_) | copy-start | bytes 1572868
  135.4 4.2 %copy-start.10 = (bf16[256,1024]{1,0:T(8,128)(2,1)}, bf16[256,1024]{1,0:T(8,128)(2,1)S(1)}, u32[]{:S(2)}) copy-start(bf16[256,1024]{1,0:T(8,128)(2,1)S(1)} %get-tuple-element.107.refs_8_) | copy-start | bytes 1572868
  135.4 4.2 %copy-start.28 = (bf16[1024,2048]{1,0:T(8,128)(2,1)S(1)}, bf16[1024,2048]{1,0:T(8,128)(2,1)}, u32[]{:S(2)}) copy-start(bf16[1024,2048]{1,0:T(8,128)(2,1)} %kv_ref.1) | copy-start | bytes 12582916
  176.7 36.3 %collective-permute-start.6 = (bf16[2,4,64,1536]{3,2,1,0:T(8,128)(2,1)}, bf16[2,4,64,1536]{3,2,1,0:T(8,128)(2,1)}, u32[]{:S(2)}, u32[]{:S(2)}) collective-permute-start(bf16[2,4,64,1536]{3,2,1,0:T(8,128)(2,1)} %get-tuple-element.127), channel_id=1, source_target_pairs={{0,1},{1,0},{2,3},{3,2},{4,5},{5,4},{6,7},{7,6},{8,9},{9,8},{10,11... | collective-permute-start | bytes 4718600 | tf_op jit(solution)/shard_map/ppermute | solution.py:58
  177.8 36.0 %collective-permute-start.7 = (bf16[2,4,64,1536]{3,2,1,0:T(8,128)(2,1)}, bf16[2,4,64,1536]{3,2,1,0:T(8,128)(2,1)}, u32[]{:S(2)}, u32[]{:S(2)}) collective-permute-start(bf16[2,4,64,1536]{3,2,1,0:T(8,128)(2,1)} %get-tuple-element.129), channel_id=1, source_target_pairs={{0,2},{1,3},{2,0},{3,1},{4,6},{5,7},{6,4},{7,5},{8,10},{9,11},{10,... | collective-permute-start | bytes 4718600 | tf_op jit(solution)/shard_map/ppermute | solution.py:58
  178.8 27.6 %collective-permute-start.8 = (bf16[4,256,512]{2,1,0:T(8,128)(2,1)}, bf16[4,256,512]{2,1,0:T(8,128)(2,1)}, u32[]{:S(2)}, u32[]{:S(2)}) collective-permute-start(bf16[4,256,512]{2,1,0:T(8,128)(2,1)} %get-tuple-element.135), channel_id=1, source_target_pairs={{0,8},{1,9},{2,10},{3,11},{4,12},{5,13},{6,14},{7,15},{8,16},{9,17... | collective-permute-start | bytes 3145736 | tf_op jit(solution)/shard_map/ppermute | solution.py:58
  296.0 5.9 %copy-start.20 = (bf16[2,256,1024]{2,1,0:T(8,128)(2,1)S(1)}, bf16[2,256,1024]{2,1,0:T(8,128)(2,1)}, u32[]{:S(2)}) copy-start(bf16[2,256,1024]{2,1,0:T(8,128)(2,1)} %get-tuple-element.199) | copy-start | bytes 3145732
